TPU v7x, 32 devices: a whole 2x2x4 slice. The times are simulated.
32 devices in a mesh: dp: 16 (over z, y, core), tensor: 2 (over x).
Axes of the slice: x: 2, y: 2, z: 4, core: 2. Of those that a mesh axis runs over, the one named last changes fastest.
Arguments:
- residual_in: bfloat16 [32768, 1024], P(('dp', 'tensor')), may hold values from -6 to 6
- mixer_gain: float32 [1024], replicated, may hold values from 0.1 to 1.9
- in_weight: bfloat16 [1024, 8, 768], P(None, 'tensor'), may hold values from -0.1875 to 0.1875
- rate_weight: bfloat16 [1024, 8, 2], P(None, 'tensor'), may hold values from -0.1875 to 0.1875
- conv_weight: bfloat16 [8, 4, 512], P('tensor'), may hold values from -3 to 3
- decay_log: float32 [8], P('tensor'), may hold values from -1.5 to 2
- decay_bias: float32 [8], P('tensor'), may hold values from -7 to -2
- head_gain: float32 [256], replicated, may hold values from 0.1 to 1.9
- out_weight: bfloat16 [8, 256, 1024], P('tensor'), may hold values from -0.25 to 0.25
- ffn_gain: float32 [1024], replicated, may hold values from 0.1 to 1.9
- gate_up: bfloat16 [1024, 2, 2816], P(None, None, 'tensor'), may hold values from -0.1875 to 0.1875
- down_weight: bfloat16 [2816, 1024], P('tensor'), may hold values from -0.109375 to 0.109375
- segments: int32 [32768], P('dp'), may hold values from 0 to 2, as said below
- pad_mask: int32 [32768], P('dp'), may hold values from 0 to 1, as said below
- out_grad: bfloat16 [32768, 1024], P(('dp', 'tensor')), may hold values from -6 to 6
Outputs:
- layer_out: bfloat16 [32768, 1024], P(('dp', 'tensor'))
- input_grad: bfloat16 [32768, 1024], P(('dp', 'tensor'))
- grad_mixer_gain: float32 [1024], replicated
- grad_in_weight: float32 [1024, 8, 768], P(None, 'tensor')
- grad_rate_weight: float32 [1024, 8, 2], P(None, 'tensor')
- grad_conv_weight: float32 [8, 4, 512], P('tensor')
- grad_decay_log: float32 [8], P('tensor')
- grad_decay_bias: float32 [8], P('tensor')
- grad_head_gain: float32 [256], replicated
- grad_out_weight: float32 [8, 256, 1024], P('tensor')
- grad_ffn_gain: float32 [1024], replicated
- grad_gate_up: float32 [1024, 2, 2816], P(None, None, 'tensor')
- grad_down_weight: float32 [2816, 1024], P('tensor')
Inputs may be any that keep to these rules, and one draw needn't show every extreme that they name: `segments`: in each aligned run of 1024 tokens (one sequence) the numbers start at 0, never fall and name three documents of 200 tokens or more; the last is followed by 1 to 128 padding tokens that carry its number. `pad_mask`: 0 exactly on the padding tokens at the end of each sequence, 1 elsewhere.
All inputs are finite; a program needn't handle non-finite values.
Results may differ from a plain program's by a relative error of at most 0.024.
Values may be sent and summed in bfloat16 or wider, within the bound.
No kernel may reach another device: no remote copies, remote signals or barrier semaphores. Data moves between devices by JAX's collectives and lax.ppermute only.
A program may use at most 512 MiB of HBM per device.

v0:
```python
import jax
import jax.numpy as jnp
from jax import lax
from jax.sharding import PartitionSpec as P

SPAN = 64
SEQ = 1024


def rms_norm(rows_in, gain_in):
    return rows_in * lax.rsqrt(jnp.mean(rows_in * rows_in, -1, keepdims=True) + 1e-05) * gain_in


def short_conv(pre_conv, seg_rows, conv_in):
    summed = pre_conv * conv_in[:, 0, :]
    for offset in range(1, conv_in.shape[1]):
        shifted = jnp.pad(pre_conv, ((0, 0), (offset, 0), (0, 0), (0, 0)))[:, :-offset]
        seg_shift = jnp.pad(seg_rows, ((0, 0), (offset, 0)), constant_values=-1)[:, :-offset]
        usable = (seg_shift == seg_rows).astype(jnp.float32)
        summed = summed + shifted * usable[:, :, None, None] * conv_in[:, offset, :]
    return jax.nn.silu(summed)


def block_inverse(key_blocks, write_blocks, decay_blocks, seg_blocks):
    width = seg_blocks.shape[-1]
    cum_decay = jnp.cumsum(decay_blocks, axis=-1)
    same_seg = seg_blocks[..., :, None] == seg_blocks[..., None, :]
    lower_strict = jnp.tril(jnp.ones((width, width), dtype=bool), -1)
    inside = (same_seg & lower_strict)[:, :, None]
    gap_decay = cum_decay[..., :, None] - cum_decay[..., None, :]
    weight_strict = jnp.where(inside, jnp.exp(jnp.where(inside, gap_decay, 0.0)), 0.0)
    key_key = jnp.einsum(
        "abhtk,abhsk->abhts", key_blocks, key_blocks, precision=lax.Precision.HIGHEST
    )
    negated = -write_blocks[..., None] * weight_strict * key_key
    identity_m = jnp.eye(width, dtype=jnp.float32)
    result = identity_m + negated
    power = negated
    for unused_level in range(width.bit_length() - 2):
        power = jnp.einsum("abhts,abhsu->abhtu", power, power, precision=lax.Precision.HIGHEST)
        result = jnp.einsum(
            "abhts,abhsu->abhtu", result, identity_m + power, precision=lax.Precision.HIGHEST
        )
    return result


def span_step(carry, block):
    current_state, last_seg = carry
    query_rows, key_vector, values_vec, write_rate, log_decay, seg_ids, keep_mask, inverse = block
    width = seg_ids.shape[0]
    cum_decay = jnp.cumsum(log_decay, axis=1)
    carry_on = (seg_ids == last_seg).astype(jnp.float32)
    same_seg = seg_ids[:, None] == seg_ids[None, :]
    lower_eq = jnp.tril(jnp.ones((width, width), dtype=bool))
    inside = same_seg & lower_eq
    gap_decay = cum_decay[:, :, None] - cum_decay[:, None, :]
    weight_eq = jnp.where(inside, jnp.exp(jnp.where(inside, gap_decay, 0.0)), 0.0)
    initial_scale = jnp.exp(cum_decay) * carry_on[None, :]
    key_from_state = jnp.einsum(
        "afy,aym->afm", key_vector, current_state, precision=lax.Precision.HIGHEST
    )
    right_side = write_rate[:, :, None] * (values_vec - initial_scale[:, :, None] * key_from_state)
    written_value = jnp.einsum("hts,hsv->htv", inverse, right_side, precision=lax.Precision.HIGHEST)
    query_key = (
        jnp.einsum("htk,hsk->hts", query_rows, key_vector, precision=lax.Precision.HIGHEST)
        * weight_eq
    )
    query_from_state = jnp.einsum(
        "afy,aym->afm", query_rows, current_state, precision=lax.Precision.HIGHEST
    )
    outputs = jnp.einsum("hts,hsv->htv", query_key, written_value, precision=lax.Precision.HIGHEST)
    outputs = (outputs + initial_scale[:, :, None] * query_from_state) * keep_mask[None, :, None]
    final_weight = weight_eq[:, -1, :]
    updated_state = initial_scale[:, -1][:, None, None] * current_state + jnp.einsum(
        "au,aul,aup->alp", final_weight, key_vector, written_value, precision=lax.Precision.HIGHEST
    )
    return ((updated_state, seg_ids[-1]), outputs)


def run_sequence(
    query_rows, key_vector, values_vec, write_rate, log_decay, seg_blocks, mask_blocks, inverses
):
    initial = (
        jnp.zeros((query_rows.shape[1], query_rows.shape[3], values_vec.shape[3]), jnp.float32),
        jnp.full((), -1, jnp.int32),
    )
    unused_state, outputs = lax.scan(
        jax.checkpoint(span_step),
        initial,
        (
            query_rows,
            key_vector,
            values_vec,
            write_rate,
            log_decay,
            seg_blocks,
            mask_blocks,
            inverses,
        ),
    )
    return outputs


def mixer_core(
    projected, rate_pre, conv_in, log_in, bias_in, gain_in, seg_in, mask_in, seq_len, span_len
):
    length, heads, in_width = projected.shape
    value_dim = gain_in.shape[0]
    mix_width = conv_in.shape[2]
    key_dim = (mix_width - value_dim) // 2
    seq_count = length // seq_len
    span_count = seq_len // span_len
    pre_conv = projected[:, :, :mix_width].reshape(seq_count, seq_len, heads, mix_width)
    seg_rows = seg_in.reshape(seq_count, seq_len)
    mask_rows = mask_in.reshape(seq_count, seq_len).astype(jnp.float32)
    mixed = short_conv(pre_conv, seg_rows, conv_in)
    query_rows = mixed[..., :key_dim]
    key_vector = mixed[..., key_dim : 2 * key_dim]
    values_vec = mixed[..., 2 * key_dim :]
    query_rows = (
        query_rows
        * lax.rsqrt(jnp.sum(query_rows * query_rows, -1, keepdims=True) + 1e-06)
        * key_dim ** (-0.5)
    )
    key_vector = key_vector * lax.rsqrt(jnp.sum(key_vector * key_vector, -1, keepdims=True) + 1e-06)
    write_rate = (
        jax.nn.sigmoid(rate_pre[..., 1]).reshape(seq_count, seq_len, heads) * mask_rows[:, :, None]
    )
    log_decay = -jnp.exp(log_in) * jax.nn.softplus(
        rate_pre[..., 0].reshape(seq_count, seq_len, heads) + bias_in
    )

    def wide_blocks(array):
        return array.reshape(seq_count, span_count, span_len, heads, -1).transpose(0, 1, 3, 2, 4)

    def flat_blocks(array):
        return array.reshape(seq_count, span_count, span_len, heads).transpose(0, 1, 3, 2)

    key_blocks = wide_blocks(key_vector)
    write_blocks = flat_blocks(write_rate)
    decay_blocks = flat_blocks(log_decay)
    seg_blocks = seg_rows.reshape(seq_count, span_count, span_len)
    inverses = block_inverse(key_blocks, write_blocks, decay_blocks, seg_blocks)
    outputs = jax.vmap(run_sequence)(
        wide_blocks(query_rows),
        key_blocks,
        wide_blocks(values_vec),
        write_blocks,
        decay_blocks,
        seg_blocks,
        mask_rows.reshape(seq_count, span_count, span_len),
        inverses,
    )
    heads_out = outputs.transpose(0, 1, 3, 2, 4).reshape(length, heads, value_dim)
    gate_part = projected[:, :, mix_width:]
    normed = (
        heads_out * lax.rsqrt(jnp.mean(heads_out * heads_out, -1, keepdims=True) + 1e-05) * gain_in
    )
    return (normed * jax.nn.silu(gate_part)).reshape(length, heads * value_dim)


def shards(
    residual_in,
    mixer_gain,
    in_weight,
    rate_weight,
    conv_weight,
    decay_log,
    decay_bias,
    head_gain,
    out_weight,
    ffn_gain,
    gate_up,
    down_weight,
    segments,
    pad_mask,
    out_grad,
):
    model_width = residual_in.shape[1]
    heads_here = in_weight.shape[1]
    in_width = in_weight.shape[2]
    hidden_here = gate_up.shape[2]
    w_in_flat = in_weight.reshape(model_width, heads_here * in_width)
    w_rate_flat = rate_weight.reshape(model_width, heads_here * 2)
    w_out_flat = out_weight.reshape(-1, model_width)
    w_gu_flat = gate_up.reshape(model_width, 2 * hidden_here)
    conv_float = conv_weight.astype(jnp.float32)
    rows_in = residual_in.astype(jnp.float32)
    normed_one, norm_one_back = jax.vjp(rms_norm, rows_in, mixer_gain)
    first_low = lax.all_gather(normed_one.astype(jnp.bfloat16), "tensor", axis=0, tiled=True)
    projected = jnp.dot(first_low, w_in_flat, preferred_element_type=jnp.float32)
    projected = projected.reshape(-1, heads_here, in_width)
    rate_pre = jnp.dot(first_low, w_rate_flat, preferred_element_type=jnp.float32).reshape(
        -1, heads_here, 2
    )

    def core_fn(proj_in, rates_in, conv_in, log_in, bias_in, gain_in):
        return mixer_core(
            proj_in, rates_in, conv_in, log_in, bias_in, gain_in, segments, pad_mask, SEQ, SPAN
        )

    core_inputs = (projected, rate_pre, conv_float, decay_log, decay_bias, head_gain)
    gated, core_back = jax.vjp(core_fn, *core_inputs)
    gated_low = gated.astype(jnp.bfloat16)
    middle = rows_in + lax.psum_scatter(
        jnp.dot(gated_low, w_out_flat, preferred_element_type=jnp.float32).astype(jnp.bfloat16),
        "tensor",
        scatter_dimension=0,
        tiled=True,
    ).astype(jnp.float32)
    normed_two, norm_two_back = jax.vjp(rms_norm, middle, ffn_gain)
    second = lax.all_gather(normed_two.astype(jnp.bfloat16), "tensor", axis=0, tiled=True)
    pre_ffn = jnp.dot(second, w_gu_flat, preferred_element_type=jnp.float32).reshape(
        -1, 2, hidden_here
    )
    gate_part = pre_ffn[:, 0]
    up_part = pre_ffn[:, 1]
    sigma_gate = jax.nn.sigmoid(gate_part)
    hidden = (gate_part * sigma_gate * up_part).astype(jnp.bfloat16)
    layer_out = (
        middle
        + lax.psum_scatter(
            jnp.dot(hidden, down_weight, preferred_element_type=jnp.float32).astype(jnp.bfloat16),
            "tensor",
            scatter_dimension=0,
            tiled=True,
        ).astype(jnp.float32)
    ).astype(jnp.bfloat16)
    ffn_cot = lax.all_gather(out_grad, "tensor", axis=0, tiled=True)
    grad_down = jnp.dot(hidden.T, ffn_cot, preferred_element_type=jnp.float32)
    grad_hidden = jnp.dot(ffn_cot, down_weight.T, preferred_element_type=jnp.float32)
    grad_gate = grad_hidden * up_part * sigma_gate * (1.0 + gate_part * (1.0 - sigma_gate))
    grad_upper = grad_hidden * gate_part * sigma_gate
    grad_pre = (
        jnp.stack([grad_gate, grad_upper], 1).astype(jnp.bfloat16).reshape(-1, 2 * hidden_here)
    )
    grad_gate_up = jnp.dot(second.T, grad_pre, preferred_element_type=jnp.float32)
    grad_gate_up = grad_gate_up.reshape(model_width, 2, hidden_here)
    grad_second = lax.psum_scatter(
        jnp.dot(grad_pre, w_gu_flat.T, preferred_element_type=jnp.float32).astype(jnp.bfloat16),
        "tensor",
        scatter_dimension=0,
        tiled=True,
    ).astype(jnp.float32)
    grad_middle_part, grad_ffn_gain = norm_two_back(grad_second)
    grad_middle = out_grad.astype(jnp.float32) + grad_middle_part
    mixer_cot = lax.all_gather(grad_middle.astype(jnp.bfloat16), "tensor", axis=0, tiled=True)
    grad_out = jnp.dot(gated_low.T, mixer_cot, preferred_element_type=jnp.float32).reshape(
        out_weight.shape
    )
    grad_gated = jnp.dot(mixer_cot, w_out_flat.T, preferred_element_type=jnp.float32)
    grad_proj, grad_rates, grad_conv, grad_log, grad_bias, grad_head_gain = core_back(grad_gated)
    proj_low = grad_proj.astype(jnp.bfloat16).reshape(-1, heads_here * in_width)
    rates_low = grad_rates.astype(jnp.bfloat16).reshape(-1, heads_here * 2)
    grad_in = jnp.dot(first_low.T, proj_low, preferred_element_type=jnp.float32).reshape(
        in_weight.shape
    )
    grad_rate = jnp.dot(first_low.T, rates_low, preferred_element_type=jnp.float32).reshape(
        rate_weight.shape
    )
    proj_part = jnp.dot(proj_low, w_in_flat.T, preferred_element_type=jnp.float32)
    rate_part = jnp.dot(rates_low, w_rate_flat.T, preferred_element_type=jnp.float32)
    grad_first = lax.psum_scatter(
        (proj_part + rate_part).astype(jnp.bfloat16), "tensor", scatter_dimension=0, tiled=True
    ).astype(jnp.float32)
    grad_rows_part, grad_mixer_gain = norm_one_back(grad_first)
    input_grad = (grad_middle + grad_rows_part).astype(jnp.bfloat16)
    grad_mixer_gain, grad_head_gain, grad_ffn_gain = lax.psum(
        (grad_mixer_gain, grad_head_gain, grad_ffn_gain), ("dp", "tensor")
    )
    grad_in, grad_rate, grad_conv, grad_log, grad_bias, grad_out, grad_gate_up, grad_down = (
        lax.psum(grad_in.astype(jnp.bfloat16), "dp").astype(jnp.float32),
        lax.psum(grad_rate.astype(jnp.bfloat16), "dp").astype(jnp.float32),
        lax.psum(grad_conv.astype(jnp.bfloat16), "dp").astype(jnp.float32),
        lax.psum(grad_log.astype(jnp.bfloat16), "dp").astype(jnp.float32),
        lax.psum(grad_bias.astype(jnp.bfloat16), "dp").astype(jnp.float32),
        lax.psum(grad_out.astype(jnp.bfloat16), "dp").astype(jnp.float32),
        lax.psum(grad_gate_up.astype(jnp.bfloat16), "dp").astype(jnp.float32),
        lax.psum(grad_down.astype(jnp.bfloat16), "dp").astype(jnp.float32),
    )
    return (
        layer_out,
        input_grad,
        grad_mixer_gain,
        grad_in,
        grad_rate,
        grad_conv,
        grad_log,
        grad_bias,
        grad_head_gain,
        grad_out,
        grad_ffn_gain,
        grad_gate_up,
        grad_down,
    )


def solution(mesh):
    return jax.shard_map(
        shards,
        mesh=mesh,
        in_specs=(
            P(("dp", "tensor"), None),
            P(),
            P(None, "tensor", None),
            P(None, "tensor", None),
            P("tensor", None, None),
            P("tensor"),
            P("tensor"),
            P(),
            P("tensor", None, None),
            P(),
            P(None, None, "tensor"),
            P("tensor", None),
            P("dp"),
            P("dp"),
            P(("dp", "tensor"), None),
        ),
        out_specs=(
            P(("dp", "tensor"), None),
            P(("dp", "tensor"), None),
            P(),
            P(None, "tensor", None),
            P(None, "tensor", None),
            P("tensor", None, None),
            P("tensor"),
            P("tensor"),
            P(),
            P("tensor", None, None),
            P(),
            P(None, None, "tensor"),
            P("tensor", None),
        ),
        check_vma=False,
    )
```

profile of v0, /device:TPU:0, one launch (start us, length us, event | category | flops | bytes accessed | tf_op | source)
XLA Modules:
  0.0 2511.7 jit_solution(6111403461707840120)
XLA Ops:
  33.9 39.8 %all-gather.5.cloned.1.call-done = bf16[2048,1024]{1,0:T(8,128)(2,1)} async-done(((bf16[1024,1024]{1,0:T(8,128)(2,1)}), bf16[2048,1024]{1,0:T(8,128)(2,1)}) %all-gather.5.cloned.1.call-update) | async-done | bytes 4194320 | tf_op jit(solution)/shard_map/all_gather | solution.py:190
  83.2 20.0 fusion.150
  120.8 34.2 %fusion.105 = (f32[2,1024,4,512]{3,1,2,0:T(8,128)}, f32[2,1024,4,512]{3,1,2,0:T(8,128)}) fusion(f32[4,512]{1,0:T(4,128)S(1)} %get-tuple-element.1073, f32[2,1024]{1,0:T(2,128)S(1)} %get-tuple-element.1070, f32[2,1024,4,512]{3,1,2,0:T(8,128)} %copy.384, f32[4,512]{1,0:T(4,128)S(1)} %get-tuple-element.1074, f32[2,1024]{1,0:T(2,128)S(1)} %get-tuple-element.1069, ...), kind=kLoop, calls=%fused_computation.171 | loop fusion | flops 58720256 | bytes 50388992 | tf_op jit(solution)/shard_map/jvp(jit(silu))/mul | solution.py:21
  176.6 11.6 fusion.271
  300.9 278.7 %while.48 = (s32[]{:T(128)}, f32[2,4,128,256]{3,2,1,0:T(8,128)}, s32[2]{0:T(128)S(1)}, f32[16,2,4,64,256]{4,3,2,1,0:T(8,128)}, f32[16,2,4,128,256]{4,3,2,1,0:T(8...) while((s32[]{:T(128)}, f32[2,4,128,256]{3,2,1,0:T(8,128)}, ...), condition=%wide.region_6.7_spmd.clone, body=%wide.region_4.6_spmd.clone.sunk | while | flops 858345728 | bytes 21453200 | solution.py:87
  604.9 54.4 %reduce-scatter.5.cloned.1.call-done = bf16[1024,1024]{1,0:T(8,128)(2,1)} async-done(((bf16[2048,1024]{1,0:T(8,128)(2,1)}), bf16[1024,1024]{1,0:T(8,128)(2,1)}) %reduce-scatter.5.cloned.1.call-update) | async-done | bytes 2097168 | tf_op jit(solution)/shard_map/reduce_scatter | solution.py:205
  680.2 41.5 %all-gather.7.cloned.1.call-done = bf16[2048,1024]{1,0:T(8,128)(2,1)} async-done(((bf16[1024,1024]{1,0:T(8,128)(2,1)}), bf16[2048,1024]{1,0:T(8,128)(2,1)}) %all-gather.7.cloned.1.call-update) | async-done | bytes 4194320 | tf_op jit(solution)/shard_map/all_gather | solution.py:212
  721.8 19.7 fusion.145
  741.5 38.5 %all-gather.9.cloned.1.call-done = bf16[2048,1024]{1,0:T(8,128)(2,1)} async-done(((bf16[1024,1024]{1,0:T(8,128)(2,1)}), bf16[2048,1024]{1,0:T(8,128)(2,1)}) %all-gather.9.cloned.1.call-update) | async-done | bytes 4194320 | tf_op jit(solution)/shard_map/all_gather | solution.py:229
  780.0 18.4 multiply_bitcast_fusion.1
  798.4 18.3 bitcast_convert_fusion
  816.7 54.4 %reduce-scatter.9.cloned.1.call-done = bf16[1024,1024]{1,0:T(8,128)(2,1)} async-done(((bf16[2048,1024]{1,0:T(8,128)(2,1)}), bf16[1024,1024]{1,0:T(8,128)(2,1)}) %reduce-scatter.9.cloned.1.call-update) | async-done | bytes 2097168 | tf_op jit(solution)/shard_map/reduce_scatter | solution.py:239
  881.3 56.9 %all-gather.11.cloned.1.call-done = bf16[2048,1024]{1,0:T(8,128)(2,1)} async-done(((bf16[1024,1024]{1,0:T(8,128)(2,1)}), bf16[2048,1024]{1,0:T(8,128)(2,1)}) %all-gather.11.cloned.1.call-update) | async-done | bytes 4194320 | tf_op jit(solution)/shard_map/all_gather | solution.py:247
  938.2 17.8 multiply_reduce_fusion.8
  982.7 710.9 %while.49 = (s32[]{:T(128)}, f32[2,4,128,256]{3,2,1,0:T(8,128)}, f32[16,2,4,64,128]{4,3,0,2,1:T(8,128)}, f32[16,2,4,64,128]{4,3,2,0,1:T(8,128)}, f32[16,2,4,64,2...) while((s32[]{:T(128)}, f32[2,4,128,256]{3,2,1,0:T(8,128)}, ...), condition=%wide.region_23.24_spmd.clone, body=%wide.region_14.23_spmd.clone.sunk | while | flops 2271367424 | bytes 58118000 | solution.py:87
  1730.8 11.2 add_add_fusion.9
  1766.1 11.4 add_add_fusion.8
  1850.9 11.3 fusion.269
  1862.3 13.1 fusion.200
  1883.9 11.6 fusion.186
  1919.7 40.0 %multiply_reduce_fusion.7 = (f32[4,512]{1,0:T(4,128)}, f32[4,512]{1,0:T(4,128)}, f32[4,512]{1,0:T(4,128)}, f32[4,512]{1,0:T(4,128)}, f32[2,1024,4,512]{3,1,2,0:T(8,128)}) fusion(f32[2,1024]{1,0:T(2,128)S(1)} %copy-done.98, f32[2,1024]{1,0:T(2,128)S(1)} %copy-done.94, f32[2,1024]{1,0:T(2,128)S(1)} %copy-done.96, f32[2,1024,4,512]{3,1,0,2:T(8,128)} %bitcast.504, ...), kind=kLoop, calls=%fused_computation.166 | loop fusion | flops 92266496 | bytes 83943424 | tf_op jit(solution)/shard_map/transpose(jvp())/reduce_sum | solution.py:20
  1959.7 21.7 multiply_multiply_fusion
  1981.4 28.9 %fusion.102 = f32[2,1024,4,512]{3,1,2,0:T(8,128)} fusion(f32[2,1024,4,512]{3,1,2,0:T(8,128)} %get-tuple-element.1049, f32[2,1024,4,512]{3,1,2,0:T(8,128)} %get-tuple-element.1048, f32[2,1024,4,512]{3,1,2,0:T(8,128)} %get-tuple-element.1047, f32[2,1024,4,512]{3,1,2,0:T(8,128)} %get-tuple-element.1028, f32[4,512]{1,0:T(4,128)S(1)} %copy-done.110), kind=kLoop, calls=%fused_computation.160 | loop fusion | flops 16777216 | bytes 83894272 | tf_op jit(solution)/shard_map/transpose(jvp())/add_any | solution.py:15
  2022.7 20.5 fusion.116
  2077.4 18.6 fusion.120
  2106.0 16.1 copy.462
  2131.6 15.3 fusion.192
  2150.6 64.1 %all-reduce.23 = (bf16[1024,4,2]{0,1,2:T(4,128)(2,1)S(1)}, bf16[4,4,512]{2,0,1:T(4,128)(2,1)S(1)}, bf16[4]{0:T(256)(128)(2,1)S(1)}, bf16[4]{0:T(256)(128)(2,1)S(1)}) all-reduce(bf16[1024,4,2]{0,1,2:T(4,128)(2,1)S(1)} %fusion.238, bf16[4,4,512]{2,0,1:T(4,128)(2,1)S(1)} %add_convert_fusion.3, ...), channel_id=1, replica_groups=mesh['dp'=16,'tensor'=2] {'dp'}, use_global_device_ids=true, to_apply=%region_35.36 | all-reduce | flops 16392 | bytes 65568 | tf_op jit(solution)/shard_map/psum | solution.py:273
  2221.1 39.1 %all-reduce.22 = (f32[1024]{0:T(1024)}, f32[256]{0:T(256)}, f32[1024]{0:T(1024)}) all-reduce(f32[1024]{0:T(1024)S(1)} %get-tuple-element.943, f32[256]{0:T(256)S(1)} %copy-done.135, f32[1024]{0:T(1024)S(1)} %copy-done.129), channel_id=1, replica_groups=mesh['dp'=16,'tensor'=2] {'dp','tensor'}, use_global_device_ids=true, to_apply=%region_33.34 | all-reduce | flops 2304 | bytes 18432 | tf_op jit(solution)/shard_map/psum | solution.py:268
  2268.1 204.4 %all-reduce.27.cloned.1.call-done = (bf16[1024,4,768]{2,0,1:T(8,128)(2,1)}, bf16[1024,2,1408]{2,0,1:T(8,128)(2,1)}, bf16[4,256,1024]{2,1,0:T(8,128)(2,1)}, bf16[1408,1024]{1,0:T(8,128)(2,1)}) async-done(((bf16[1024,4,768]{2,0,1:T(8,128)(2,1)}, bf16[1024,2,1408]{2,0,1:T(8,128)(2,1)}, bf16[4,256,1024]{2,1,0:T(8,128)(2,1)}, bf16[1408,1024]{1,0:T(8,128)(2,1)}), (bf16[1024,4,768]{2,0,1:T(8,128)(2,1)}, ...) | async-done | bytes 17039376 | tf_op jit(solution)/shard_map/psum | solution.py:272
  2479.9 12.4 copy.469
  2492.3 12.6 copy.472
  (1800 shorter events, 1512.5 us)
Async XLA Ops:
  7.2 772.8 %copy-start = (bf16[1408,1024]{1,0:T(8,128)(2,1)S(1)}, bf16[1408,1024]{1,0:T(8,128)(2,1)}, u32[]{:S(2)}) copy-start(bf16[1408,1024]{1,0:T(8,128)(2,1)} %param.30) | copy-start | bytes 8650756
  7.2 66.5 %all-gather.5.cloned.1.call-start = ((), (), s32[]{:S(2)}) async-start(), calls=%async_computation.4 | async-start | bytes 6291456 | tf_op jit(solution)/shard_map/all_gather | solution.py:190
  14.2 645.1 %reduce-scatter.5.cloned.1.call-start = ((), (), s32[]{:S(2)}) async-start(), calls=%async_computation.5 | async-start | bytes 6291456 | tf_op jit(solution)/shard_map/reduce_scatter | solution.py:205
  32.2 254.5 %copy-start.68 = (f32[64,64]{0,1:T(8,128)}, f32[64,64]{0,1:T(8,128)S(1)}, u32[]{:S(2)}) copy-start(f32[64,64]{0,1:T(8,128)S(1)} %fusion.256) | copy-start | bytes 49156
  32.9 87.9 %copy-start.93 = (f32[2,1024]{1,0:T(2,128)}, f32[2,1024]{1,0:T(2,128)S(1)}, u32[]{:S(2)}) copy-start(f32[2,1024]{1,0:T(2,128)S(1)} %get-tuple-element.1068) | copy-start | bytes 24580
  32.9 87.9 %copy-start.95 = (f32[2,1024]{1,0:T(2,128)}, f32[2,1024]{1,0:T(2,128)S(1)}, u32[]{:S(2)}) copy-start(f32[2,1024]{1,0:T(2,128)S(1)} %get-tuple-element.1069) | copy-start | bytes 24580
  32.9 87.9 %copy-start.97 = (f32[2,1024]{1,0:T(2,128)}, f32[2,1024]{1,0:T(2,128)S(1)}, u32[]{:S(2)}) copy-start(f32[2,1024]{1,0:T(2,128)S(1)} %get-tuple-element.1070) | copy-start | bytes 24580
  33.5 87.2 %copy-start.103 = (f32[4,512]{1,0:T(4,128)}, f32[4,512]{1,0:T(4,128)S(1)}, u32[]{:S(2)}) copy-start(f32[4,512]{1,0:T(4,128)S(1)} %get-tuple-element.1075) | copy-start | bytes 24580
  33.6 87.2 %copy-start.105 = (f32[4,512]{1,0:T(4,128)}, f32[4,512]{1,0:T(4,128)S(1)}, u32[]{:S(2)}) copy-start(f32[4,512]{1,0:T(4,128)S(1)} %get-tuple-element.1073) | copy-start | bytes 24580
  33.6 87.2 %copy-start.107 = (f32[4,512]{1,0:T(4,128)}, f32[4,512]{1,0:T(4,128)S(1)}, u32[]{:S(2)}) copy-start(f32[4,512]{1,0:T(4,128)S(1)} %get-tuple-element.1074) | copy-start | bytes 24580
  33.9 219.7 %copy-start.59 = (pred[2,16,64,64]{2,3,1,0:T(8,128)(4,1)}, pred[2,16,64,64]{2,3,1,0:T(8,128)(4,1)S(1)}, u32[]{:S(2)}) copy-start(pred[2,16,64,64]{2,3,1,0:T(8,128)(4,1)S(1)} %compare_and_fusion.2) | copy-start | bytes 393220
  83.2 170.5 %copy-start.64 = (f32[2,16,4,64]{3,2,1,0:T(4,128)}, f32[2,16,4,64]{3,2,1,0:T(4,128)S(1)}, u32[]{:S(2)}) copy-start(f32[2,16,4,64]{3,2,1,0:T(4,128)S(1)} %copy.391) | copy-start | bytes 98308
  175.4 78.2 %copy-start.71 = (f32[2,16,4,64]{3,2,0,1:T(4,128)}, f32[2,16,4,64]{3,2,0,1:T(4,128)S(1)}, u32[]{:S(2)}) copy-start(f32[2,16,4,64]{3,2,0,1:T(4,128)S(1)} %get-tuple-element.1057) | copy-start | bytes 98308
  604.8 57.6 %copy-start.111 = (f32[1024]{0:T(1024)S(1)}, f32[1024]{0:T(1024)}, u32[]{:S(2)}) copy-start(f32[1024]{0:T(1024)} %param.28) | copy-start | bytes 12292
  604.8 117.0 %all-gather.7.cloned.1.call-start = ((), (), s32[]{:S(2)}) async-start(), calls=%async_computation.6 | async-start | bytes 6291456 | tf_op jit(solution)/shard_map/all_gather | solution.py:212
  662.7 213.8 %copy-start.99 = (f32[1024]{0:T(1024)}, f32[1024]{0:T(1024)S(1)}, u32[]{:S(2)}) copy-start(f32[1024]{0:T(1024)S(1)} %fusion.260) | copy-start | bytes 12292
  664.8 115.2 %all-gather.9.cloned.1.call-start = ((), (), s32[]{:S(2)}) async-start(), calls=%async_computation.8 | async-start | bytes 6291456 | tf_op jit(solution)/shard_map/all_gather | solution.py:229
  665.4 205.7 %reduce-scatter.9.cloned.1.call-start = ((), (), s32[]{:S(2)}) async-start(), calls=%async_computation.9 | async-start | bytes 6291456 | tf_op jit(solution)/shard_map/reduce_scatter | solution.py:239
  816.7 121.5 %all-gather.11.cloned.1.call-start = ((), (), s32[]{:S(2)}) async-start(), calls=%async_computation.10 | async-start | bytes 6291456 | tf_op jit(solution)/shard_map/all_gather | solution.py:247
  881.2 1335.8 %reduce-scatter.11.cloned.1.call-start = ((), (), s32[]{:S(2)}) async-start(), calls=%async_computation.11 | async-start | bytes 6291456 | tf_op jit(solution)/shard_map/reduce_scatter | solution.py:263
  881.3 74.7 %copy-start.85 = (f32[2048,4]{0,1:T(4,128)S(1)}, f32[2048,4]{0,1:T(4,128)}, u32[]{:S(2)}) copy-start(f32[2048,4]{0,1:T(4,128)} %copy-done.84) | copy-start | bytes 98308
  982.7 710.9 %copy-start.69 = (f32[64,64]{0,1:T(8,128)S(1)}, f32[64,64]{0,1:T(8,128)}, u32[]{:S(2)}) copy-start(f32[64,64]{0,1:T(8,128)} %copy-done.68) | copy-start | bytes 49156
  2049.9 210.3 %reduce-scatter.7.cloned.1.call-start = ((), (), s32[]{:S(2)}) async-start(), calls=%async_computation.7 | async-start | bytes 6291456 | tf_op jit(solution)/shard_map/reduce_scatter | solution.py:222
  2070.8 401.7 %all-reduce.27.cloned.1.call-start = ((), (), s32[]{:S(2)}) async-start(), calls=%async_computation.12 | async-start | bytes 34078720 | tf_op jit(solution)/shard_map/psum | solution.py:272
  2147.0 70.0 %copy-start.118 = (f32[1024]{0:T(1024)S(1)}, f32[1024]{0:T(1024)}, u32[]{:S(2)}) copy-start(f32[1024]{0:T(1024)} %copy-done.117) | copy-start | bytes 12292
  2147.0 70.0 %copy-start.123 = (f32[1024]{0:T(1024)S(1)}, f32[1024]{0:T(1024)}, u32[]{:S(2)}) copy-start(f32[1024]{0:T(1024)} %param.20) | copy-start | bytes 12292
  2147.7 73.3 %copy-start.129 = (f32[1024]{0:T(1024)S(1)}, f32[1024]{0:T(1024)}, u32[]{:S(2)}) copy-start(f32[1024]{0:T(1024)} %get-tuple-element.941) | copy-start | bytes 12292
  2147.7 73.3 %copy-start.135 = (f32[256]{0:T(256)S(1)}, f32[256]{0:T(256)}, u32[]{:S(2)}) copy-start(f32[256]{0:T(256)} %get-tuple-element.928) | copy-start | bytes 3076
  2147.7 112.5 %copy-start.122 = (f32[1024]{0:T(1024)S(1)}, f32[1024]{0:T(1024)}, u32[]{:S(2)}) copy-start(f32[1024]{0:T(1024)} %copy-done.121) | copy-start | bytes 12292
  2147.8 112.5 %copy-start.100 = (f32[1024]{0:T(1024)S(1)}, f32[1024]{0:T(1024)}, u32[]{:S(2)}) copy-start(f32[1024]{0:T(1024)} %copy-done.99) | copy-start | bytes 12292
  2147.8 112.5 %copy-start.112 = (f32[1024]{0:T(1024)S(1)}, f32[1024]{0:T(1024)}, u32[]{:S(2)}) copy-start(f32[1024]{0:T(1024)} %param.28) | copy-start | bytes 12292
  2147.8 112.5 %copy-start.120 = (f32[1024]{0:T(1024)S(1)}, f32[1024]{0:T(1024)}, u32[]{:S(2)}) copy-start(f32[1024]{0:T(1024)} %copy-done.119) | copy-start | bytes 12292
  (330 other events, 2022.6 us)
Sparse Core Ops, SparseCore 0:
  14.3 59.4 all-gather.4
  604.9 54.2 reduce-scatter.4
  665.0 56.7 all-gather.6
  723.2 56.7 all-gather.8
  816.8 54.3 reduce-scatter.8
  881.3 56.7 all-gather.10
  2050.0 54.2 reduce-scatter.10
  2106.8 54.3 reduce-scatter.6
  2166.9 305.5 all-reduce.26
where the time goes:
time: 2530 us; the launch traced here: 2510 us
  matrix products  1070 us (42%)
  waiting for transfers between devices  491 us (19%)
  local copies, waits for them, and re-layouts  451 us (18%)
  other arithmetic  377 us (15%)
  blocking collectives  103 us (4%)
    psum x1, waiting for transfers between devices, shards(): lax.psum(grad_in.astype(jnp.bfloat16), 'dp').astype(jnp.float32)  204 us
    squeeze x128, local copies, waits for them, and re-layouts, run_sequence(): lax.scan(jax.checkpoint(span_step), initial, (query_rows, key_vector, val...  169 us
    dot_general x64, matrix products, span_step(): jnp.einsum('afy,aym->afm', query_rows, current_state, precision=lax.Preci...  147 us
    dot_general x64, matrix products, span_step(): jnp.einsum('afy,aym->afm', key_vector, current_state, precision=lax.Preci...  141 us
    dot_general x15, matrix products, block_inverse(): jnp.einsum('abhts,abhsu->abhtu', power, power, precision=lax.Precision.HI...  130 us
    dot_general x15, matrix products, block_inverse(): jnp.einsum('abhts,abhsu->abhtu', result, identity_m + power, precision=la...  124 us
    dot_general x64, matrix products, span_step(): jnp.einsum('hts,hsv->htv', inverse, right_side, precision=lax.Precision.H...  100 us
    dot_general x64, matrix products, span_step(): jnp.einsum('htk,hsk->hts', query_rows, key_vector, precision=lax.Precisio...  99.7 us
  transfers between devices with their start and end apart: 9, of which 7 were waited for; matrix products, arithmetic and copies ran while one was open for 7% of the time, Pallas kernels for 0%

commit v1 on v0

v1 whole, which is shorter than its diff:
```python
import functools

import jax
import jax.numpy as jnp
from jax import lax
from jax.experimental import pallas as pl
from jax.experimental.pallas import tpu as pltpu
from jax.sharding import PartitionSpec as P

SEQ = 1024
BLOCK = 256
PART = 512
HALO = 16
F32 = jnp.float32
BF16 = jnp.bfloat16
VMEM_BYTES = 56 * 1024 * 1024


def dot_nn(left, right):
    return lax.dot_general(left, right, (((1,), (0,)), ((), ())), preferred_element_type=F32)


def dot_nt(left, right):
    return lax.dot_general(left, right, (((1,), (1,)), ((), ())), preferred_element_type=F32)


def dot_tn(left, right):
    return lax.dot_general(left, right, (((0,), (0,)), ((), ())), preferred_element_type=F32)


def sigmoid(values):
    return 0.5 * jnp.tanh(0.5 * values) + 0.5


def row_sum(values):
    return jnp.sum(values, axis=1, keepdims=True)


MASK, BACK, AHEAD, SEGMENT, PER_HEAD = 0, 1, 4, 7, 8
WRITE, CUM, START, LAST = 0, 1, 2, 3


def fill_level_masks(mask_ref):
    levels, width, unused_width = mask_ref.shape
    later = lax.broadcasted_iota(jnp.int32, (width, width), 0)
    earlier = lax.broadcasted_iota(jnp.int32, (width, width), 1)
    apart = later ^ earlier
    for level in range(levels):
        chosen = (later > earlier) & ((apart >> level) == 1)
        mask_ref[level] = jnp.where(chosen, 1.0, 0.0).astype(BF16)


def unit_lower_inverses(systems, mask_ref):
    width = systems[0].shape[0]
    identity = jnp.where(
        lax.broadcasted_iota(jnp.int32, (width, width), 0)
        == lax.broadcasted_iota(jnp.int32, (width, width), 1),
        1.0,
        0.0,
    ).astype(BF16)
    inverses = [identity - system * mask_ref[0] for system in systems]
    level = 1
    while (2 << level) <= width:
        size = 1 << level
        if size < 16:
            halves = [dot_nn(inv, system).astype(BF16) for inv, system in zip(inverses, systems)]
            joined = [dot_nn(half, inv).astype(BF16) for half, inv in zip(halves, inverses)]
            inverses = [inv - both * mask_ref[level] for inv, both in zip(inverses, joined)]
        elif (2 << level) < width:
            starts = range(size, width, 2 * size)
            odd = [
                jnp.concatenate([inv[at : at + size] for at in starts], axis=0) for inv in inverses
            ]
            halves = [dot_nn(rows, system).astype(BF16) for rows, system in zip(odd, systems)]
            joined = [dot_nn(half, inv).astype(BF16) for half, inv in zip(halves, inverses)]
            chosen = jnp.concatenate([mask_ref[level, at : at + size, :] for at in starts], axis=0)
            odd = [rows - both * chosen for rows, both in zip(odd, joined)]
            inverses = [
                jnp.concatenate(
                    [
                        part
                        for place, at in enumerate(starts)
                        for part in (
                            inv[at - size : at],
                            rows[place * size : (place + 1) * size],
                        )
                    ],
                    axis=0,
                )
                for inv, rows in zip(inverses, odd)
            ]
        else:
            halves = [
                dot_nn(inv[size:, size:], system[size:, :size]).astype(BF16)
                for inv, system in zip(inverses, systems)
            ]
            joined = [
                dot_nn(half, inv[:size, :size]).astype(BF16) for half, inv in zip(halves, inverses)
            ]
            inverses = [
                jnp.concatenate(
                    [inv[:size], jnp.concatenate([-both, inv[size:, size:]], axis=1)], axis=0
                )
                for inv, both in zip(inverses, joined)
            ]
        level += 1
    return inverses


def conv_rows(padded_ref, head, cols, conv_ref):
    width = cols.shape[0]
    taps = conv_ref.shape[1]
    shifted = [padded_ref[head, HALO : HALO + width, :]]
    for offset in range(1, taps):
        usable = cols[:, BACK + offset - 1 : BACK + offset]
        shifted.append(padded_ref[head, HALO - offset : HALO - offset + width, :] * usable)
    summed = shifted[0] * conv_ref[head, 0:1, :]
    for offset in range(1, taps):
        summed = summed + shifted[offset] * conv_ref[head, offset : offset + 1, :]
    return summed, shifted


def gap_offsets(cols, rows):
    width = cols.shape[0]
    later = lax.broadcasted_iota(jnp.int32, (width, width), 0)
    earlier = lax.broadcasted_iota(jnp.int32, (width, width), 1)
    inside = (cols[:, SEGMENT : SEGMENT + 1] == rows[0:1, :]) & (later >= earlier)
    return jnp.where(inside, 0.0, -1e30)


def head_column(cols, head, which):
    place = PER_HEAD + 4 * head + which
    return cols[:, place : place + 1]


def fill_halo(padded_ref, head, at, before_ref, halo_ref, first):
    mix_width = padded_ref.shape[2]

    @pl.when(first)
    def _():
        padded_ref[head, 0:HALO, :] = before_ref[:, at : at + mix_width].astype(F32)

    @pl.when(jnp.logical_not(first))
    def _():
        padded_ref[head, 0:HALO, :] = halo_ref[:, at : at + mix_width].astype(F32)


def fwd_kernel(
    proj_ref, halo_ref, before_ref, cols_ref, rows_ref, conv_ref, gain_ref, initial_ref,
    gated_ref, out_ref, written_ref, inverse_ref, start_ref, state_ref,
    padded_ref, mask_ref,
):
    heads, taps, mix_width = conv_ref.shape
    value_dim = gain_ref.shape[1]
    key_dim = (mix_width - value_dim) // 2
    in_width = mix_width + value_dim
    width = proj_ref.shape[0]
    block = pl.program_id(0)

    @pl.when(block == 0)
    def _():
        fill_level_masks(mask_ref)
        state_ref[...] = initial_ref[...]

    for h in range(heads):
        fill_halo(padded_ref, h, h * in_width, before_ref, halo_ref, block == 0)

    cols = cols_ref[...]
    rows = rows_ref[...]
    offsets = gap_offsets(cols, rows)
    every = range(heads)
    queries, keys, values = [], [], []
    for h in every:
        at = h * in_width
        padded_ref[h, HALO : HALO + width, :] = proj_ref[:, at : at + mix_width].astype(F32)
        summed, unused_rows = conv_rows(padded_ref, h, cols, conv_ref)
        mixed = summed * sigmoid(summed)
        query = mixed[:, :key_dim]
        key = mixed[:, key_dim : 2 * key_dim]
        query = query * (lax.rsqrt(row_sum(query * query) + 1e-06) * key_dim ** (-0.5))
        key = key * lax.rsqrt(row_sum(key * key) + 1e-06)
        queries.append(query.astype(BF16))
        keys.append(key)
        values.append(mixed[:, 2 * key_dim :])
    keys_low = [key.astype(BF16) for key in keys]
    stacked = [jnp.concatenate([k, q], axis=0) for k, q in zip(keys_low, queries)]
    products = [dot_nt(both, key) for both, key in zip(stacked, keys_low)]
    weights = [
        jnp.exp(head_column(cols, h, CUM) - rows[1 + h : 2 + h, :] + offsets) for h in every
    ]
    systems = [
        (products[h][:width] * weights[h] * head_column(cols, h, WRITE)).astype(BF16)
        for h in every
    ]
    reads = [(products[h][width:] * weights[h]).astype(BF16) for h in every]
    inverses = unit_lower_inverses(systems, mask_ref)
    states = [state_ref[h] for h in every]
    states_low = [state.astype(BF16) for state in states]
    from_state = [dot_nn(both, state) for both, state in zip(stacked, states_low)]
    right = [
        (
            head_column(cols, h, WRITE)
            * (values[h] - head_column(cols, h, START) * from_state[h][:width])
        ).astype(BF16)
        for h in every
    ]
    written = [dot_nn(inv, side).astype(BF16) for inv, side in zip(inverses, right)]
    inner = [dot_nn(read, value) for read, value in zip(reads, written)]
    added = [
        dot_tn((keys[h] * head_column(cols, h, LAST)).astype(BF16), written[h]) for h in every
    ]
    keep = cols[:, MASK : MASK + 1]
    for h in every:
        start_ref[0, h] = states_low[h]
        inverse_ref[0, h] = inverses[h]
        written_ref[:, h * value_dim : (h + 1) * value_dim] = written[h]
        final = head_column(cols, h, START)[width - 1 : width, :]
        state_ref[h] = final * states[h] + added[h]
        out = (inner[h] + head_column(cols, h, START) * from_state[h][width:]) * keep
        out_ref[:, h * value_dim : (h + 1) * value_dim] = out.astype(BF16)
        scale = lax.rsqrt(row_sum(out * out) * (1.0 / value_dim) + 1e-05)
        at = h * in_width + mix_width
        gate = proj_ref[:, at : at + value_dim].astype(F32)
        gated = out * scale * gain_ref[...] * (gate * sigmoid(gate))
        gated_ref[:, h * value_dim : (h + 1) * value_dim] = gated.astype(BF16)


def bwd_kernel(
    cot_ref, proj_ref, halo_ref, before_ref, cols_ref, rows_ref, conv_ref, gain_ref,
    out_ref, written_ref, inverse_ref, start_ref, initial_ref, after_ref,
    grad_ref, tokens_ref, colsum_ref, conv_grad_ref, gain_grad_ref, state_ref, stash_ref,
    padded_ref, ahead_ref,
):
    heads, taps, mix_width = conv_ref.shape
    value_dim = gain_ref.shape[1]
    key_dim = (mix_width - value_dim) // 2
    in_width = mix_width + value_dim
    width = proj_ref.shape[0]
    step = pl.program_id(0)

    @pl.when(step == 0)
    def _():
        conv_grad_ref[...] = jnp.zeros_like(conv_grad_ref)
        gain_grad_ref[...] = jnp.zeros_like(gain_grad_ref)
        state_ref[...] = initial_ref[...]
        ahead_ref[:, width : width + HALO, :] = after_ref[...]

    for h in range(heads):
        fill_halo(
            padded_ref, h, h * in_width, before_ref, halo_ref, step == pl.num_programs(0) - 1
        )

    cols = cols_ref[...]
    rows = rows_ref[...]
    offsets = gap_offsets(cols, rows)
    every = range(heads)
    keep = cols[:, MASK : MASK + 1]
    strict = (
        lax.broadcasted_iota(jnp.int32, (width, width), 0)
        > lax.broadcasted_iota(jnp.int32, (width, width), 1)
    )

    cots, gain_grad = [], jnp.zeros((1, value_dim), F32)
    for h in every:
        at = h * in_width + mix_width
        cot = cot_ref[:, h * value_dim : (h + 1) * value_dim].astype(F32)
        out = out_ref[:, h * value_dim : (h + 1) * value_dim].astype(F32)
        gate = proj_ref[:, at : at + value_dim].astype(F32)
        scale = lax.rsqrt(row_sum(out * out) * (1.0 / value_dim) + 1e-05)
        gate_sig = sigmoid(gate)
        normed = out * scale
        through = cot * gate * gate_sig
        gain_grad = gain_grad + jnp.sum(through * normed, axis=0, keepdims=True)
        grad_normed = through * gain_ref[...]
        mean = row_sum(grad_normed * normed) * (1.0 / value_dim)
        cots.append((scale * (grad_normed - normed * mean) * keep))
        grad_gate = cot * normed * gain_ref[...] * gate_sig * (1.0 + gate * (1.0 - gate_sig))
        grad_ref[:, at : at + value_dim] = grad_gate.astype(BF16)
    gain_grad_ref[...] += gain_grad

    queries, keys = [], []
    for h in every:
        at = h * in_width
        padded_ref[h, HALO : HALO + width, :] = proj_ref[:, at : at + mix_width].astype(F32)
        summed, unused_rows = conv_rows(padded_ref, h, cols, conv_ref)
        qk = summed[:, : 2 * key_dim]
        mixed = qk * sigmoid(qk)
        query = mixed[:, :key_dim]
        key = mixed[:, key_dim:]
        query = query * (lax.rsqrt(row_sum(query * query) + 1e-06) * key_dim ** (-0.5))
        key = key * lax.rsqrt(row_sum(key * key) + 1e-06)
        queries.append(query)
        keys.append(key)
        ahead_ref[h, 0:width, :] = summed
    keys_low = [key.astype(BF16) for key in keys]
    queries_low = [query.astype(BF16) for query in queries]
    products = [
        dot_nt(jnp.concatenate([k, q], axis=0), k) for k, q in zip(keys_low, queries_low)
    ]
    weights = [
        jnp.exp(head_column(cols, h, CUM) - rows[1 + h : 2 + h, :] + offsets) for h in every
    ]
    cots_low = [cot.astype(BF16) for cot in cots]
    grad_states = [state_ref[h] for h in every]
    grad_states_low = [state.astype(BF16) for state in grad_states]
    written = [written_ref[:, h * value_dim : (h + 1) * value_dim] for h in every]
    reads = [(products[h][width:] * weights[h]).astype(BF16) for h in every]
    last_keys = [keys[h] * head_column(cols, h, LAST) for h in every]
    grad_written = [
        (
            dot_tn(reads[h], cots_low[h]) + dot_nn(last_keys[h].astype(BF16), grad_states_low[h])
        ).astype(BF16)
        for h in every
    ]
    grad_right = [dot_tn(inverse_ref[0, h], grad_written[h]) for h in every]
    grad_values = [grad_right[h] * head_column(cols, h, WRITE) for h in every]
    against = [
        dot_nt(jnp.concatenate([cots_low[h], grad_right[h].astype(BF16)], axis=0), written[h])
        for h in every
    ]
    grad_reads = [against[h][:width] * weights[h] for h in every]
    grad_pairs = [
        jnp.where(strict, against[h][width:] * weights[h], 0.0) * -head_column(cols, h, WRITE)
        for h in every
    ]
    gaps = [
        grad_reads[h] * products[h][width:] + grad_pairs[h] * products[h][:width] for h in every
    ]
    starts = [
        jnp.concatenate(
            [
                (cots[h] * head_column(cols, h, START)).astype(BF16),
                (grad_values[h] * -head_column(cols, h, START)).astype(BF16),
            ],
            axis=0,
        )
        for h in every
    ]
    both_grads = [
        jnp.concatenate([grad_reads[h].astype(BF16), grad_pairs[h].astype(BF16)], axis=0)
        for h in every
    ]
    by_key = [dot_nn(both_grads[h], keys_low[h]) for h in every]
    by_state = [dot_nt(starts[h], start_ref[0, h]) for h in every]
    both_rows = [
        jnp.concatenate([queries_low[h], keys_low[h]], axis=0) for h in every
    ]
    turned = [dot_tn(both_grads[h], both_rows[h]) for h in every]
    by_last = [dot_nt(written[h], grad_states_low[h]) for h in every]
    states_part = [dot_tn(both_rows[h], starts[h]) for h in every]

    lane = lax.broadcasted_iota(jnp.int32, tokens_ref.shape, 1)
    place = lax.broadcasted_iota(jnp.int32, (width, 1), 0)
    packed = jnp.zeros(tokens_ref.shape, F32)
    for h in every:
        from_state = by_state[h]
        grad_query = by_key[h][:width] + from_state[:width]
        grad_key = (
            by_key[h][width:]
            + from_state[width:]
            + turned[h]
            + by_last[h] * head_column(cols, h, LAST)
        )
        log_last = row_sum(by_last[h] * last_keys[h])
        log_start = row_sum(queries[h] * from_state[:width] + keys[h] * from_state[width:])
        final = head_column(cols, h, START)[width - 1 : width, :]
        start_f32 = start_ref[0, h].astype(F32)
        total = jnp.sum(log_last, axis=0, keepdims=True) + final * jnp.sum(
            row_sum(start_f32 * grad_states[h]), axis=0, keepdims=True
        )
        grad_cum = row_sum(gaps[h]) + log_start - log_last + jnp.where(
            place == width - 1, total, 0.0
        )
        grad_logit = row_sum(grad_right[h] * written[h].astype(F32))
        packed = packed + jnp.where(lane == 2 * h, grad_cum, 0.0)
        packed = packed + jnp.where(lane == 2 * h + 1, grad_logit, 0.0)
        colsum_ref[h : h + 1, :] = jnp.sum(gaps[h], axis=0, keepdims=True)
        state_ref[h] = final * grad_states[h] + states_part[h]

        summed = ahead_ref[h, 0:width, :]
        sig = sigmoid(summed)
        slope = sig * (1.0 + summed * (1.0 - sig))
        mixed = summed[:, : 2 * key_dim] * sig[:, : 2 * key_dim]
        query = mixed[:, :key_dim]
        key = mixed[:, key_dim:]
        query_scale = lax.rsqrt(row_sum(query * query) + 1e-06)
        key_scale = lax.rsqrt(row_sum(key * key) + 1e-06)
        grad_query = grad_query * key_dim ** (-0.5)
        query_unit = query * query_scale
        key_unit = key * key_scale
        grad_query = query_scale * (grad_query - query_unit * row_sum(grad_query * query_unit))
        grad_key = key_scale * (grad_key - key_unit * row_sum(grad_key * key_unit))
        ahead_ref[h, 0:width, 0:key_dim] = grad_query * slope[:, :key_dim]
        ahead_ref[h, 0:width, key_dim : 2 * key_dim] = (
            grad_key * slope[:, key_dim : 2 * key_dim]
        )
        ahead_ref[h, 0:width, 2 * key_dim :] = grad_values[h] * slope[:, 2 * key_dim :]
        grad_summed = ahead_ref[h, 0:width, :]
        at = h * in_width
        grad_pre = grad_summed * conv_ref[h, 0:1, :]
        conv_grad_ref[h, 0:1, :] += jnp.sum(
            grad_summed * padded_ref[h, HALO : HALO + width, :], axis=0, keepdims=True
        )
        for offset in range(1, taps):
            usable = cols[:, AHEAD + offset - 1 : AHEAD + offset]
            later = ahead_ref[h, offset : offset + width, :] * usable
            grad_pre = grad_pre + later * conv_ref[h, offset : offset + 1, :]
            back = cols[:, BACK + offset - 1 : BACK + offset]
            earlier = padded_ref[h, HALO - offset : HALO - offset + width, :] * back
            conv_grad_ref[h, offset : offset + 1, :] += jnp.sum(
                grad_summed * earlier, axis=0, keepdims=True
            )
        grad_ref[:, at : at + mix_width] = grad_pre.astype(BF16)
        ahead_ref[h, width : width + HALO, :] = ahead_ref[h, 0:HALO, :]
        stash_ref[h] = ahead_ref[h, 0:HALO, :]
    tokens_ref[...] = packed


def segment_tables(segments, pad_mask, width):
    length = segments.shape[0]
    place = jnp.arange(length, dtype=jnp.int32)

    def moved(array, by):
        if by > 0:
            return jnp.concatenate([jnp.full((by,), -1, array.dtype), array[:-by]])
        return jnp.concatenate([array[-by:], jnp.full((-by,), -1, array.dtype)])

    back = [
        ((moved(segments, by) == segments) & (place >= by)).astype(F32) for by in (1, 2, 3)
    ]
    ahead = [
        ((moved(segments, -by) == segments) & (place + by < length)).astype(F32)
        for by in (1, 2, 3)
    ]
    seg_blocks = segments.reshape(-1, width)
    ends = seg_blocks[:, -1]
    carried = (seg_blocks == moved(ends, 1)[:, None]).astype(F32).reshape(-1)
    to_last = (seg_blocks == ends[:, None]).astype(F32).reshape(-1)
    return jnp.stack(
        [pad_mask.astype(F32), *back, *ahead, segments.astype(F32), carried, to_last]
    )


def token_tables(rate_rows, table, decay_log, decay_bias, width):
    heads, length = rate_rows.shape[1:]
    write = jax.nn.sigmoid(rate_rows[1]) * table[0]
    log_decay = -jnp.exp(decay_log)[:, None] * jax.nn.softplus(
        rate_rows[0] + decay_bias[:, None]
    )
    upper = jnp.triu(jnp.ones((width, width), F32))
    cum = jnp.dot(
        log_decay.reshape(-1, width), upper, precision=lax.Precision.HIGHEST
    ).reshape(heads, length)
    cum_blocks = cum.reshape(heads, -1, width)
    start = jnp.exp(cum) * table[8]
    last = jnp.exp(cum_blocks[:, :, -1:] - cum_blocks).reshape(heads, length) * table[9]
    per_head = jnp.stack([write, cum, start, last], axis=1).reshape(4 * heads, length)
    cols = jnp.concatenate([table[:8], per_head]).T
    rows = jnp.concatenate(
        [table[7:8], cum, jnp.zeros((-(1 + heads) % 8, length), F32)], axis=0
    )
    return cols, rows, log_decay


def whole_block(array):
    return pl.BlockSpec(array.shape, lambda c: (0,) * array.ndim)


def mixer_forward(proj, before, cols, rows, conv, gain, initial, width):
    heads, taps, mix_width = conv.shape
    value_dim = gain.shape[1]
    key_dim = (mix_width - value_dim) // 2
    length = proj.shape[0]
    steps = length // width

    def here(c):
        return (c, 0)

    def halo(c):
        return (jnp.maximum(c * (width // HALO) - 1, 0), 0)

    levels = width.bit_length() - 1
    wide = pl.BlockSpec((width, heads * value_dim), here)
    wide_shape = jax.ShapeDtypeStruct((length, heads * value_dim), BF16)
    return pl.pallas_call(
        fwd_kernel,
        grid=(steps,),
        in_specs=[
            pl.BlockSpec((width, proj.shape[1]), here),
            pl.BlockSpec((HALO, proj.shape[1]), halo),
            whole_block(before),
            pl.BlockSpec((width, cols.shape[1]), here),
            pl.BlockSpec((rows.shape[0], width), lambda c: (0, c)),
            whole_block(conv),
            whole_block(gain),
            whole_block(initial),
        ],
        out_specs=[
            wide,
            wide,
            wide,
            pl.BlockSpec((1, heads, width, width), lambda c: (c, 0, 0, 0)),
            pl.BlockSpec((1, heads, key_dim, value_dim), lambda c: (c, 0, 0, 0)),
            whole_block(initial),
        ],
        out_shape=[
            wide_shape,
            wide_shape,
            wide_shape,
            jax.ShapeDtypeStruct((steps, heads, width, width), BF16),
            jax.ShapeDtypeStruct((steps, heads, key_dim, value_dim), BF16),
            jax.ShapeDtypeStruct(initial.shape, F32),
        ],
        scratch_shapes=[
            pltpu.VMEM((heads, HALO + width, mix_width), F32),
            pltpu.VMEM((levels, width, width), BF16),
        ],
        compiler_params=pltpu.CompilerParams(vmem_limit_bytes=VMEM_BYTES),
        cost_estimate=pl.CostEstimate(
            flops=heads * steps * 16 * width * width * value_dim,
            bytes_accessed=6 * length * heads * in_total(conv, gain),
            transcendentals=0,
        ),
        name="mixer_forward",
    )(proj, proj, before, cols, rows, conv, gain, initial)


def in_total(conv, gain):
    return conv.shape[2] + gain.shape[1]


def mixer_backward(cot, proj, before, cols, rows, conv, gain, kept, initial, after, width):
    out, written, inverse, start = kept
    heads, taps, mix_width = conv.shape
    value_dim = gain.shape[1]
    key_dim = (mix_width - value_dim) // 2
    length = proj.shape[0]
    steps = length // width

    def at(c):
        return steps - 1 - c

    def here(c):
        return (at(c), 0)

    def halo(c):
        return (jnp.maximum(at(c) * (width // HALO) - 1, 0), 0)

    wide = pl.BlockSpec((width, heads * value_dim), here)
    sums = -(-heads // 8) * 8
    return pl.pallas_call(
        bwd_kernel,
        grid=(steps,),
        in_specs=[
            wide,
            pl.BlockSpec((width, proj.shape[1]), here),
            pl.BlockSpec((HALO, proj.shape[1]), halo),
            whole_block(before),
            pl.BlockSpec((width, cols.shape[1]), here),
            pl.BlockSpec((rows.shape[0], width), lambda c: (0, at(c))),
            whole_block(conv),
            whole_block(gain),
            wide,
            wide,
            pl.BlockSpec((1, heads, width, width), lambda c: (at(c), 0, 0, 0)),
            pl.BlockSpec((1, heads, key_dim, value_dim), lambda c: (at(c), 0, 0, 0)),
            whole_block(initial),
            whole_block(after),
        ],
        out_specs=[
            pl.BlockSpec((width, proj.shape[1]), here),
            pl.BlockSpec((width, 2 * heads), here),
            pl.BlockSpec((sums, width), lambda c: (0, at(c))),
            whole_block(conv),
            whole_block(gain),
            whole_block(initial),
            whole_block(after),
        ],
        out_shape=[
            jax.ShapeDtypeStruct(proj.shape, BF16),
            jax.ShapeDtypeStruct((length, 2 * heads), F32),
            jax.ShapeDtypeStruct((sums, length), F32),
            jax.ShapeDtypeStruct(conv.shape, F32),
            jax.ShapeDtypeStruct(gain.shape, F32),
            jax.ShapeDtypeStruct(initial.shape, F32),
            jax.ShapeDtypeStruct(after.shape, F32),
        ],
        scratch_shapes=[
            pltpu.VMEM((heads, HALO + width, mix_width), F32),
            pltpu.VMEM((heads, width + HALO, mix_width), F32),
        ],
        compiler_params=pltpu.CompilerParams(vmem_limit_bytes=VMEM_BYTES),
        cost_estimate=pl.CostEstimate(
            flops=heads * steps * 16 * width * width * value_dim,
            bytes_accessed=8 * length * heads * in_total(conv, gain),
            transcendentals=0,
        ),
        name="mixer_backward",
    )(cot, proj, proj, before, cols, rows, conv, gain, out, written, inverse, start, initial, after)


def rate_gradients(tokens, colsum, rate_rows, mask_row, decay_log, decay_bias, log_decay, width):
    heads, length = log_decay.shape
    turned = tokens.T.reshape(heads, 2, length)
    grad_cum = turned[:, 0] - colsum[:heads]
    lower = jnp.tril(jnp.ones((width, width), F32))
    grad_log_decay = jnp.dot(
        grad_cum.reshape(-1, width), lower, precision=lax.Precision.HIGHEST
    ).reshape(heads, length)
    shifted = rate_rows[0] + decay_bias[:, None]
    grad_decay = grad_log_decay * -jnp.exp(decay_log)[:, None] * jax.nn.sigmoid(shifted)
    grad_write = turned[:, 1] * (1.0 - jax.nn.sigmoid(rate_rows[1])) * mask_row
    return (
        jnp.stack([grad_decay, grad_write]),
        jnp.sum(grad_log_decay * log_decay, axis=1),
        jnp.sum(grad_decay, axis=1),
    )


def ffn_kernel(
    second_ref, second_turned_ref, cot_ref, cot_turned_ref, gate_ref, up_ref, down_ref,
    sum_ref, back_ref, grads_ref,
):
    shares, unused_kinds, rows, tile = grads_ref.shape

    @pl.when(pl.program_id(0) == 0)
    def _():
        sum_ref[...] = jnp.zeros_like(sum_ref)
        back_ref[...] = jnp.zeros_like(back_ref)

    gate = dot_nn(second_ref[...], gate_ref[...])
    up = dot_nn(second_ref[...], up_ref[...])
    grad_hidden = dot_nn(cot_ref[...], down_ref[...])
    sig = sigmoid(gate)
    active = gate * sig
    hidden = (active * up).astype(BF16)
    grad_up = (grad_hidden * active).astype(BF16)
    grad_gate = (grad_hidden * up * sig * (1.0 + gate * (1.0 - sig))).astype(BF16)
    sum_ref[...] += dot_nt(hidden, down_ref[...])
    back_ref[...] += dot_nt(grad_gate, gate_ref[...]) + dot_nt(grad_up, up_ref[...])
    for kind, (turned_ref, right) in enumerate(
        ((second_turned_ref, grad_gate), (second_turned_ref, grad_up), (cot_turned_ref, hidden))
    ):
        grads_ref[:, kind] = (
            dot_nn(turned_ref[...], right).astype(BF16).reshape(shares, rows, tile)
        )


def feed_forward(second, second_turned, cot, weights, shares):
    length, model_width = second.shape
    hidden = weights.shape[1] // 3
    tile = 256
    tiles = hidden // tile
    square = jax.ShapeDtypeStruct((length, model_width), F32)
    rows = model_width // shares

    def third(kind):
        return pl.BlockSpec((model_width, tile), lambda j: (0, kind * tiles + j))

    turned = (second_turned, cot.T)
    return pl.pallas_call(
        ffn_kernel,
        grid=(tiles,),
        in_specs=[
            whole_block(second),
            whole_block(turned[0]),
            whole_block(cot),
            whole_block(turned[1]),
            third(0),
            third(1),
            third(2),
        ],
        out_specs=[
            whole_block(square),
            whole_block(square),
            pl.BlockSpec((shares, 3, rows, tile), lambda j: (0, 0, 0, j)),
        ],
        out_shape=[square, square, jax.ShapeDtypeStruct((shares, 3, rows, hidden), BF16)],
        compiler_params=pltpu.CompilerParams(vmem_limit_bytes=VMEM_BYTES),
        cost_estimate=pl.CostEstimate(
            flops=6 * length * model_width * hidden,
            bytes_accessed=12 * model_width * hidden,
            transcendentals=0,
        ),
        name="feed_forward",
    )(second, turned[0], cot, turned[1], weights, weights, weights)


def in_grad_kernel(count, *refs):
    low_refs, refs, grad_ref, turned_ref = (
        refs[:count], refs[count : 2 * count], refs[-2], refs[-1]
    )
    size = refs[0].shape[0]

    @pl.when(pl.program_id(0) == 0)
    def _():
        for place, ref in enumerate(low_refs):
            turned_ref[:, place * size : (place + 1) * size] = (
                ref[...].astype(F32).T.astype(BF16)
            )

    total = dot_nn(turned_ref[:, 0:size], refs[0][...])
    for place, ref in enumerate(refs[1:], 1):
        total = total + dot_nn(turned_ref[:, place * size : (place + 1) * size], ref[...])
    grad_ref[...] = total.astype(BF16)


def in_grad(lows, parts, tile):
    size, model_width = lows[0].shape
    columns = parts[0].shape[1]
    return pl.pallas_call(
        functools.partial(in_grad_kernel, len(parts)),
        grid=(columns // tile,),
        in_specs=[whole_block(low) for low in lows]
        + [pl.BlockSpec((size, tile), lambda j: (0, j)) for unused in parts],
        out_specs=pl.BlockSpec((model_width, tile), lambda j: (0, j)),
        out_shape=jax.ShapeDtypeStruct((model_width, columns), BF16),
        scratch_shapes=[pltpu.VMEM((model_width, size * len(parts)), BF16)],
        compiler_params=pltpu.CompilerParams(vmem_limit_bytes=VMEM_BYTES),
        cost_estimate=pl.CostEstimate(
            flops=2 * model_width * size * columns,
            bytes_accessed=2 * model_width * columns,
            transcendentals=0,
        ),
        name="in_grad",
    )(*lows, *parts)


ROWS = 256


def norm_kernel(rows_ref, gain_ref, low_ref):
    rows = rows_ref[...].astype(F32)
    scale = lax.rsqrt(row_sum(rows * rows) * (1.0 / rows.shape[1]) + 1e-05)
    low_ref[...] = (rows * scale * gain_ref[...]).astype(BF16)


def part_specs(parts):
    specs, starts, start = [], [], 0
    for part in parts:
        blocks = part.shape[0] // ROWS
        specs.append(
            pl.BlockSpec(
                (ROWS, part.shape[1]),
                lambda i, start=start, blocks=blocks: (jnp.clip(i - start, 0, blocks - 1), 0),
            )
        )
        starts.append(start)
        start += blocks
    return specs, starts


def gathered_rows(part_refs, starts, total_ref):
    block = pl.program_id(0)
    for refs, start, end in zip(part_refs, starts, starts[1:] + [1 << 30]):

        @pl.when((block >= start) & (block < end))
        def _(refs=refs):
            total = refs[0][...].astype(F32)
            for ref in refs[1:]:
                total = total + ref[...].astype(F32)
            total_ref[...] = total

    return total_ref[...]


def middle_kernel(starts, per_part, rows_ref, gain_ref, *refs):
    part_refs = refs[: len(starts) * per_part]
    middle_ref, second_ref, turned_ref, total_ref = refs[len(part_refs) :]
    grouped = [part_refs[at : at + per_part] for at in range(0, len(part_refs), per_part)]
    middle = rows_ref[...].astype(F32) + gathered_rows(grouped, starts, total_ref)
    scale = lax.rsqrt(row_sum(middle * middle) * (1.0 / middle.shape[1]) + 1e-05)
    second = middle * scale * gain_ref[...]
    middle_ref[...] = middle
    second_ref[...] = second.astype(BF16)
    turned_ref[...] = second.T.astype(BF16)


def norm_back(rows, gain, grad):
    width = rows.shape[1]
    scale = lax.rsqrt(row_sum(rows * rows) * (1.0 / width) + 1e-05)
    unit = rows * scale
    through = grad * gain
    grad_rows = scale * (through - unit * (row_sum(through * unit) * (1.0 / width)))
    return grad_rows, jnp.sum(grad * unit, axis=0, keepdims=True)


def add_rows(total_ref, row):
    @pl.when(pl.program_id(0) == 0)
    def _():
        total_ref[...] = jnp.zeros_like(total_ref)

    total_ref[...] += row


def second_back_kernel(
    back_ref, middle_ref, cot_ref, sum_ref, gain_ref, out_ref, grad_ref, low_ref, gain_grad_ref
):
    middle = middle_ref[...]
    out_ref[...] = (middle + sum_ref[...]).astype(BF16)
    grad_rows, gain_grad = norm_back(middle, gain_ref[...], back_ref[...])
    add_rows(gain_grad_ref, gain_grad)
    grad_middle = cot_ref[...].astype(F32) + grad_rows
    grad_ref[...] = grad_middle
    low_ref[...] = grad_middle.astype(BF16)


def first_back_kernel(starts, per_part, rows_ref, middle_grad_ref, gain_ref, *refs):
    part_refs = refs[: len(starts) * per_part]
    grad_ref, gain_grad_ref, total_ref = refs[len(part_refs) :]
    grouped = [part_refs[at : at + per_part] for at in range(0, len(part_refs), per_part)]
    grad = gathered_rows(grouped, starts, total_ref)
    grad_rows, gain_grad = norm_back(rows_ref[...].astype(F32), gain_ref[...], grad)
    add_rows(gain_grad_ref, gain_grad)
    grad_ref[...] = (middle_grad_ref[...] + grad_rows).astype(BF16)


def row_call(kernel, rows, operands, outs, scratch, name):
    width = rows[1]
    block = pl.BlockSpec((ROWS, width), lambda i: (i, 0))
    kinds = {
        "rows": (block, (rows[0], width)),
        "turned": (pl.BlockSpec((width, ROWS), lambda i: (0, i)), (width, rows[0])),
        "gain": (pl.BlockSpec((1, width), lambda i: (0, 0)), (1, width)),
    }
    return pl.pallas_call(
        kernel,
        grid=(rows[0] // ROWS,),
        in_specs=[block if spec is None else spec for unused, spec in operands],
        out_specs=[kinds[kind][0] for kind, unused in outs],
        out_shape=[jax.ShapeDtypeStruct(kinds[kind][1], dtype) for kind, dtype in outs],
        scratch_shapes=scratch,
        compiler_params=pltpu.CompilerParams(vmem_limit_bytes=VMEM_BYTES),
        name=name,
    )(*[array for array, unused in operands])


def norm_rows(rows, gain):
    gain = gain[None]
    return row_call(
        norm_kernel, rows.shape, [(rows, None), (gain, whole_block(gain))], [("rows", BF16)], [], "norm_rows"
    )[0]


def middle_rows(rows, gain, parts):
    gain = gain[None]
    specs, starts = part_specs([terms[0] for terms in parts])
    operands = [(rows, None), (gain, whole_block(gain))]
    for terms, spec in zip(parts, specs):
        operands += [(term, spec) for term in terms]
    return row_call(
        functools.partial(middle_kernel, starts, len(parts[0])),
        rows.shape,
        operands,
        [("rows", F32), ("rows", BF16), ("turned", BF16)],
        [pltpu.VMEM((ROWS, rows.shape[1]), F32)],
        "middle_rows",
    )


def second_back(back, middle, cot, ffn_out, gain):
    gain = gain[None]
    return row_call(
        second_back_kernel,
        middle.shape,
        [(back, None), (middle, None), (cot, None), (ffn_out, None), (gain, whole_block(gain))],
        [("rows", BF16), ("rows", F32), ("rows", BF16), ("gain", F32)],
        [],
        "second_back",
    )


def first_back(rows, grad_middle, gain, parts):
    gain = gain[None]
    specs, starts = part_specs([terms[0] for terms in parts])
    operands = [(rows, None), (grad_middle, None), (gain, whole_block(gain))]
    for terms, spec in zip(parts, specs):
        operands += [(term, spec) for term in terms]
    return row_call(
        functools.partial(first_back_kernel, starts, len(parts[0])),
        rows.shape,
        operands,
        [("rows", BF16), ("gain", F32)],
        [pltpu.VMEM((ROWS, rows.shape[1]), F32)],
        "first_back",
    )


def after(array, other):
    return lax.optimization_barrier((array, other))[0]


def turn(array, axis, shift):
    size = lax.axis_size(axis)
    return lax.ppermute(array, axis, [((i + shift) % size, i) for i in range(size)])


def partner(array, axis, bit):
    return lax.ppermute(array, axis, [(i, i ^ bit) for i in range(lax.axis_size(axis))])


def is_power(size):
    return size & (size - 1) == 0


def sum_small(array, axis):
    size = lax.axis_size(axis)
    if not is_power(size):
        return lax.psum(array, axis)
    bit = 1
    while bit < size:
        array = array + partner(array, axis, bit)
        bit *= 2
    return array


def scatter_sum_dp(array, meanwhile=None):
    size = lax.axis_size("dp")
    if not is_power(size):
        return lax.psum_scatter(array, "dp", scatter_dimension=0, tiled=True)
    index = lax.axis_index("dp")
    columns = array.shape[1]
    blocks = array.reshape(size, -1, columns)
    bit = 1
    while bit < size:
        halves = blocks.reshape(-1, 2, blocks.shape[1], columns)
        mine = (index // bit) % 2
        keep = lax.dynamic_index_in_dim(halves, mine, 1, keepdims=False)
        send = lax.dynamic_index_in_dim(halves, 1 - mine, 1, keepdims=False)
        other = partner(send, "dp", bit)
        if bit == 2 and meanwhile is not None:
            other = after(other, meanwhile)
        blocks = keep + other
        bit *= 2
    return blocks[0]


def shards(
    residual_in,
    mixer_gain,
    in_weight,
    rate_weight,
    conv_weight,
    decay_log,
    decay_bias,
    head_gain,
    out_weight,
    ffn_gain,
    gate_up,
    down_weight,
    segments,
    pad_mask,
    out_grad,
):
    rows_here, model_width = residual_in.shape
    heads_here, in_width = in_weight.shape[1:]
    hidden_here = gate_up.shape[2]
    members = lax.axis_size("tensor")
    share = lax.axis_size("dp")
    index = lax.axis_index("dp")
    pair = members == 2 and rows_here == SEQ
    value_dim = head_gain.shape[0]
    key_dim = (conv_weight.shape[2] - value_dim) // 2

    def sequences(rows):
        if pair:
            own = [rows[at : at + PART] for at in range(0, SEQ, PART)]
            return [own, [turn(part, "tensor", 1) for part in own]]
        whole = lax.all_gather(rows, "tensor", axis=0, tiled=True)
        return [
            [whole[at + by : at + by + PART] for by in range(0, SEQ, PART)]
            for at in range(0, whole.shape[0], SEQ)
        ]

    def token_parts(array):
        if pair:
            own = lax.axis_index("tensor")
            return [
                lax.dynamic_slice_in_dim(array, which * SEQ, SEQ) for which in (own, 1 - own)
            ]
        return [array[at : at + SEQ] for at in range(0, array.shape[0], SEQ)]

    def owner_parts(parts):
        if pair:
            return [[mine, other] for mine, other in zip(*parts)]
        return [
            [
                lax.psum_scatter(
                    jnp.concatenate([part for here in parts for part in here]).astype(BF16),
                    "tensor",
                    scatter_dimension=0,
                    tiled=True,
                )
            ]
        ]

    w_in = in_weight.reshape(model_width, heads_here * in_width)
    w_rate = rate_weight.transpose(2, 1, 0).reshape(2 * heads_here, model_width)
    w_out = out_weight.reshape(-1, model_width)
    conv_float = conv_weight.astype(F32)
    gain_row = head_gain[None]
    normed = norm_rows(residual_in, mixer_gain)

    rows_share = model_width // share
    gate_up_piece = lax.dynamic_slice_in_dim(gate_up, index * rows_share, rows_share)
    piece = jnp.stack(
        [
            gate_up_piece[:, 0],
            gate_up_piece[:, 1],
            lax.dynamic_slice_in_dim(down_weight, index * rows_share, rows_share, axis=1).T,
        ]
    )
    pieces = [piece] + [
        after(turn(piece, "tensor", shift), normed) for shift in range(1, members)
    ]
    pieces = jnp.concatenate(
        [part[kind] for kind in range(3) for part in pieces], axis=1
    )
    weights = lax.all_gather(pieces, "dp", axis=0, tiled=True)
    first = sequences(normed)


    tables = [
        segment_tables(seg, mask, BLOCK)
        for seg, mask in zip(token_parts(segments), token_parts(pad_mask))
    ]
    local = len(first)
    count = SEQ // PART
    states = [jnp.zeros((heads_here, key_dim, value_dim), F32)] * local
    befores = [jnp.zeros((HALO, heads_here * in_width), BF16)] * local
    forward = [[None] * count for unused in range(local)]
    out_parts = [[None] * count for unused in range(local)]
    if pair:
        order = [(0, 0)] + [(1, p) for p in range(count)] + [(0, p) for p in range(1, count)]
    else:
        order = [(s, p) for p in range(count) for s in range(local)]
    done = None
    for place, (s, p) in enumerate(order):
            low_rows = first[s][p]
            if done is not None:
                low_rows = after(low_rows, done)
            if pair and place == len(order) - 1:
                low_rows = after(low_rows, arrived)
            projected = dot_nn(low_rows, w_in).astype(BF16)
            rate_rows = dot_nt(w_rate, low_rows).reshape(2, heads_here, PART)
            cols, rows, log_decay = token_tables(
                rate_rows, tables[s][:, p * PART : (p + 1) * PART], decay_log, decay_bias, BLOCK
            )
            gated, *kept, states[s] = mixer_forward(
                projected, befores[s], cols, rows, conv_float, gain_row, states[s], BLOCK
            )
            forward[s][p] = (
                projected, befores[s], rate_rows, cols, rows, log_decay, gated, kept
            )
            befores[s] = projected[-HALO:]
            out_parts[s][p] = dot_nn(gated, w_out)
            done = out_parts[s][p]
            if pair and s == 1:
                out_parts[s][p] = turn(out_parts[s][p].astype(BF16), "tensor", 1)
                if p < count - 1:
                    arrived = out_parts[s][p]
    middle, second, second_turned = middle_rows(residual_in, ffn_gain, owner_parts(out_parts))
    ffn_out, grad_second, grads_ffn = feed_forward(
        second, second_turned, out_grad, weights, share
    )
    ffn_shares = lax.psum_scatter(
        grads_ffn.reshape(-1, grads_ffn.shape[-1]), "dp", scatter_dimension=0, tiled=True
    )
    layer_out, grad_middle, grad_mix, grad_ffn_gain = second_back(
        grad_second, middle, out_grad, ffn_out, ffn_gain
    )
    cots = sequences(grad_mix)
    every = [(s, p) for s in range(local) for p in range(count)]
    gated_all = jnp.concatenate([forward[s][p][6] for s, p in every])
    cots_all = jnp.concatenate([cots[s][p] for s, p in every])
    grad_out = dot_tn(gated_all, cots_all).astype(BF16)
    grad_states = [jnp.zeros((heads_here, key_dim, value_dim), F32)] * local
    afters = [jnp.zeros((heads_here, HALO, conv_weight.shape[2]), F32)] * local
    first_parts = [[None] * count for unused in range(local)]
    proj_lows = [[None] * count for unused in range(local)]
    grad_rate, sums = 0.0, 0.0
    done = None
    for place, (s, p) in enumerate(reversed(order)):
            projected, before, rate_rows, cols, rows, log_decay, gated, kept = forward[s][p]
            grad_gated = dot_nt(cots[s][p], w_out).astype(BF16)
            if done is not None:
                grad_gated = after(grad_gated, done)
            if place == local * count // 2:
                grad_gated = after(grad_gated, grad_out)
            proj_low, tokens, colsum, grad_conv, grad_head_gain, grad_states[s], afters[s] = (
                mixer_backward(
                    grad_gated, projected, before, cols, rows, conv_float, gain_row, kept,
                    grad_states[s], afters[s], BLOCK,
                )
            )
            grad_rates, grad_log, grad_bias = rate_gradients(
                tokens, colsum, rate_rows, tables[s][0, p * PART : (p + 1) * PART],
                decay_log, decay_bias, log_decay, BLOCK,
            )
            rates_low = grad_rates.astype(BF16).reshape(2 * heads_here, PART)
            grad_rate = grad_rate + dot_nn(rates_low, first[s][p])
            first_parts[s][p] = dot_nt(proj_low, w_in) + dot_tn(rates_low, w_rate)
            proj_lows[s][p] = after(proj_low, first_parts[s][p])
            done = first_parts[s][p]
            if pair and s == 1:
                first_parts[s][p] = turn(first_parts[s][p].astype(BF16), "tensor", 1)
            sums = sums + jnp.concatenate(
                [grad_conv.reshape(-1), grad_head_gain[0], grad_log, grad_bias]
            )
    input_grad, grad_mixer_gain = first_back(
        residual_in, grad_middle, mixer_gain, owner_parts(first_parts)
    )
    share_out = scatter_sum_dp(grad_out)
    proj_lows[0][0] = after(proj_lows[0][0], share_out)
    grad_in = in_grad(
        [first[s][p] for s, p in every], [proj_lows[s][p] for s, p in every], in_width
    )
    ffn_shares = after(ffn_shares, done)
    share_ffn = ffn_shares[:, :hidden_here]
    for shift in range(1, members):
        share_ffn = share_ffn + turn(
            ffn_shares[:, shift * hidden_here : (shift + 1) * hidden_here], "tensor", -shift
        )
    share_ffn = share_ffn.reshape(3, rows_share, hidden_here)
    share_early = jnp.concatenate([*share_ffn, share_out.reshape(rows_share, -1)], axis=1)
    early = lax.all_gather(share_early, "dp", axis=0, tiled=True)
    if pair:
        grad_in = after(grad_in, first_parts[1])
    grad_in = after(grad_in, share_early)

    small = jnp.concatenate([sums, grad_rate.reshape(-1), grad_mixer_gain[0], grad_ffn_gain[0]])
    length = small.shape[0]
    small = jnp.pad(small, (0, -length % 1024)).reshape(-1, 1024)
    small = sum_small(small, "dp").reshape(-1)
    share_in = scatter_sum_dp(grad_in, small)
    conv_size = conv_weight.size
    rate_size = rate_weight.size
    grad_conv = small[:conv_size].reshape(conv_weight.shape)
    at = conv_size + value_dim
    grad_log = small[at : at + heads_here]
    grad_bias = small[at + heads_here : at + 2 * heads_here]
    at += 2 * heads_here
    grad_rate = small[at : at + rate_size].reshape(2, heads_here, model_width).transpose(2, 1, 0)
    at += rate_size
    gains = jnp.concatenate([small[conv_size : conv_size + value_dim], small[at:length]])
    gains = sum_small(gains, "tensor")
    grad_head_gain = gains[:value_dim]
    grad_mixer_gain = gains[value_dim : value_dim + model_width]
    grad_ffn_gain = gains[value_dim + model_width :]

    share_in = share_in.reshape(rows_share, heads_here, in_width)
    grad_in = lax.all_gather(share_in, "dp", axis=0, tiled=True)
    width = 2 * hidden_here
    grad_gate_up = early[:, :width].reshape(gate_up.shape).astype(F32)
    grad_down = early[:, width : width + hidden_here].astype(F32).T
    grad_out = early[:, width + hidden_here :].astype(F32).reshape(out_weight.shape)
    grad_in = after(grad_in, (grad_gate_up, grad_down, grad_out)).astype(F32)
    return (
        layer_out,
        input_grad,
        grad_mixer_gain,
        grad_in,
        grad_rate,
        grad_conv,
        grad_log,
        grad_bias,
        grad_head_gain,
        grad_out,
        grad_ffn_gain,
        grad_gate_up,
        grad_down,
    )


def solution(mesh):
    return jax.shard_map(
        shards,
        mesh=mesh,
        in_specs=(
            P(("dp", "tensor"), None),
            P(),
            P(None, "tensor", None),
            P(None, "tensor", None),
            P("tensor", None, None),
            P("tensor"),
            P("tensor"),
            P(),
            P("tensor", None, None),
            P(),
            P(None, None, "tensor"),
            P("tensor", None),
            P("dp"),
            P("dp"),
            P(("dp", "tensor"), None),
        ),
        out_specs=(
            P(("dp", "tensor"), None),
            P(("dp", "tensor"), None),
            P(),
            P(None, "tensor", None),
            P(None, "tensor", None),
            P("tensor", None, None),
            P("tensor"),
            P("tensor"),
            P(),
            P("tensor", None, None),
            P(),
            P(None, None, "tensor"),
            P("tensor", None),
        ),
        check_vma=False,
    )
```

time: 2530 us -> 697 us (0.28)
  matrix products: 1070 us -> 115 us
  local copies, waits for them, and re-layouts: 451 us -> 95.6 us
  waiting for transfers between devices: 491 us -> 137 us
  other arithmetic: 377 us -> 30.6 us
  Pallas kernels: 0 us -> 267 us
  blocking collectives: 103 us -> 0 us
  starting transfers between devices: 0.37 us -> 30.3 us
    dot_general x400 -> x37, matrix products: 1070 us -> 115 us  [the longest x12 48.6 us: dot_nn(): lax.dot_general(left, right, (((1,), (0,)), ((), ())), preferred_element_...]
    pallas_call x0 -> x14, Pallas kernels: none -> 267 us  [the longest x4 99.2 us: mixer_backward(): pl.pallas_call(bwd_kernel, grid=(steps,), in_specs=[wide, pl.BlockSpec((w...]
    psum x1 -> x0, waiting for transfers between devices: 204 us -> none  [shards(): lax.psum(grad_in.astype(jnp.bfloat16), 'dp').astype(jnp.float32)]
    all_gather x4 -> x3, waiting for transfers between devices: 177 us -> 12.4 us  [the longest x1 12.4 us: shards(): grad_in = lax.all_gather(share_in, 'dp', axis=0, tiled=True)]
    squeeze x129 -> x13, local copies, waits for them, and re-layouts: 169 us -> 5.9 us  [the longest x8 5.69 us: scatter_sum_dp(): send = lax.dynamic_index_in_dim(halves, 1 - mine, 1, keepdims=False)]
    ppermute x0 -> x23, waiting for transfers between devices: none -> 124 us  [the longest x13 88.4 us: partner(): lax.ppermute(array, axis, [(i, i ^ bit) for i in range(lax.axis_size(axis...]
    reduce_scatter x4 -> x0, waiting for transfers between devices: 109 us -> none  [the longest x1 54.4 us: shards(): lax.psum_scatter(jnp.dot(grad_pre, w_gu_flat.T, preferred_element_type=jn...]
    psum x2 -> x0, blocking collectives: 103 us -> none  [the longest x1 64.1 us: shards(): lax.psum(grad_rate.astype(jnp.bfloat16), 'dp').astype(jnp.float32)]
  transfers between devices with their start and end apart: 9 -> 27, of which waited for: 7 -> 15; matrix products, arithmetic and copies ran while one was open for 7% -> 31% of each run, Pallas kernels for 0% -> 30%
where the time goes in v1:
time: 697 us; the launch traced here: 691 us
  Pallas kernels  267 us (38%)
  waiting for transfers between devices  137 us (20%)
  matrix products  115 us (16%)
  local copies, waits for them, and re-layouts  95.6 us (14%)
  other arithmetic  30.6 us (4%)
  starting transfers between devices  30.3 us (4%)
  between operations  15.4 us (2%)
    pallas_call x4, Pallas kernels, mixer_backward(): pl.pallas_call(bwd_kernel, grid=(steps,), in_specs=[wide, pl.BlockSpec((w...  99.2 us
    ppermute x13, waiting for transfers between devices, partner(): lax.ppermute(array, axis, [(i, i ^ bit) for i in range(lax.axis_size(axis...  88.4 us
    pallas_call x1, Pallas kernels, feed_forward(): pl.pallas_call(ffn_kernel, grid=(tiles,), in_specs=[whole_block(second),...  63.2 us
    pallas_call x4, Pallas kernels, mixer_forward(): pl.pallas_call(fwd_kernel, grid=(steps,), in_specs=[pl.BlockSpec((width,...  55 us
    dot_general x12, matrix products, dot_nn(): lax.dot_general(left, right, (((1,), (0,)), ((), ())), preferred_element_...  48.6 us
    dot_general x12, matrix products, dot_nt(): lax.dot_general(left, right, (((1,), (1,)), ((), ())), preferred_element_...  48.4 us
    unnamed x113, local copies, waits for them, and re-layouts  47.6 us
    ppermute x10, waiting for transfers between devices, turn(): lax.ppermute(array, axis, [((i + shift) % size, i) for i in range(size)])  36 us
  transfers between devices with their start and end apart: 27, of which 15 were waited for; matrix products, arithmetic and copies ran while one was open for 31% of the time, Pallas kernels for 30%

profile of v1, /device:TPU:0, one launch (start us, length us, event | category | flops | bytes accessed | tf_op | source)
XLA Modules:
  0.0 691.2 jit_solution(17316310565951880260)
XLA Ops:
  19.1 7.4 %collective-permute-done.4 = bf16[3,64,1408]{2,1,0:T(8,128)(2,1)S(1)} collective-permute-done((bf16[3,64,1408]{2,1,0:T(8,128)(2,1)S(1)}, bf16[3,64,1408]{2,1,0:T(8,128)(2,1)S(1)}, u32[]{:S(2)}, u32[]{:S(2)}) %collective-permute-start.4) | collective-permute-done | bytes 540704 | tf_op jit(solution)/shard_map/ppermute | solution.py:895
  51.0 13.5 %mixer_forward.4 = (bf16[512,1024]{1,0:T(8,128)(2,1)}, bf16[512,1024]{1,0:T(8,128)(2,1)}, bf16[512,1024]{1,0:T(8,128)(2,1)}, bf16[2,4,256,256]{3,2,1,0:T(8,128)(...) custom-call(bf16[512,3072]{1,0:T(8,128)(2,1)} %convolution_convert_fusion.3.proj_ref.halo_ref, ...), custom_call_target="tpu_custom_call" | custom-call | flops 2147483648 | bytes 9437184 | tf_op jit(solution)/shard_map/mixer_forward/pallas_call | solution.py:485
  75.6 8.3 %convolution_convert_fusion.2.proj_ref.halo_ref = bf16[512,3072]{1,0:T(8,128)(2,1)} fusion(bf16[512,1024]{1,0:T(8,128)(2,1)} %collective-permute-done.refs_2_, bf16[1024,3072]{1,0:T(8,128)(2,1)} %bitcast.287), kind=kOutput, calls=%fused_computation.3 | convolution fusion | flops 3222798336 | bytes 10485760 | tf_op jit(solution)/shard_map/dot_general | solution.py:20
  85.5 13.7 %mixer_forward.5 = (bf16[512,1024]{1,0:T(8,128)(2,1)}, bf16[512,1024]{1,0:T(8,128)(2,1)}, bf16[512,1024]{1,0:T(8,128)(2,1)}, bf16[2,4,256,256]{3,2,1,0:T(8,128)(...) custom-call(bf16[512,3072]{1,0:T(8,128)(2,1)} %convolution_convert_fusion.2.proj_ref.halo_ref, ...), custom_call_target="tpu_custom_call" | custom-call | flops 2147483648 | bytes 9437184 | tf_op jit(solution)/shard_map/mixer_forward/pallas_call | solution.py:485
  106.9 8.4 %convolution_convert_fusion.1.proj_ref.halo_ref = bf16[512,3072]{1,0:T(8,128)(2,1)} fusion(bf16[512,1024]{1,0:T(8,128)(2,1)} %collective-permute-done.2.refs_3_, bf16[1024,3072]{1,0:T(8,128)(2,1)} %bitcast.288), kind=kOutput, calls=%fused_computation.2 | convolution fusion | flops 3222798336 | bytes 10485760 | tf_op jit(solution)/shard_map/dot_general | solution.py:20
  118.5 14.1 %mixer_forward.6 = (bf16[512,1024]{1,0:T(8,128)(2,1)}, bf16[512,1024]{1,0:T(8,128)(2,1)}, bf16[512,1024]{1,0:T(8,128)(2,1)}, bf16[2,4,256,256]{3,2,1,0:T(8,128)(...) custom-call(bf16[512,3072]{1,0:T(8,128)(2,1)} %convolution_convert_fusion.1.proj_ref.halo_ref, ...), custom_call_target="tpu_custom_call" | custom-call | flops 2147483648 | bytes 9437184 | tf_op jit(solution)/shard_map/mixer_forward/pallas_call | solution.py:485
  138.9 8.3 %convolution_convert_fusion.proj_ref.halo_ref = bf16[512,3072]{1,0:T(8,128)(2,1)} fusion(bf16[512,1024]{1,0:T(8,128)(2,1)} %get-tuple-element.97.refs_1_, bf16[1024,3072]{1,0:T(8,128)(2,1)} %bitcast.289), kind=kOutput, calls=%fused_computation.1 | convolution fusion | flops 3222798336 | bytes 10485760 | tf_op jit(solution)/shard_map/dot_general | solution.py:20
  148.8 13.7 %mixer_forward.7 = (bf16[512,1024]{1,0:T(8,128)(2,1)}, bf16[512,1024]{1,0:T(8,128)(2,1)}, bf16[512,1024]{1,0:T(8,128)(2,1)}, bf16[2,4,256,256]{3,2,1,0:T(8,128)(...) custom-call(bf16[512,3072]{1,0:T(8,128)(2,1)} %convolution_convert_fusion.proj_ref.halo_ref, ...), custom_call_target="tpu_custom_call" | custom-call | flops 2147483648 | bytes 9437184 | tf_op jit(solution)/shard_map/mixer_forward/pallas_call | solution.py:485
  167.2 7.7 %middle_rows.1 = (f32[1024,1024]{1,0:T(8,128)}, bf16[1024,1024]{1,0:T(8,128)(2,1)}, bf16[1024,1024]{1,0:T(8,128)(2,1)}) custom-call(bf16[1024,1024]{1,0:T(8,128)(2,1)} %rows_ref.5, f32[1,1024]{1,0:T(1,128)} %bitcast.375, f32[512,1024]{1,0:T(8,128)} %fusion.181.refs_0_, bf16[512,1024]{1,0:T(8,128)(2,1)} %copy-done.14, f32[512,1024]{1,0:T(8,128)} %fusion.184.refs_2_, ...), custom_call_target="tpu_custom_call" | custom-call | tf_op jit(solution)/shard_map/middle_rows/pallas_call | solution.py:826
  175.0 63.2 %feed_forward.1 = (f32[1024,1024]{1,0:T(8,128)}, f32[1024,1024]{1,0:T(8,128)}, bf16[16,3,64,2816]{3,2,1,0:T(8,128)(2,1)}) custom-call(bf16[1024,1024]{1,0:T(8,128)(2,1)} %get-tuple-element.100.second_ref, bf16[1024,1024]{1,0:T(8,128)(2,1)} %get-tuple-element.101.second_turned_ref, bf16[1024,1024]{1,0:T(8,128)(2,1)} %cot_ref.3, bf16[1024,1024]{1,0:T(8,128)(2,1)} %bitcast.298, ...), custom_call_target="tpu_custom_call" | custom-call | flops 17716740096 | bytes 34603008 | tf_op jit(solution)/shard_map/feed_forward/pallas_call | solution.py:661
  238.8 10.1 %second_back.1 = (bf16[1024,1024]{1,0:T(8,128)(2,1)}, f32[1024,1024]{1,0:T(8,128)}, bf16[1024,1024]{1,0:T(8,128)(2,1)}, f32[1,1024]{1,0:T(1,128)}) custom-call(f32[1024,1024]{1,0:T(8,128)} %get-tuple-element.103.back_ref, f32[1024,1024]{1,0:T(8,128)} %get-tuple-element.104.middle_ref, bf16[1024,1024]{1,0:T(8,128)(2,1)} %cot_ref.3, ...), custom_call_target="tpu_custom_call" | custom-call | tf_op jit(solution)/shard_map/second_back/pallas_call | solution.py:826
  257.6 25.6 %mixer_backward.4 = (bf16[512,3072]{1,0:T(8,128)(2,1)}, f32[512,8]{1,0:T(8,128)}, f32[8,512]{1,0:T(8,128)}, f32[4,4,512]{2,1,0:T(4,128)}, f32[1,256]{1,0:T(1,128...) custom-call(bf16[512,1024]{1,0:T(8,128)(2,1)} %convolution_convert_fusion.4.cot_ref, ...), custom_call_target="tpu_custom_call" | custom-call | flops 2147483648 | bytes 12582912 | tf_op jit(solution)/shard_map/mixer_backward/pallas_call | solution.py:551
  284.9 8.5 %fusion.185 = f32[512,1024]{1,0:T(8,128)} fusion(bf16[512,3072]{1,0:T(8,128)(2,1)} %get-tuple-element.158.refs_5_, bf16[1024,3072]{1,0:T(8,128)(2,1)} %bitcast.290), kind=kOutput, calls=%fused_computation.323 | convolution fusion | flops 3221225472 | bytes 11534336 | tf_op jit(solution)/shard_map/dot_general | solution.py:24
  303.2 24.0 %mixer_backward.5 = (bf16[512,3072]{1,0:T(8,128)(2,1)}, f32[512,8]{1,0:T(8,128)}, f32[8,512]{1,0:T(8,128)}, f32[4,4,512]{2,1,0:T(4,128)}, f32[1,256]{1,0:T(1,128...) custom-call(bf16[512,1024]{1,0:T(8,128)(2,1)} %convolution_convert_fusion.5.cot_ref, ...), custom_call_target="tpu_custom_call" | custom-call | flops 2147483648 | bytes 12582912 | tf_op jit(solution)/shard_map/mixer_backward/pallas_call | solution.py:551
  329.3 7.0 %fusion.186 = f32[512,1024]{1,0:T(8,128)S(1)} fusion(bf16[512,3072]{1,0:T(8,128)(2,1)} %get-tuple-element.160.refs_7_, bf16[1024,3072]{1,0:T(8,128)(2,1)} %bitcast.291), kind=kOutput, calls=%fused_computation.324 | convolution fusion | flops 3221225472 | bytes 11534336 | tf_op jit(solution)/shard_map/dot_general | solution.py:24
  341.9 6.3 fusion.13
  348.2 24.9 %mixer_backward.6 = (bf16[512,3072]{1,0:T(8,128)(2,1)}, f32[512,8]{1,0:T(8,128)}, f32[8,512]{1,0:T(8,128)}, f32[4,4,512]{2,1,0:T(4,128)}, f32[1,256]{1,0:T(1,128...) custom-call(bf16[512,1024]{1,0:T(8,128)(2,1)} %convolution_convert_fusion.6.cot_ref, ...), custom_call_target="tpu_custom_call" | custom-call | flops 2147483648 | bytes 12582912 | tf_op jit(solution)/shard_map/mixer_backward/pallas_call | solution.py:551
  375.3 6.8 fusion.187
  383.6 24.8 %mixer_backward.7 = (bf16[512,3072]{1,0:T(8,128)(2,1)}, f32[512,8]{1,0:T(8,128)}, f32[8,512]{1,0:T(8,128)}, f32[4,4,512]{2,1,0:T(4,128)}, f32[1,256]{1,0:T(1,128...) custom-call(bf16[512,1024]{1,0:T(8,128)(2,1)} %convolution_convert_fusion.7.cot_ref, ...), custom_call_target="tpu_custom_call" | custom-call | flops 2147483648 | bytes 12582912 | tf_op jit(solution)/shard_map/mixer_backward/pallas_call | solution.py:551
  409.7 8.7 %fusion.188 = f32[512,1024]{1,0:T(8,128)} fusion(bf16[512,3072]{1,0:T(8,128)(2,1)} %get-tuple-element.157.refs_4_, bf16[1024,3072]{1,0:T(8,128)(2,1)} %bitcast.293), kind=kOutput, calls=%fused_computation.326 | convolution fusion | flops 3221225472 | bytes 11534336 | tf_op jit(solution)/shard_map/dot_general | solution.py:24
  421.2 12.1 %collective-permute-done.15 = bf16[4,64,1024]{2,1,0:T(8,128)(2,1)S(1)} collective-permute-done((bf16[4,64,1024]{2,1,0:T(8,128)(2,1)S(1)}, bf16[4,64,1024]{2,1,0:T(8,128)(2,1)S(1)}, u32[]{:S(2)}, u32[]{:S(2)}) %collective-permute-start.15) | collective-permute-done | bytes 524320 | tf_op jit(solution)/shard_map/ppermute | solution.py:899
  460.9 19.8 %in_grad.1 = bf16[1024,3072]{1,0:T(8,128)(2,1)} custom-call(bf16[512,1024]{1,0:T(8,128)(2,1)} %get-tuple-element.229.refs_0_, bf16[512,1024]{1,0:T(8,128)(2,1)} %get-tuple-element.97.refs_1_, bf16[512,1024]{1,0:T(8,128)(2,1)} %collective-permute-done.refs_2_, bf16[512,1024]{1,0:T(8,128)(2,1)} %collective-permute-done.2.refs_3_, ...), custom_call_target="tpu_custom_call" | custom-call | flops 3221225472 | bytes 6291456 | tf_op jit(solution)/shard_map/in_grad/pallas_call | solution.py:711
  485.2 20.1 %collective-permute-done.8.refs_3_ = bf16[512,1024]{1,0:T(8,128)(2,1)S(1)} collective-permute-done((bf16[512,1024]{1,0:T(8,128)(2,1)S(1)}, bf16[512,1024]{1,0:T(8,128)(2,1)S(1)}, u32[]{:S(2)}, u32[]{:S(2)}) %collective-permute-start.8) | collective-permute-done | bytes 1048608 | tf_op jit(solution)/shard_map/ppermute | solution.py:895
  528.6 8.1 %first_back.1 = (bf16[1024,1024]{1,0:T(8,128)(2,1)}, f32[1,1024]{1,0:T(1,128)}) custom-call(bf16[1024,1024]{1,0:T(8,128)(2,1)} %rows_ref.5, f32[1024,1024]{1,0:T(8,128)} %get-tuple-element.107.middle_grad_ref, f32[1,1024]{1,0:T(1,128)} %bitcast.346, f32[512,1024]{1,0:T(8,128)} %bitcast_add_fusion.1.refs_0_, bf16[512,1024]{1,0:T(8,128)(2,1)} %copy-done.12, ...), custom_call_target="tpu_custom_call" | custom-call | tf_op jit(solution)/shard_map/first_back/pallas_call | solution.py:826
  539.0 25.3 %collective-permute-done.10 = f32[19,1024]{1,0:T(8,128)S(1)} collective-permute-done((f32[19,1024]{1,0:T(8,128)S(1)}, f32[19,1024]{1,0:T(8,128)S(1)}, u32[]{:S(2)}, u32[]{:S(2)}) %collective-permute-start.10) | collective-permute-done | bytes 77856 | tf_op jit(solution)/shard_map/ppermute | solution.py:899
  578.4 16.5 %collective-permute-done.21 = bf16[2,64,3072]{2,1,0:T(8,128)(2,1)S(1)} collective-permute-done((bf16[2,64,3072]{2,1,0:T(8,128)(2,1)S(1)}, bf16[2,64,3072]{2,1,0:T(8,128)(2,1)S(1)}, u32[]{:S(2)}, u32[]{:S(2)}) %collective-permute-start.21) | collective-permute-done | bytes 786464 | tf_op jit(solution)/shard_map/ppermute | solution.py:899
  597.7 14.3 %collective-permute-done.22 = bf16[1,64,3072]{2,1,0:T(8,128)(2,1)S(1)} collective-permute-done((bf16[1,64,3072]{2,1,0:T(8,128)(2,1)S(1)}, bf16[1,64,3072]{2,1,0:T(8,128)(2,1)S(1)}, u32[]{:S(2)}, u32[]{:S(2)}) %collective-permute-start.22) | collective-permute-done | bytes 393248 | tf_op jit(solution)/shard_map/ppermute | solution.py:899
  623.8 8.3 %copy.201 = bf16[1024,2816]{0,1:T(8,128)(2,1)} copy(bf16[1024,2816]{1,0:T(8,128)(2,1)} %slice.506) | data formatting | bytes 11534336
  636.2 15.6 %copy.181 = f32[1024,2,1408]{2,1,0:T(2,128)} copy(bf16[1024,2,1408]{0,2,1:T(8,128)(2,1)} %bitcast.278) | data formatting | bytes 17301504
  656.5 6.2 copy.182
  662.7 12.4 %all-gather.6.cloned.1.call-done = bf16[1024,4,768]{2,1,0:T(4,128)(2,1)} async-done(((bf16[64,4,768]{2,1,0:T(4,128)(2,1)}), bf16[1024,4,768]{2,1,0:T(4,128)(2,1)}) %all-gather.6.cloned.1.call-update) | async-done | bytes 6291472 | tf_op jit(solution)/shard_map/all_gather | solution.py:1152
  675.1 9.3 %convert_element_type.171 = f32[1024,4,768]{2,1,0:T(4,128)} convert(bf16[1024,4,768]{2,1,0:T(4,128)(2,1)} %all-gather.6.cloned.1.call-done) | non-fusion elementwise | flops 3145728 | bytes 18874368 | tf_op jit(solution)/shard_map/convert_element_type | solution.py:1157
  (410 shorter events, 202.8 us)
Async XLA Ops:
  7.2 167.8 %all-gather.4.cloned.1.call-start = ((), (), s32[]{:S(2)}) async-start(), calls=%async_computation.1 | async-start | bytes 18382848 | tf_op jit(solution)/shard_map/all_gather | solution.py:1019
  11.2 15.2 %collective-permute-start.4 = (bf16[3,64,1408]{2,1,0:T(8,128)(2,1)S(1)}, bf16[3,64,1408]{2,1,0:T(8,128)(2,1)S(1)}, u32[]{:S(2)}, u32[]{:S(2)}) collective-permute-start(bf16[3,64,1408]{2,1,0:T(8,128)(2,1)S(1)} %pad_maximum_fusion.1), channel_id=1, source_target_pairs={{1,0},{0,1},{3,2},{2,3},{5,4},{4,5},{7,6},{6,7},{9,8},{8,9},{11,10... | collective-permute-start | bytes 1622024 | tf_op jit(solution)/shard_map/ppermute | solution.py:895
  30.0 408.4 %reduce-scatter.4.cloned.1.call-start = ((), (), s32[]{:S(2)}) async-start(), calls=%async_computation.4 | async-start | bytes 18382848
  31.5 41.7 %collective-permute-start = (bf16[512,1024]{1,0:T(8,128)(2,1)}, bf16[512,1024]{1,0:T(8,128)(2,1)}, u32[]{:S(2)}, u32[]{:S(2)}) collective-permute-start(bf16[512,1024]{1,0:T(8,128)(2,1)} %get-tuple-element.229.refs_0_), channel_id=1, source_target_pairs={{1,0},{0,1},{3,2},{2,3},{5,4},{4,5},{7,6},{6,7},{9,8},{8,9},{11,10... | collective-permute-start | bytes 3145736 | tf_op jit(solution)/shard_map/ppermute | solution.py:895
  33.3 69.5 %collective-permute-start.2 = (bf16[512,1024]{1,0:T(8,128)(2,1)}, bf16[512,1024]{1,0:T(8,128)(2,1)}, u32[]{:S(2)}, u32[]{:S(2)}) collective-permute-start(bf16[512,1024]{1,0:T(8,128)(2,1)} %get-tuple-element.97.refs_1_), channel_id=1, source_target_pairs={{1,0},{0,1},{3,2},{2,3},{5,4},{4,5},{7,6},{6,7},{9,8},{8,9},{11,10... | collective-permute-start | bytes 3145736 | tf_op jit(solution)/shard_map/ppermute | solution.py:895
  51.0 15.1 %copy-start.5 = (bf16[1024,1024]{1,0:T(8,128)(2,1)S(1)}, bf16[1024,1024]{1,0:T(8,128)(2,1)}, u32[]{:S(2)}) copy-start(bf16[1024,1024]{1,0:T(8,128)(2,1)} %cot_ref.3) | copy-start | bytes 6291460
  85.5 13.7 %copy-start.31 = (bf16[4,256,1024]{2,1,0:T(8,128)(2,1)S(1)}, bf16[4,256,1024]{2,1,0:T(8,128)(2,1)}, u32[]{:S(2)}) copy-start(bf16[4,256,1024]{2,1,0:T(8,128)(2,1)} %param.23) | copy-start | bytes 6291460
  104.8 31.4 %collective-permute-start.1 = (bf16[512,1024]{1,0:T(8,128)(2,1)}, bf16[512,1024]{1,0:T(8,128)(2,1)S(1)}, u32[]{:S(2)}, u32[]{:S(2)}) collective-permute-start(bf16[512,1024]{1,0:T(8,128)(2,1)} %fusion.182), channel_id=1, source_target_pairs={{1,0},{0,1},{3,2},{2,3},{5,4},{4,5},{7,6},{6,7},{9,8},{8,9},{11,10... | collective-permute-start | bytes 3145736 | tf_op jit(solution)/shard_map/ppermute | solution.py:895
  118.5 14.1 %copy-start.32 = (bf16[4,256,1024]{2,1,0:T(8,128)(2,1)S(1)}, bf16[4,256,1024]{2,1,0:T(8,128)(2,1)}, u32[]{:S(2)}) copy-start(bf16[4,256,1024]{2,1,0:T(8,128)(2,1)} %param.23) | copy-start | bytes 6291460
  136.0 30.2 %collective-permute-start.3 = (bf16[512,1024]{1,0:T(8,128)(2,1)}, bf16[512,1024]{1,0:T(8,128)(2,1)S(1)}, u32[]{:S(2)}, u32[]{:S(2)}) collective-permute-start(bf16[512,1024]{1,0:T(8,128)(2,1)} %fusion.183), channel_id=1, source_target_pairs={{1,0},{0,1},{3,2},{2,3},{5,4},{4,5},{7,6},{6,7},{9,8},{8,9},{11,10... | collective-permute-start | bytes 3145736 | tf_op jit(solution)/shard_map/ppermute | solution.py:895
  238.2 379.9 %all-gather.8.cloned.1.call-start = ((), (), s32[]{:S(2)}) async-start(), calls=%async_computation.3 | async-start | bytes 11419648 | tf_op jit(solution)/shard_map/all_gather | solution.py:1126
  252.6 85.3 %collective-permute-start.5 = (bf16[512,1024]{1,0:T(8,128)(2,1)}, bf16[512,1024]{1,0:T(8,128)(2,1)}, u32[]{:S(2)}, u32[]{:S(2)}) collective-permute-start(bf16[512,1024]{1,0:T(8,128)(2,1)} %get-tuple-element.227), channel_id=1, source_target_pairs={{1,0},{0,1},{3,2},{2,3},{5,4},{4,5},{7,6},{6,7},{9,8},{8,9},{11,10... | collective-permute-start | bytes 3145736 | tf_op jit(solution)/shard_map/ppermute | solution.py:895
  254.4 45.3 %collective-permute-start.6 = (bf16[512,1024]{1,0:T(8,128)(2,1)}, bf16[512,1024]{1,0:T(8,128)(2,1)}, u32[]{:S(2)}, u32[]{:S(2)}) collective-permute-start(bf16[512,1024]{1,0:T(8,128)(2,1)} %get-tuple-element.226), channel_id=1, source_target_pairs={{1,0},{0,1},{3,2},{2,3},{5,4},{4,5},{7,6},{6,7},{9,8},{8,9},{11,10... | collective-permute-start | bytes 3145736 | tf_op jit(solution)/shard_map/ppermute | solution.py:895
  348.2 61.3 %copy-start.7 = (bf16[1024,1024]{1,0:T(8,128)(2,1)}, bf16[1024,1024]{1,0:T(8,128)(2,1)S(1)}, u32[]{:S(2)}) copy-start(bf16[1024,1024]{1,0:T(8,128)(2,1)S(1)} %fusion.13) | copy-start | bytes 6291460
  409.6 8.8 %collective-permute-start.14 = (bf16[8,64,1024]{2,1,0:T(8,128)(2,1)S(1)}, bf16[8,64,1024]{2,1,0:T(8,128)(2,1)S(1)}, u32[]{:S(2)}, u32[]{:S(2)}) collective-permute-start(bf16[8,64,1024]{2,1,0:T(8,128)(2,1)S(1)} %dynamic-slice_bitcast_fusion.2), channel_id=1, source_target_pairs={{0,2},{2,0},{4,6},{6,4},{8,10},{10,8},{12,14},{14,12},{16,18},{18,... | collective-permute-start | bytes 3145736 | tf_op jit(solution)/shard_map/ppermute | solution.py:899
  418.6 14.7 %collective-permute-start.15 = (bf16[4,64,1024]{2,1,0:T(8,128)(2,1)S(1)}, bf16[4,64,1024]{2,1,0:T(8,128)(2,1)S(1)}, u32[]{:S(2)}, u32[]{:S(2)}) collective-permute-start(bf16[4,64,1024]{2,1,0:T(8,128)(2,1)S(1)} %dynamic-slice_bitcast_fusion.4), channel_id=1, source_target_pairs={{0,4},{2,6},{4,0},{6,2},{8,12},{10,14},{12,8},{14,10},{16,20},{18,... | collective-permute-start | bytes 1572872 | tf_op jit(solution)/shard_map/ppermute | solution.py:899
  433.4 9.2 %collective-permute-start.16 = (bf16[2,64,1024]{2,1,0:T(8,128)(2,1)S(1)}, bf16[2,64,1024]{2,1,0:T(8,128)(2,1)S(1)}, u32[]{:S(2)}, u32[]{:S(2)}) collective-permute-start(bf16[2,64,1024]{2,1,0:T(8,128)(2,1)S(1)} %dynamic-slice_bitcast_fusion.5), channel_id=1, source_target_pairs={{0,8},{2,10},{4,12},{6,14},{8,0},{10,2},{12,4},{14,6},{16,24},{18,... | collective-permute-start | bytes 786440 | tf_op jit(solution)/shard_map/ppermute | solution.py:899
  441.1 14.1 %collective-permute-start.18 = (bf16[192,1408]{1,0:T(8,128)(2,1)}, bf16[192,1408]{1,0:T(8,128)(2,1)}, u32[]{:S(2)}, u32[]{:S(2)}) collective-permute-start(bf16[192,1408]{1,0:T(8,128)(2,1)} %copy.175), channel_id=1, source_target_pairs={{1,0},{0,1},{3,2},{2,3},{5,4},{4,5},{7,6},{6,7},{9,8},{8,9},{11,10... | collective-permute-start | bytes 1622024 | tf_op jit(solution)/shard_map/ppermute | solution.py:895
  442.6 8.3 %collective-permute-start.17 = (bf16[1,64,1024]{2,1,0:T(8,128)(2,1)S(1)}, bf16[1,64,1024]{2,1,0:T(8,128)(2,1)S(1)}, u32[]{:S(2)}, u32[]{:S(2)}) collective-permute-start(bf16[1,64,1024]{2,1,0:T(8,128)(2,1)S(1)} %constant_dynamic-slice_fusion.2), channel_id=1, source_target_pairs={{0,16},{2,18},{4,20},{6,22},{8,24},{10,26},{12,28},{14,30},{16,0},... | collective-permute-start | bytes 393224 | tf_op jit(solution)/shard_map/ppermute | solution.py:899
  458.8 216.3 %all-gather.6.cloned.1.call-start = ((), (), s32[]{:S(2)}) async-start(), calls=%async_computation.2 | async-start | bytes 6684672 | tf_op jit(solution)/shard_map/all_gather | solution.py:1152
  458.9 26.4 %collective-permute-start.7 = (bf16[512,1024]{1,0:T(8,128)(2,1)}, bf16[512,1024]{1,0:T(8,128)(2,1)S(1)}, u32[]{:S(2)}, u32[]{:S(2)}) collective-permute-start(bf16[512,1024]{1,0:T(8,128)(2,1)} %bitcast_add_fusion.2), channel_id=1, source_target_pairs={{1,0},{0,1},{3,2},{2,3},{5,4},{4,5},{7,6},{6,7},{9,8},{8,9},{11,10... | collective-permute-start | bytes 3145736 | tf_op jit(solution)/shard_map/ppermute | solution.py:895
  460.2 45.1 %collective-permute-start.8 = (bf16[512,1024]{1,0:T(8,128)(2,1)S(1)}, bf16[512,1024]{1,0:T(8,128)(2,1)S(1)}, u32[]{:S(2)}, u32[]{:S(2)}) collective-permute-start(bf16[512,1024]{1,0:T(8,128)(2,1)S(1)} %copy-done.11), channel_id=1, source_target_pairs={{1,0},{0,1},{3,2},{2,3},{5,4},{4,5},{7,6},{6,7},{9,8},{8,9},{11,10... | collective-permute-start | bytes 3145736 | tf_op jit(solution)/shard_map/ppermute | solution.py:895
  485.2 20.1 %copy-start.12 = (bf16[512,1024]{1,0:T(8,128)(2,1)}, bf16[512,1024]{1,0:T(8,128)(2,1)S(1)}, u32[]{:S(2)}) copy-start(bf16[512,1024]{1,0:T(8,128)(2,1)S(1)} %collective-permute-done.7.refs_1_) | copy-start | bytes 3145732
  509.5 6.0 collective-permute-start.19
  521.7 54.0 %collective-permute-start.20 = (bf16[4,64,3072]{2,1,0:T(8,128)(2,1)}, bf16[4,64,3072]{2,1,0:T(8,128)(2,1)}, u32[]{:S(2)}, u32[]{:S(2)}) collective-permute-start(bf16[4,64,3072]{2,1,0:T(8,128)(2,1)} %dynamic-slice_bitcast_fusion.1), channel_id=1, source_target_pairs={{0,4},{2,6},{4,0},{6,2},{8,12},{10,14},{12,8},{14,10},{16,20},{18,... | collective-permute-start | bytes 4718600 | tf_op jit(solution)/shard_map/ppermute | solution.py:899
  537.5 1.4 collective-permute-start.9
  538.9 25.4 %collective-permute-start.10 = (f32[19,1024]{1,0:T(8,128)S(1)}, f32[19,1024]{1,0:T(8,128)S(1)}, u32[]{:S(2)}, u32[]{:S(2)}) collective-permute-start(f32[19,1024]{1,0:T(8,128)S(1)} %add.415), channel_id=1, source_target_pairs={{0,4},{2,6},{4,0},{6,2},{8,12},{10,14},{12,8},{14,10},{16,20},{18,... | collective-permute-start | bytes 233480 | tf_op jit(solution)/shard_map/ppermute | solution.py:899
  564.3 4.7 collective-permute-start.11
  569.0 6.6 collective-permute-start.12
  577.8 17.0 %collective-permute-start.21 = (bf16[2,64,3072]{2,1,0:T(8,128)(2,1)S(1)}, bf16[2,64,3072]{2,1,0:T(8,128)(2,1)S(1)}, u32[]{:S(2)}, u32[]{:S(2)}) collective-permute-start(bf16[2,64,3072]{2,1,0:T(8,128)(2,1)S(1)} %dynamic-slice_bitcast_fusion.3), channel_id=1, source_target_pairs={{0,8},{2,10},{4,12},{6,14},{8,0},{10,2},{12,4},{14,6},{16,24},{18,... | collective-permute-start | bytes 2359304 | tf_op jit(solution)/shard_map/ppermute | solution.py:899
  595.0 17.0 %collective-permute-start.22 = (bf16[1,64,3072]{2,1,0:T(8,128)(2,1)S(1)}, bf16[1,64,3072]{2,1,0:T(8,128)(2,1)S(1)}, u32[]{:S(2)}, u32[]{:S(2)}) collective-permute-start(bf16[1,64,3072]{2,1,0:T(8,128)(2,1)S(1)} %constant_dynamic-slice_fusion.1), channel_id=1, source_target_pairs={{0,16},{2,18},{4,20},{6,22},{8,24},{10,26},{12,28},{14,30},{16,0},... | collective-permute-start | bytes 1179656 | tf_op jit(solution)/shard_map/ppermute | solution.py:899
  613.2 3.8 collective-permute-start.13
  (38 other events, 201.9 us)
Sparse Core Ops, SparseCore 0:
  30.0 93.0 all-gather.3
  238.3 185.6 reduce-scatter.3
  458.9 92.8 all-gather.7
  613.2 61.8 all-gather.5

commit v2 on v1

--- a/solution.py
+++ b/solution.py
@@ -10,10 +10,12 @@
 SEQ = 1024
 BLOCK = 256
 PART = 512
+LANES = 128
 HALO = 16
 F32 = jnp.float32
 BF16 = jnp.bfloat16
 VMEM_BYTES = 56 * 1024 * 1024
+MIXER_VMEM_BYTES = 56 * 1024 * 1024
 
 
 def dot_nn(left, right):
@@ -36,8 +38,9 @@
     return jnp.sum(values, axis=1, keepdims=True)
 
 
-MASK, BACK, AHEAD, SEGMENT, PER_HEAD = 0, 1, 4, 7, 8
-WRITE, CUM, START, LAST = 0, 1, 2, 3
+MASK, BACK, AHEAD, SEGMENT, CARRIED, TO_LAST = 0, 1, 4, 7, 8, 9
+WRITE, CUM, START, LAST = 8, 16, 24, 32
+SLOTS = 8
 
 
 def fill_level_masks(mask_ref):
@@ -129,50 +132,77 @@
 
 
 def head_column(cols, head, which):
-    place = PER_HEAD + 4 * head + which
-    return cols[:, place : place + 1]
-
-
-def fill_halo(padded_ref, head, at, before_ref, halo_ref, first):
-    mix_width = padded_ref.shape[2]
-
-    @pl.when(first)
-    def _():
-        padded_ref[head, 0:HALO, :] = before_ref[:, at : at + mix_width].astype(F32)
-
-    @pl.when(jnp.logical_not(first))
-    def _():
-        padded_ref[head, 0:HALO, :] = halo_ref[:, at : at + mix_width].astype(F32)
+    return cols[:, which + head : which + head + 1]
+
+
+def softplus(values):
+    return jnp.maximum(values, 0.0) + jnp.log1p(jnp.exp(-jnp.abs(values)))
+
+
+def exact_dot(left, right):
+    return lax.dot_general(
+        left, right, (((1,), (0,)), ((), ())), precision=lax.Precision.HIGHEST,
+        preferred_element_type=F32,
+    )
+
+
+def triangle(width, upper):
+    one = lax.broadcasted_iota(jnp.int32, (width, width), 0)
+    other = lax.broadcasted_iota(jnp.int32, (width, width), 1)
+    return jnp.where(one <= other if upper else one >= other, 1.0, 0.0)
 
 
 def fwd_kernel(
-    proj_ref, halo_ref, before_ref, cols_ref, rows_ref, conv_ref, gain_ref, initial_ref,
-    gated_ref, out_ref, written_ref, inverse_ref, start_ref, state_ref,
+    low_ref, before_ref, table_ref, w_in_ref, w_rate_ref, w_out_ref, decay_ref,
+    conv_ref, gain_ref, initial_ref,
+    part_ref, proj_ref, rates_ref, cols_ref, gated_ref, out_ref, written_ref, inverse_ref,
+    start_ref, state_ref,
     padded_ref, mask_ref,
 ):
     heads, taps, mix_width = conv_ref.shape
     value_dim = gain_ref.shape[1]
     key_dim = (mix_width - value_dim) // 2
     in_width = mix_width + value_dim
-    width = proj_ref.shape[0]
+    width = low_ref.shape[0]
     block = pl.program_id(0)
+    every = range(heads)
 
     @pl.when(block == 0)
     def _():
         fill_level_masks(mask_ref)
         state_ref[...] = initial_ref[...]
-
-    for h in range(heads):
-        fill_halo(padded_ref, h, h * in_width, before_ref, halo_ref, block == 0)
-
-    cols = cols_ref[...]
-    rows = rows_ref[...]
-    offsets = gap_offsets(cols, rows)
-    every = range(heads)
+        for h in range(heads):
+            at = h * in_width
+            padded_ref[h, 0:HALO, :] = before_ref[:, at : at + mix_width].astype(F32)
+
+    @pl.when(block > 0)
+    def _():
+        for h in range(heads):
+            padded_ref[h, 0:HALO, :] = padded_ref[h, width : width + HALO, :]
+
+    low = low_ref[...]
+    gates = []
+    for h in every:
+        at = h * in_width
+        projected = dot_nn(low, w_in_ref[:, at : at + in_width])
+        proj_ref[:, at : at + in_width] = projected.astype(BF16)
+        padded_ref[h, HALO : HALO + width, :] = projected[:, :mix_width]
+        gates.append(projected[:, mix_width:])
+
+    table = table_ref[...]
+    rates = dot_nt(w_rate_ref[...], low)
+    rates_ref[...] = rates
+    log_decay = decay_ref[:, 0:1] * softplus(rates[:SLOTS] + decay_ref[:, 1:2])
+    cum = exact_dot(log_decay, triangle(width, True))
+    write = sigmoid(rates[SLOTS:]) * table[MASK : MASK + 1]
+    start = jnp.exp(cum) * table[CARRIED : CARRIED + 1]
+    last = jnp.exp(cum[:, width - 1 : width] - cum) * table[TO_LAST : TO_LAST + 1]
+    cols = jnp.concatenate([table[:SLOTS], write, cum, start, last], axis=0).T
+    cols_ref[...] = cols
+    offsets = gap_offsets(cols, table[SEGMENT : SEGMENT + 1])
+
     queries, keys, values = [], [], []
     for h in every:
-        at = h * in_width
-        padded_ref[h, HALO : HALO + width, :] = proj_ref[:, at : at + mix_width].astype(F32)
         summed, unused_rows = conv_rows(padded_ref, h, cols, conv_ref)
         mixed = summed * sigmoid(summed)
         query = mixed[:, :key_dim]
@@ -185,9 +215,7 @@
     keys_low = [key.astype(BF16) for key in keys]
     stacked = [jnp.concatenate([k, q], axis=0) for k, q in zip(keys_low, queries)]
     products = [dot_nt(both, key) for both, key in zip(stacked, keys_low)]
-    weights = [
-        jnp.exp(head_column(cols, h, CUM) - rows[1 + h : 2 + h, :] + offsets) for h in every
-    ]
+    weights = [jnp.exp(head_column(cols, h, CUM) - cum[h : h + 1, :] + offsets) for h in every]
     systems = [
         (products[h][:width] * weights[h] * head_column(cols, h, WRITE)).astype(BF16)
         for h in every
@@ -219,16 +247,18 @@
         out = (inner[h] + head_column(cols, h, START) * from_state[h][width:]) * keep
         out_ref[:, h * value_dim : (h + 1) * value_dim] = out.astype(BF16)
         scale = lax.rsqrt(row_sum(out * out) * (1.0 / value_dim) + 1e-05)
-        at = h * in_width + mix_width
-        gate = proj_ref[:, at : at + value_dim].astype(F32)
+        gate = gates[h]
         gated = out * scale * gain_ref[...] * (gate * sigmoid(gate))
         gated_ref[:, h * value_dim : (h + 1) * value_dim] = gated.astype(BF16)
+    part_ref[...] = dot_nn(gated_ref[...], w_out_ref[...]).astype(part_ref.dtype)
 
 
 def bwd_kernel(
-    cot_ref, proj_ref, halo_ref, before_ref, cols_ref, rows_ref, conv_ref, gain_ref,
+    cot_ref, low_ref, proj_ref, halo_ref, before_ref, table_ref, rates_ref, cols_ref,
+    w_in_ref, w_rate_ref, w_out_ref, decay_ref, conv_ref, gain_ref,
     out_ref, written_ref, inverse_ref, start_ref, initial_ref, after_ref,
-    grad_ref, tokens_ref, colsum_ref, conv_grad_ref, gain_grad_ref, state_ref, stash_ref,
+    part_ref, grad_ref, conv_grad_ref, gain_grad_ref, rate_grad_ref, decay_grad_ref,
+    state_ref, stash_ref,
     padded_ref, ahead_ref,
 ):
     heads, taps, mix_width = conv_ref.shape
@@ -237,23 +267,36 @@
     in_width = mix_width + value_dim
     width = proj_ref.shape[0]
     step = pl.program_id(0)
+    first = step == pl.num_programs(0) - 1
+    every = range(heads)
 
     @pl.when(step == 0)
     def _():
         conv_grad_ref[...] = jnp.zeros_like(conv_grad_ref)
         gain_grad_ref[...] = jnp.zeros_like(gain_grad_ref)
+        rate_grad_ref[...] = jnp.zeros_like(rate_grad_ref)
+        decay_grad_ref[...] = jnp.zeros_like(decay_grad_ref)
         state_ref[...] = initial_ref[...]
         ahead_ref[:, width : width + HALO, :] = after_ref[...]
 
-    for h in range(heads):
-        fill_halo(
-            padded_ref, h, h * in_width, before_ref, halo_ref, step == pl.num_programs(0) - 1
-        )
+    @pl.when(first)
+    def _():
+        for h in range(heads):
+            at = h * in_width
+            padded_ref[h, 0:HALO, :] = before_ref[:, at : at + mix_width].astype(F32)
+
+    @pl.when(jnp.logical_not(first))
+    def _():
+        for h in range(heads):
+            at = h * in_width
+            padded_ref[h, 0:HALO, :] = halo_ref[:, at : at + mix_width].astype(F32)
 
     cols = cols_ref[...]
-    rows = rows_ref[...]
-    offsets = gap_offsets(cols, rows)
-    every = range(heads)
+    table = table_ref[...]
+    offsets = gap_offsets(cols, table[SEGMENT : SEGMENT + 1])
+    rates = rates_ref[...]
+    log_decay = decay_ref[:, 0:1] * softplus(rates[:SLOTS] + decay_ref[:, 1:2])
+    cum = exact_dot(log_decay, triangle(width, True))
     keep = cols[:, MASK : MASK + 1]
     strict = (
         lax.broadcasted_iota(jnp.int32, (width, width), 0)
@@ -263,7 +306,7 @@
     cots, gain_grad = [], jnp.zeros((1, value_dim), F32)
     for h in every:
         at = h * in_width + mix_width
-        cot = cot_ref[:, h * value_dim : (h + 1) * value_dim].astype(F32)
+        cot = dot_nt(cot_ref[...], w_out_ref[h * value_dim : (h + 1) * value_dim, :])
         out = out_ref[:, h * value_dim : (h + 1) * value_dim].astype(F32)
         gate = proj_ref[:, at : at + value_dim].astype(F32)
         scale = lax.rsqrt(row_sum(out * out) * (1.0 / value_dim) + 1e-05)
@@ -297,9 +340,7 @@
     products = [
         dot_nt(jnp.concatenate([k, q], axis=0), k) for k, q in zip(keys_low, queries_low)
     ]
-    weights = [
-        jnp.exp(head_column(cols, h, CUM) - rows[1 + h : 2 + h, :] + offsets) for h in every
-    ]
+    weights = [jnp.exp(head_column(cols, h, CUM) - cum[h : h + 1, :] + offsets) for h in every]
     cots_low = [cot.astype(BF16) for cot in cots]
     grad_states = [state_ref[h] for h in every]
     grad_states_low = [state.astype(BF16) for state in grad_states]
@@ -342,16 +383,16 @@
     ]
     by_key = [dot_nn(both_grads[h], keys_low[h]) for h in every]
     by_state = [dot_nt(starts[h], start_ref[0, h]) for h in every]
-    both_rows = [
-        jnp.concatenate([queries_low[h], keys_low[h]], axis=0) for h in every
-    ]
+    both_rows = [jnp.concatenate([queries_low[h], keys_low[h]], axis=0) for h in every]
     turned = [dot_tn(both_grads[h], both_rows[h]) for h in every]
     by_last = [dot_nt(written[h], grad_states_low[h]) for h in every]
     states_part = [dot_tn(both_rows[h], starts[h]) for h in every]
 
-    lane = lax.broadcasted_iota(jnp.int32, tokens_ref.shape, 1)
+    lane = lax.broadcasted_iota(jnp.int32, (width, 2 * SLOTS), 1)
     place = lax.broadcasted_iota(jnp.int32, (width, 1), 0)
-    packed = jnp.zeros(tokens_ref.shape, F32)
+    packed = jnp.zeros((width, 2 * SLOTS), F32)
+    slot = lax.broadcasted_iota(jnp.int32, (SLOTS, width), 0)
+    column_sums = jnp.zeros((SLOTS, width), F32)
     for h in every:
         from_state = by_state[h]
         grad_query = by_key[h][:width] + from_state[:width]
@@ -372,9 +413,11 @@
             place == width - 1, total, 0.0
         )
         grad_logit = row_sum(grad_right[h] * written[h].astype(F32))
-        packed = packed + jnp.where(lane == 2 * h, grad_cum, 0.0)
-        packed = packed + jnp.where(lane == 2 * h + 1, grad_logit, 0.0)
-        colsum_ref[h : h + 1, :] = jnp.sum(gaps[h], axis=0, keepdims=True)
+        packed = packed + jnp.where(lane == h, grad_cum, 0.0)
+        packed = packed + jnp.where(lane == SLOTS + h, grad_logit, 0.0)
+        column_sums = column_sums + jnp.where(
+            slot == h, jnp.sum(gaps[h], axis=0, keepdims=True), 0.0
+        )
         state_ref[h] = final * grad_states[h] + states_part[h]
 
         summed = ahead_ref[h, 0:width, :]
@@ -413,7 +456,21 @@
         grad_ref[:, at : at + mix_width] = grad_pre.astype(BF16)
         ahead_ref[h, width : width + HALO, :] = ahead_ref[h, 0:HALO, :]
         stash_ref[h] = ahead_ref[h, 0:HALO, :]
-    tokens_ref[...] = packed
+
+    turned_rows = packed.T
+    grad_log_decay = exact_dot(turned_rows[:SLOTS] - column_sums, triangle(width, False))
+    shifted = rates[:SLOTS] + decay_ref[:, 1:2]
+    grad_decay = grad_log_decay * decay_ref[:, 0:1] * sigmoid(shifted)
+    grad_write = (
+        turned_rows[SLOTS:] * (1.0 - sigmoid(rates[SLOTS:])) * table[MASK : MASK + 1]
+    )
+    decay_grad_ref[0:SLOTS, :] += grad_log_decay * log_decay
+    decay_grad_ref[SLOTS : 2 * SLOTS, :] += grad_decay
+    grad_rates = jnp.concatenate([grad_decay, grad_write], axis=0).astype(BF16)
+    rate_grad_ref[...] += dot_nn(grad_rates, low_ref[...])
+    part_ref[...] = (
+        dot_nt(grad_ref[...], w_in_ref[...]) + dot_tn(grad_rates, w_rate_ref[...])
+    ).astype(part_ref.dtype)
 
 
 def segment_tables(segments, pad_mask, width):
@@ -436,184 +493,149 @@
     ends = seg_blocks[:, -1]
     carried = (seg_blocks == moved(ends, 1)[:, None]).astype(F32).reshape(-1)
     to_last = (seg_blocks == ends[:, None]).astype(F32).reshape(-1)
-    return jnp.stack(
-        [pad_mask.astype(F32), *back, *ahead, segments.astype(F32), carried, to_last]
-    )
-
-
-def token_tables(rate_rows, table, decay_log, decay_bias, width):
-    heads, length = rate_rows.shape[1:]
-    write = jax.nn.sigmoid(rate_rows[1]) * table[0]
-    log_decay = -jnp.exp(decay_log)[:, None] * jax.nn.softplus(
-        rate_rows[0] + decay_bias[:, None]
-    )
-    upper = jnp.triu(jnp.ones((width, width), F32))
-    cum = jnp.dot(
-        log_decay.reshape(-1, width), upper, precision=lax.Precision.HIGHEST
-    ).reshape(heads, length)
-    cum_blocks = cum.reshape(heads, -1, width)
-    start = jnp.exp(cum) * table[8]
-    last = jnp.exp(cum_blocks[:, :, -1:] - cum_blocks).reshape(heads, length) * table[9]
-    per_head = jnp.stack([write, cum, start, last], axis=1).reshape(4 * heads, length)
-    cols = jnp.concatenate([table[:8], per_head]).T
-    rows = jnp.concatenate(
-        [table[7:8], cum, jnp.zeros((-(1 + heads) % 8, length), F32)], axis=0
-    )
-    return cols, rows, log_decay
+    rows = [pad_mask.astype(F32), *back, *ahead, segments.astype(F32), carried, to_last]
+    return jnp.concatenate([jnp.stack(rows), jnp.zeros((-len(rows) % SLOTS, length), F32)])
 
 
 def whole_block(array):
     return pl.BlockSpec(array.shape, lambda c: (0,) * array.ndim)
 
 
-def mixer_forward(proj, before, cols, rows, conv, gain, initial, width):
+def kept_block(array):
+    return pl.BlockSpec(
+        array.shape, lambda c: (0,) * array.ndim, pipeline_mode=pl.Buffered(1)
+    )
+
+
+def last_rows(array):
+    return pl.BlockSpec((HALO, array.shape[1]), lambda c: (array.shape[0] // HALO - 1, 0))
+
+
+def mixer_forward(low, before, table, weights, decay, conv, gain, initial, width, part_dtype):
     heads, taps, mix_width = conv.shape
     value_dim = gain.shape[1]
     key_dim = (mix_width - value_dim) // 2
-    length = proj.shape[0]
+    in_width = heads * (mix_width + value_dim)
+    length, model_width = low.shape
     steps = length // width
-
-    def here(c):
-        return (c, 0)
-
-    def halo(c):
-        return (jnp.maximum(c * (width // HALO) - 1, 0), 0)
-
     levels = width.bit_length() - 1
-    wide = pl.BlockSpec((width, heads * value_dim), here)
-    wide_shape = jax.ShapeDtypeStruct((length, heads * value_dim), BF16)
+
+    def rows_of(columns):
+        return pl.BlockSpec((width, columns), lambda c: (c, 0))
+
+    def lanes_of(rows):
+        return pl.BlockSpec((rows, width), lambda c: (0, c))
+
+    def shape(dims, dtype):
+        return jax.ShapeDtypeStruct(dims, dtype)
+
+    value_width = heads * value_dim
     return pl.pallas_call(
         fwd_kernel,
         grid=(steps,),
-        in_specs=[
-            pl.BlockSpec((width, proj.shape[1]), here),
-            pl.BlockSpec((HALO, proj.shape[1]), halo),
-            whole_block(before),
-            pl.BlockSpec((width, cols.shape[1]), here),
-            pl.BlockSpec((rows.shape[0], width), lambda c: (0, c)),
-            whole_block(conv),
-            whole_block(gain),
-            whole_block(initial),
-        ],
+        in_specs=[rows_of(model_width), last_rows(before), lanes_of(table.shape[0])]
+        + [kept_block(array) for array in weights]
+        + [whole_block(array) for array in (decay, conv, gain, initial)],
         out_specs=[
-            wide,
-            wide,
-            wide,
+            rows_of(model_width),
+            rows_of(in_width),
+            lanes_of(2 * SLOTS),
+            rows_of(5 * SLOTS),
+            rows_of(value_width),
+            rows_of(value_width),
+            rows_of(value_width),
             pl.BlockSpec((1, heads, width, width), lambda c: (c, 0, 0, 0)),
             pl.BlockSpec((1, heads, key_dim, value_dim), lambda c: (c, 0, 0, 0)),
             whole_block(initial),
         ],
         out_shape=[
-            wide_shape,
-            wide_shape,
-            wide_shape,
-            jax.ShapeDtypeStruct((steps, heads, width, width), BF16),
-            jax.ShapeDtypeStruct((steps, heads, key_dim, value_dim), BF16),
-            jax.ShapeDtypeStruct(initial.shape, F32),
+            shape((length, model_width), part_dtype),
+            shape((length, in_width), BF16),
+            shape((2 * SLOTS, length), F32),
+            shape((length, 5 * SLOTS), F32),
+            shape((length, value_width), BF16),
+            shape((length, value_width), BF16),
+            shape((length, value_width), BF16),
+            shape((steps, heads, width, width), BF16),
+            shape((steps, heads, key_dim, value_dim), BF16),
+            shape(initial.shape, F32),
         ],
         scratch_shapes=[
             pltpu.VMEM((heads, HALO + width, mix_width), F32),
             pltpu.VMEM((levels, width, width), BF16),
         ],
-        compiler_params=pltpu.CompilerParams(vmem_limit_bytes=VMEM_BYTES),
+        compiler_params=pltpu.CompilerParams(vmem_limit_bytes=MIXER_VMEM_BYTES),
         cost_estimate=pl.CostEstimate(
-            flops=heads * steps * 16 * width * width * value_dim,
-            bytes_accessed=6 * length * heads * in_total(conv, gain),
-            transcendentals=0,
+            flops=length * model_width * 1024, bytes_accessed=length * 1024, transcendentals=0
         ),
         name="mixer_forward",
-    )(proj, proj, before, cols, rows, conv, gain, initial)
-
-
-def in_total(conv, gain):
-    return conv.shape[2] + gain.shape[1]
-
-
-def mixer_backward(cot, proj, before, cols, rows, conv, gain, kept, initial, after, width):
-    out, written, inverse, start = kept
+    )(low, before, table, *weights, decay, conv, gain, initial)
+
+
+def mixer_backward(
+    cot, low, table, weights, decay, conv, gain, kept, initial, after, width, part_dtype
+):
+    before, proj, rates, cols, out, written, inverse, start = kept
     heads, taps, mix_width = conv.shape
     value_dim = gain.shape[1]
     key_dim = (mix_width - value_dim) // 2
-    length = proj.shape[0]
+    length, model_width = low.shape
     steps = length // width
 
-    def at(c):
-        return steps - 1 - c
-
-    def here(c):
-        return (at(c), 0)
+    def rows_of(columns):
+        return pl.BlockSpec((width, columns), lambda c: (steps - 1 - c, 0))
+
+    def lanes_of(rows):
+        return pl.BlockSpec((rows, width), lambda c: (0, steps - 1 - c))
 
     def halo(c):
-        return (jnp.maximum(at(c) * (width // HALO) - 1, 0), 0)
-
-    wide = pl.BlockSpec((width, heads * value_dim), here)
-    sums = -(-heads // 8) * 8
+        return (jnp.maximum((steps - 1 - c) * (width // HALO) - 1, 0), 0)
+
+    def shape(dims, dtype=F32):
+        return jax.ShapeDtypeStruct(dims, dtype)
+
+    wide = rows_of(heads * value_dim)
+    rate_shape, decay_shape = (2 * SLOTS, model_width), (2 * SLOTS, width)
+    fixed = [conv.shape, gain.shape, rate_shape, decay_shape, initial.shape, after.shape]
     return pl.pallas_call(
         bwd_kernel,
         grid=(steps,),
         in_specs=[
-            wide,
-            pl.BlockSpec((width, proj.shape[1]), here),
+            rows_of(model_width),
+            rows_of(model_width),
+            rows_of(proj.shape[1]),
             pl.BlockSpec((HALO, proj.shape[1]), halo),
-            whole_block(before),
-            pl.BlockSpec((width, cols.shape[1]), here),
-            pl.BlockSpec((rows.shape[0], width), lambda c: (0, at(c))),
-            whole_block(conv),
-            whole_block(gain),
+            last_rows(before),
+            lanes_of(table.shape[0]),
+            lanes_of(2 * SLOTS),
+            rows_of(5 * SLOTS),
+        ]
+        + [kept_block(array) for array in weights]
+        + [whole_block(array) for array in (decay, conv, gain)]
+        + [
             wide,
             wide,
-            pl.BlockSpec((1, heads, width, width), lambda c: (at(c), 0, 0, 0)),
-            pl.BlockSpec((1, heads, key_dim, value_dim), lambda c: (at(c), 0, 0, 0)),
+            pl.BlockSpec((1, heads, width, width), lambda c: (steps - 1 - c, 0, 0, 0)),
+            pl.BlockSpec((1, heads, key_dim, value_dim), lambda c: (steps - 1 - c, 0, 0, 0)),
             whole_block(initial),
             whole_block(after),
         ],
-        out_specs=[
-            pl.BlockSpec((width, proj.shape[1]), here),
-            pl.BlockSpec((width, 2 * heads), here),
-            pl.BlockSpec((sums, width), lambda c: (0, at(c))),
-            whole_block(conv),
-            whole_block(gain),
-            whole_block(initial),
-            whole_block(after),
-        ],
-        out_shape=[
-            jax.ShapeDtypeStruct(proj.shape, BF16),
-            jax.ShapeDtypeStruct((length, 2 * heads), F32),
-            jax.ShapeDtypeStruct((sums, length), F32),
-            jax.ShapeDtypeStruct(conv.shape, F32),
-            jax.ShapeDtypeStruct(gain.shape, F32),
-            jax.ShapeDtypeStruct(initial.shape, F32),
-            jax.ShapeDtypeStruct(after.shape, F32),
-        ],
+        out_specs=[rows_of(model_width), rows_of(proj.shape[1])]
+        + [pl.BlockSpec(dims, lambda c, dims=dims: (0,) * len(dims)) for dims in fixed],
+        out_shape=[shape((length, model_width), part_dtype), shape(proj.shape, BF16)]
+        + [shape(dims) for dims in fixed],
         scratch_shapes=[
             pltpu.VMEM((heads, HALO + width, mix_width), F32),
             pltpu.VMEM((heads, width + HALO, mix_width), F32),
         ],
-        compiler_params=pltpu.CompilerParams(vmem_limit_bytes=VMEM_BYTES),
+        compiler_params=pltpu.CompilerParams(vmem_limit_bytes=MIXER_VMEM_BYTES),
         cost_estimate=pl.CostEstimate(
-            flops=heads * steps * 16 * width * width * value_dim,
-            bytes_accessed=8 * length * heads * in_total(conv, gain),
-            transcendentals=0,
+            flops=length * model_width * 1024, bytes_accessed=length * 1024, transcendentals=0
         ),
         name="mixer_backward",
-    )(cot, proj, proj, before, cols, rows, conv, gain, out, written, inverse, start, initial, after)
-
-
-def rate_gradients(tokens, colsum, rate_rows, mask_row, decay_log, decay_bias, log_decay, width):
-    heads, length = log_decay.shape
-    turned = tokens.T.reshape(heads, 2, length)
-    grad_cum = turned[:, 0] - colsum[:heads]
-    lower = jnp.tril(jnp.ones((width, width), F32))
-    grad_log_decay = jnp.dot(
-        grad_cum.reshape(-1, width), lower, precision=lax.Precision.HIGHEST
-    ).reshape(heads, length)
-    shifted = rate_rows[0] + decay_bias[:, None]
-    grad_decay = grad_log_decay * -jnp.exp(decay_log)[:, None] * jax.nn.sigmoid(shifted)
-    grad_write = turned[:, 1] * (1.0 - jax.nn.sigmoid(rate_rows[1])) * mask_row
-    return (
-        jnp.stack([grad_decay, grad_write]),
-        jnp.sum(grad_log_decay * log_decay, axis=1),
-        jnp.sum(grad_decay, axis=1),
+    )(
+        cot, low, proj, proj, before, table, rates, cols, *weights, decay, conv, gain,
+        out, written, inverse, start, initial, after,
     )
 
 
@@ -686,7 +708,7 @@
     )(second, turned[0], cot, turned[1], weights, weights, weights)
 
 
-def in_grad_kernel(count, *refs):
+def token_products_kernel(count, *refs):
     low_refs, refs, grad_ref, turned_ref = (
         refs[:count], refs[count : 2 * count], refs[-2], refs[-1]
     )
@@ -705,14 +727,15 @@
     grad_ref[...] = total.astype(BF16)
 
 
-def in_grad(lows, parts, tile):
+def token_products(lows, parts, tile, first=0, tiles=None):
     size, model_width = lows[0].shape
-    columns = parts[0].shape[1]
+    tiles = parts[0].shape[1] // tile if tiles is None else tiles
+    columns = tiles * tile
     return pl.pallas_call(
-        functools.partial(in_grad_kernel, len(parts)),
-        grid=(columns // tile,),
+        functools.partial(token_products_kernel, len(parts)),
+        grid=(tiles,),
         in_specs=[whole_block(low) for low in lows]
-        + [pl.BlockSpec((size, tile), lambda j: (0, j)) for unused in parts],
+        + [pl.BlockSpec((size, tile), lambda j: (0, first + j)) for unused in parts],
         out_specs=pl.BlockSpec((model_width, tile), lambda j: (0, j)),
         out_shape=jax.ShapeDtypeStruct((model_width, columns), BF16),
         scratch_shapes=[pltpu.VMEM((model_width, size * len(parts)), BF16)],
@@ -722,17 +745,28 @@
             bytes_accessed=2 * model_width * columns,
             transcendentals=0,
         ),
-        name="in_grad",
+        name="token_products",
     )(*lows, *parts)
 
 
 ROWS = 256
 
 
-def norm_kernel(rows_ref, gain_ref, low_ref):
+def store_part(part_refs, values):
+    block = pl.program_id(0)
+    blocks = part_refs[0].shape[0] // ROWS
+    for place, ref in enumerate(part_refs):
+
+        @pl.when(block // blocks == place)
+        def _(ref=ref):
+            at = pl.multiple_of((block % blocks) * ROWS, ROWS)
+            ref[pl.ds(at, ROWS), :] = values
+
+
+def norm_kernel(rows_ref, gain_ref, *low_refs):
     rows = rows_ref[...].astype(F32)
     scale = lax.rsqrt(row_sum(rows * rows) * (1.0 / rows.shape[1]) + 1e-05)
-    low_ref[...] = (rows * scale * gain_ref[...]).astype(BF16)
+    store_part(low_refs, (rows * scale * gain_ref[...]).astype(BF16))
 
 
 def part_specs(parts):
@@ -794,7 +828,7 @@
 
 
 def second_back_kernel(
-    back_ref, middle_ref, cot_ref, sum_ref, gain_ref, out_ref, grad_ref, low_ref, gain_grad_ref
+    back_ref, middle_ref, cot_ref, sum_ref, gain_ref, out_ref, grad_ref, gain_grad_ref, *low_refs
 ):
     middle = middle_ref[...]
     out_ref[...] = (middle + sum_ref[...]).astype(BF16)
@@ -802,7 +836,7 @@
     add_rows(gain_grad_ref, gain_grad)
     grad_middle = cot_ref[...].astype(F32) + grad_rows
     grad_ref[...] = grad_middle
-    low_ref[...] = grad_middle.astype(BF16)
+    store_part(low_refs, grad_middle.astype(BF16))
 
 
 def first_back_kernel(starts, per_part, rows_ref, middle_grad_ref, gain_ref, *refs):
@@ -823,6 +857,8 @@
         "turned": (pl.BlockSpec((width, ROWS), lambda i: (0, i)), (width, rows[0])),
         "gain": (pl.BlockSpec((1, width), lambda i: (0, 0)), (1, width)),
     }
+    part = min(PART, rows[0])
+    kinds["part"] = (pl.BlockSpec((part, width), lambda i: (0, 0)), (part, width))
     return pl.pallas_call(
         kernel,
         grid=(rows[0] // ROWS,),
@@ -838,8 +874,9 @@
 def norm_rows(rows, gain):
     gain = gain[None]
     return row_call(
-        norm_kernel, rows.shape, [(rows, None), (gain, whole_block(gain))], [("rows", BF16)], [], "norm_rows"
-    )[0]
+        norm_kernel, rows.shape, [(rows, None), (gain, whole_block(gain))],
+        [("part", BF16)] * max(1, rows.shape[0] // PART), [], "norm_rows"
+    )
 
 
 def middle_rows(rows, gain, parts):
@@ -864,7 +901,8 @@
         second_back_kernel,
         middle.shape,
         [(back, None), (middle, None), (cot, None), (ffn_out, None), (gain, whole_block(gain))],
-        [("rows", BF16), ("rows", F32), ("rows", BF16), ("gain", F32)],
+        [("rows", BF16), ("rows", F32), ("gain", F32)]
+        + [("part", BF16)] * max(1, middle.shape[0] // PART),
         [],
         "second_back",
     )
@@ -886,6 +924,89 @@
     )
 
 
+def share_kernel(kinds, own_ref, *refs):
+    received, out_ref, share_ref = refs[:-2], refs[-2], refs[-1]
+    rows, hidden = share_ref.shape[0], received[0].shape[1]
+    for kind in range(kinds):
+        at = slice(kind * rows, (kind + 1) * rows)
+        total = own_ref[at, 0:hidden].astype(F32)
+        for ref in received:
+            total = total + ref[at, :].astype(F32)
+        share_ref[:, kind * hidden : (kind + 1) * hidden] = total.astype(BF16)
+    share_ref[:, kinds * hidden :] = out_ref[...]
+
+
+def join_shares(own, received, out):
+    hidden, rows = received[0].shape[1], out.shape[0]
+    kinds = own.shape[0] // rows
+    if hidden % 128:
+        total = own[:, :hidden]
+        for part in received:
+            total = total + part
+        return jnp.concatenate([*total.reshape(kinds, rows, hidden), out], axis=1)
+    operands = (own, *received, out)
+    shape = (rows, kinds * hidden + out.shape[1])
+    return pl.pallas_call(
+        functools.partial(share_kernel, kinds),
+        grid=(1,),
+        in_specs=[whole_block(array) for array in operands],
+        out_specs=pl.BlockSpec(shape, lambda c: (0, 0)),
+        out_shape=jax.ShapeDtypeStruct(shape, BF16),
+        name="join_shares",
+    )(*operands)
+
+
+def spread_kernel(hidden, grads_ref, gate_up_ref, down_ref, out_ref, in_ref):
+    grads = grads_ref[...]
+    for kind in range(2):
+        gate_up_ref[:, kind, :] = grads[:, kind * hidden : (kind + 1) * hidden].astype(F32)
+    down_ref[...] = grads[:, 2 * hidden : 3 * hidden].astype(F32).T
+    at = 3 * hidden
+    out_ref[...] = grads[:, at : at + out_ref.shape[1]].astype(F32)
+    at += out_ref.shape[1]
+    heads, in_width = in_ref.shape[1:]
+    for h in range(heads):
+        in_ref[:, h, :] = grads[:, at + h * in_width : at + (h + 1) * in_width].astype(F32)
+
+
+def spread_grads(grads, hidden, heads, in_width):
+    model_width, columns = grads.shape
+    out_width = columns - 3 * hidden - heads * in_width
+    if hidden % 128:
+        at = 3 * hidden + out_width
+        wide = grads.astype(F32)
+        return (
+            wide[:, : 2 * hidden].reshape(model_width, 2, hidden),
+            wide[:, 2 * hidden : 3 * hidden].T,
+            wide[:, 3 * hidden : at],
+            wide[:, at:].reshape(model_width, heads, in_width),
+        )
+    rows = 128
+
+    def shape(*dims):
+        return jax.ShapeDtypeStruct(dims, F32)
+
+    return pl.pallas_call(
+        functools.partial(spread_kernel, hidden),
+        grid=(model_width // rows,),
+        in_specs=[pl.BlockSpec((rows, columns), lambda c: (c, 0))],
+        out_specs=[
+            pl.BlockSpec((rows, 2, hidden), lambda c: (c, 0, 0)),
+            pl.BlockSpec((hidden, rows), lambda c: (0, c)),
+            pl.BlockSpec((rows, out_width), lambda c: (c, 0)),
+            pl.BlockSpec((rows, heads, in_width), lambda c: (c, 0, 0)),
+        ],
+        out_shape=[
+            shape(model_width, 2, hidden),
+            shape(hidden, model_width),
+            shape(model_width, out_width),
+            shape(model_width, heads, in_width),
+        ],
+        compiler_params=pltpu.CompilerParams(vmem_limit_bytes=VMEM_BYTES),
+        name="spread_grads",
+    )(grads)
+
+
 def after(array, other):
     return lax.optimization_barrier((array, other))[0]
 
@@ -914,25 +1035,27 @@
     return array
 
 
-def scatter_sum_dp(array, meanwhile=None):
+def scatter_steps(array, meanwhile):
     size = lax.axis_size("dp")
     if not is_power(size):
-        return lax.psum_scatter(array, "dp", scatter_dimension=0, tiled=True)
+        yield lax.psum_scatter(array, "dp", scatter_dimension=0, tiled=True)
+        return
     index = lax.axis_index("dp")
     columns = array.shape[1]
     blocks = array.reshape(size, -1, columns)
-    bit = 1
+    bit, step = 1, 0
     while bit < size:
         halves = blocks.reshape(-1, 2, blocks.shape[1], columns)
         mine = (index // bit) % 2
         keep = lax.dynamic_index_in_dim(halves, mine, 1, keepdims=False)
         send = lax.dynamic_index_in_dim(halves, 1 - mine, 1, keepdims=False)
         other = partner(send, "dp", bit)
-        if bit == 2 and meanwhile is not None:
-            other = after(other, meanwhile)
+        waits = meanwhile(step)
+        if waits is not None:
+            other = after(other, waits)
         blocks = keep + other
-        bit *= 2
-    return blocks[0]
+        bit, step = bit * 2, step + 1
+        yield blocks if bit < size else blocks[0]
 
 
 def shards(
@@ -962,11 +1085,10 @@
     value_dim = head_gain.shape[0]
     key_dim = (conv_weight.shape[2] - value_dim) // 2
 
-    def sequences(rows):
+    def sequences(own):
         if pair:
-            own = [rows[at : at + PART] for at in range(0, SEQ, PART)]
             return [own, [turn(part, "tensor", 1) for part in own]]
-        whole = lax.all_gather(rows, "tensor", axis=0, tiled=True)
+        whole = lax.all_gather(jnp.concatenate(own), "tensor", axis=0, tiled=True)
         return [
             [whole[at + by : at + by + PART] for by in range(0, SEQ, PART)]
             for at in range(0, whole.shape[0], SEQ)
@@ -995,10 +1117,16 @@
         ]
 
     w_in = in_weight.reshape(model_width, heads_here * in_width)
-    w_rate = rate_weight.transpose(2, 1, 0).reshape(2 * heads_here, model_width)
+    w_rate = jnp.pad(
+        rate_weight.transpose(2, 1, 0), ((0, 0), (0, SLOTS - heads_here), (0, 0))
+    ).reshape(2 * SLOTS, model_width)
+    decay = jnp.pad(
+        jnp.stack([-jnp.exp(decay_log), decay_bias], axis=1), ((0, SLOTS - heads_here), (0, 0))
+    )
     w_out = out_weight.reshape(-1, model_width)
     conv_float = conv_weight.astype(F32)
     gain_row = head_gain[None]
+    mixer_weights = (w_in, w_rate, w_out)
     normed = norm_rows(residual_in, mixer_gain)
 
     rows_share = model_width // share
@@ -1011,7 +1139,7 @@
         ]
     )
     pieces = [piece] + [
-        after(turn(piece, "tensor", shift), normed) for shift in range(1, members)
+        after(turn(piece, "tensor", shift), (normed, w_in)) for shift in range(1, members)
     ]
     pieces = jnp.concatenate(
         [part[kind] for kind in range(3) for part in pieces], axis=1
@@ -1036,29 +1164,25 @@
         order = [(s, p) for p in range(count) for s in range(local)]
     done = None
     for place, (s, p) in enumerate(order):
-            low_rows = first[s][p]
-            if done is not None:
-                low_rows = after(low_rows, done)
-            if pair and place == len(order) - 1:
-                low_rows = after(low_rows, arrived)
-            projected = dot_nn(low_rows, w_in).astype(BF16)
-            rate_rows = dot_nt(w_rate, low_rows).reshape(2, heads_here, PART)
-            cols, rows, log_decay = token_tables(
-                rate_rows, tables[s][:, p * PART : (p + 1) * PART], decay_log, decay_bias, BLOCK
-            )
-            gated, *kept, states[s] = mixer_forward(
-                projected, befores[s], cols, rows, conv_float, gain_row, states[s], BLOCK
-            )
-            forward[s][p] = (
-                projected, befores[s], rate_rows, cols, rows, log_decay, gated, kept
-            )
-            befores[s] = projected[-HALO:]
-            out_parts[s][p] = dot_nn(gated, w_out)
-            done = out_parts[s][p]
-            if pair and s == 1:
-                out_parts[s][p] = turn(out_parts[s][p].astype(BF16), "tensor", 1)
-                if p < count - 1:
-                    arrived = out_parts[s][p]
+        low_rows = first[s][p]
+        if done is not None:
+            low_rows = after(low_rows, done)
+        if pair and place == len(order) - 1:
+            low_rows = after(low_rows, arrived)
+        table = tables[s][:, p * PART : (p + 1) * PART]
+        travels = pair and s == 1
+        part, proj, rates, cols, gated, *kept, states[s] = mixer_forward(
+            low_rows, befores[s], table, mixer_weights, decay, conv_float, gain_row, states[s],
+            BLOCK, BF16 if travels else F32,
+        )
+        forward[s][p] = (table, gated, (befores[s], proj, rates, cols, *kept))
+        befores[s] = proj
+        done = part
+        out_parts[s][p] = part
+        if travels:
+            out_parts[s][p] = turn(part, "tensor", 1)
+            if p < count - 1:
+                arrived = out_parts[s][p]
     middle, second, second_turned = middle_rows(residual_in, ffn_gain, owner_parts(out_parts))
     ffn_out, grad_second, grads_ffn = feed_forward(
         second, second_turned, out_grad, weights, share
@@ -1066,73 +1190,95 @@
     ffn_shares = lax.psum_scatter(
         grads_ffn.reshape(-1, grads_ffn.shape[-1]), "dp", scatter_dimension=0, tiled=True
     )
-    layer_out, grad_middle, grad_mix, grad_ffn_gain = second_back(
+    layer_out, grad_middle, grad_ffn_gain, *grad_mix = second_back(
         grad_second, middle, out_grad, ffn_out, ffn_gain
     )
     cots = sequences(grad_mix)
     every = [(s, p) for s in range(local) for p in range(count)]
-    gated_all = jnp.concatenate([forward[s][p][6] for s, p in every])
-    cots_all = jnp.concatenate([cots[s][p] for s, p in every])
-    grad_out = dot_tn(gated_all, cots_all).astype(BF16)
     grad_states = [jnp.zeros((heads_here, key_dim, value_dim), F32)] * local
     afters = [jnp.zeros((heads_here, HALO, conv_weight.shape[2]), F32)] * local
     first_parts = [[None] * count for unused in range(local)]
     proj_lows = [[None] * count for unused in range(local)]
-    grad_rate, sums = 0.0, 0.0
+    sums = 0.0
     done = None
+    half = local * count // 2
+    out_waits = {}
+    grad_in = None
     for place, (s, p) in enumerate(reversed(order)):
-            projected, before, rate_rows, cols, rows, log_decay, gated, kept = forward[s][p]
-            grad_gated = dot_nt(cots[s][p], w_out).astype(BF16)
-            if done is not None:
-                grad_gated = after(grad_gated, done)
-            if place == local * count // 2:
-                grad_gated = after(grad_gated, grad_out)
-            proj_low, tokens, colsum, grad_conv, grad_head_gain, grad_states[s], afters[s] = (
-                mixer_backward(
-                    grad_gated, projected, before, cols, rows, conv_float, gain_row, kept,
-                    grad_states[s], afters[s], BLOCK,
-                )
+        table, gated, kept = forward[s][p]
+        cot = cots[s][p]
+        if done is not None:
+            cot = after(cot, done)
+        if place == half:
+            grad_out = token_products(
+                [after(forward[s][p][1], done) for s, p in every],
+                [cots[s][p] for s, p in every],
+                model_width // 2,
             )
-            grad_rates, grad_log, grad_bias = rate_gradients(
-                tokens, colsum, rate_rows, tables[s][0, p * PART : (p + 1) * PART],
-                decay_log, decay_bias, log_decay, BLOCK,
+            out_steps = scatter_steps(grad_out, out_waits.get)
+        if place >= half:
+            share_out = next(out_steps)
+            cot = after(cot, share_out)
+        travels = pair and s == 1
+        part, proj_low, grad_conv, grad_gain, grad_rate, grad_decay, grad_states[s], afters[s] = (
+            mixer_backward(
+                cot, first[s][p], table, mixer_weights, decay, conv_float, gain_row,
+                kept, grad_states[s], afters[s], BLOCK, BF16 if travels else F32,
             )
-            rates_low = grad_rates.astype(BF16).reshape(2 * heads_here, PART)
-            grad_rate = grad_rate + dot_nn(rates_low, first[s][p])
-            first_parts[s][p] = dot_nt(proj_low, w_in) + dot_tn(rates_low, w_rate)
-            proj_lows[s][p] = after(proj_low, first_parts[s][p])
-            done = first_parts[s][p]
-            if pair and s == 1:
-                first_parts[s][p] = turn(first_parts[s][p].astype(BF16), "tensor", 1)
-            sums = sums + jnp.concatenate(
-                [grad_conv.reshape(-1), grad_head_gain[0], grad_log, grad_bias]
-            )
+        )
+        proj_lows[s][p] = proj_low
+        done = part
+        first_parts[s][p] = turn(part, "tensor", 1) if travels else part
+        out_waits[place - half + 1] = done
+        grad_decay = jnp.sum(grad_decay.reshape(2, SLOTS, BLOCK), axis=2)
+        sums = sums + jnp.concatenate(
+            [
+                grad_conv.reshape(-1),
+                grad_gain[0],
+                grad_decay[:, :heads_here].reshape(-1),
+                grad_rate.reshape(2, SLOTS, model_width)[:, :heads_here].reshape(-1),
+            ]
+        )
     input_grad, grad_mixer_gain = first_back(
         residual_in, grad_middle, mixer_gain, owner_parts(first_parts)
     )
-    share_out = scatter_sum_dp(grad_out)
+    proj_lows[0][0] = after(proj_lows[0][0], first_parts[-1])
+    share_out = next(out_steps)
     proj_lows[0][0] = after(proj_lows[0][0], share_out)
-    grad_in = in_grad(
-        [first[s][p] for s, p in every], [proj_lows[s][p] for s, p in every], in_width
-    )
-    ffn_shares = after(ffn_shares, done)
-    share_ffn = ffn_shares[:, :hidden_here]
-    for shift in range(1, members):
-        share_ffn = share_ffn + turn(
-            ffn_shares[:, shift * hidden_here : (shift + 1) * hidden_here], "tensor", -shift
-        )
-    share_ffn = share_ffn.reshape(3, rows_share, hidden_here)
-    share_early = jnp.concatenate([*share_ffn, share_out.reshape(rows_share, -1)], axis=1)
-    early = lax.all_gather(share_early, "dp", axis=0, tiled=True)
-    if pair:
-        grad_in = after(grad_in, first_parts[1])
-    grad_in = after(grad_in, share_early)
-
-    small = jnp.concatenate([sums, grad_rate.reshape(-1), grad_mixer_gain[0], grad_ffn_gain[0]])
+    lows = [first[s][p] for s, p in every]
+    proj_parts = [proj_lows[s][p] for s, p in every]
+    columns = heads_here * in_width // 2
+    tile = columns // 2 if columns % (2 * LANES) == 0 else columns
+    grad_in_one = token_products(lows, proj_parts, tile, 0, columns // tile)
+    out_waits[3] = grad_in_one
+    for share_out in out_steps:
+        pass
+    waits_one, waits_two = {}, {}
+    steps_one = scatter_steps(after(grad_in_one, share_out), waits_one.get)
+    share_one = next(steps_one)
+    proj_parts[0] = after(proj_parts[0], share_one)
+    grad_in_two = token_products(lows, proj_parts, tile, columns // tile, columns // tile)
+    small = jnp.concatenate([sums, grad_mixer_gain[0], grad_ffn_gain[0]])
     length = small.shape[0]
     small = jnp.pad(small, (0, -length % 1024)).reshape(-1, 1024)
     small = sum_small(small, "dp").reshape(-1)
-    share_in = scatter_sum_dp(grad_in, small)
+    waits_one[1] = grad_in_two
+    share_one = next(steps_one, share_one)
+    steps_two = scatter_steps(after(grad_in_two, share_one), waits_two.get)
+    share_two = next(steps_two)
+    ffn_shares = after(ffn_shares, share_two)
+    received = [
+        turn(ffn_shares[:, shift * hidden_here : (shift + 1) * hidden_here], "tensor", -shift)
+        for shift in range(1, members)
+    ]
+    share_early = join_shares(ffn_shares, received, share_out.reshape(rows_share, -1))
+    waits_one[2] = share_two
+    for step, share_one in enumerate(steps_one, 2):
+        waits_two[step - 1] = [share_one, received] if step == 3 else share_one
+        share_two = next(steps_two, share_two)
+    waits_two[3] = share_early
+    for share_two in steps_two:
+        pass
     conv_size = conv_weight.size
     rate_size = rate_weight.size
     grad_conv = small[:conv_size].reshape(conv_weight.shape)
@@ -1148,13 +1294,11 @@
     grad_mixer_gain = gains[value_dim : value_dim + model_width]
     grad_ffn_gain = gains[value_dim + model_width :]
 
-    share_in = share_in.reshape(rows_share, heads_here, in_width)
-    grad_in = lax.all_gather(share_in, "dp", axis=0, tiled=True)
-    width = 2 * hidden_here
-    grad_gate_up = early[:, :width].reshape(gate_up.shape).astype(F32)
-    grad_down = early[:, width : width + hidden_here].astype(F32).T
-    grad_out = early[:, width + hidden_here :].astype(F32).reshape(out_weight.shape)
-    grad_in = after(grad_in, (grad_gate_up, grad_down, grad_out)).astype(F32)
+    grads = jnp.concatenate([share_early, share_one, share_two], axis=1)
+    grads = lax.all_gather(grads, "dp", axis=0, tiled=True)
+    grad_gate_up, grad_down, grad_out, grad_in = spread_grads(
+        grads, hidden_here, heads_here, in_width
+    )
     return (
         layer_out,
         input_grad,
@@ -1165,7 +1309,7 @@
         grad_log,
         grad_bias,
         grad_head_gain,
-        grad_out,
+        grad_out.reshape(out_weight.shape),
         grad_ffn_gain,
         grad_gate_up,
         grad_down,

time: 697 us -> 582 us (0.84)
  matrix products: 115 us -> 0 us
  Pallas kernels: 267 us -> 357 us
  local copies, waits for them, and re-layouts: 95.6 us -> 38.4 us
  other arithmetic: 30.6 us -> 7.17 us
  waiting for transfers between devices: 137 us -> 129 us
    dot_general x37 -> x0, matrix products: 115 us -> none  [the longest x12 48.6 us: dot_nn(): lax.dot_general(left, right, (((1,), (0,)), ((), ())), preferred_element_...]
    pallas_call x9 -> x13, Pallas kernels: 174 us -> 264 us  [the longest x4 121 us: mixer_backward(): pl.pallas_call(bwd_kernel, grid=(steps,), in_specs=[rows_of(model_width),...]
    all_gather x2 -> x1, waiting for transfers between devices: 12.4 us -> 52.4 us  [shards(): grads = lax.all_gather(grads, 'dp', axis=0, tiled=True)]
    ppermute x10, waiting for transfers between devices: 36 us -> 2.13 us  [turn(): lax.ppermute(array, axis, [((i + shift) % size, i) for i in range(size)])]
    unnamed x113 -> x104, local copies, waits for them, and re-layouts: 47.6 us -> 20.2 us
    slice x25 -> x2, local copies, waits for them, and re-layouts: 15.8 us -> 1.25 us  [shards(): table = tables[s][:, p * PART:(p + 1) * PART]]
    ppermute x13 -> x17, waiting for transfers between devices: 88.4 us -> 74.1 us  [partner(): lax.ppermute(array, axis, [(i, i ^ bit) for i in range(lax.axis_size(axis...]
    convert_element_type x5 -> x2, other arithmetic: 9.37 us -> 0.17 us  [segment_tables(): to_last = (seg_blocks == ends[:, None]).astype(F32).reshape(-1)]
  transfers between devices with their start and end apart: 27 -> 30, of which waited for: 15 -> 17; matrix products, arithmetic and copies ran while one was open for 31% -> 6% of each run, Pallas kernels for 30% -> 48%
where the time goes in v2:
time: 582 us; the launch traced here: 574 us
  Pallas kernels  357 us (61%)
  waiting for transfers between devices  129 us (22%)
  local copies, waits for them, and re-layouts  38.4 us (7%)
  starting transfers between devices  27.9 us (5%)
  between operations  14.9 us (3%)
  other arithmetic  7.17 us (1%)
    pallas_call x4, Pallas kernels, mixer_backward(): pl.pallas_call(bwd_kernel, grid=(steps,), in_specs=[rows_of(model_width),...  121 us
    pallas_call x4, Pallas kernels, mixer_forward(): pl.pallas_call(fwd_kernel, grid=(steps,), in_specs=[rows_of(model_width),...  86.1 us
    ppermute x17, waiting for transfers between devices, partner(): lax.ppermute(array, axis, [(i, i ^ bit) for i in range(lax.axis_size(axis...  74.1 us
    pallas_call x1, Pallas kernels, feed_forward(): pl.pallas_call(ffn_kernel, grid=(tiles,), in_specs=[whole_block(second),...  63.3 us
    all_gather x1, waiting for transfers between devices, shards(): grads = lax.all_gather(grads, 'dp', axis=0, tiled=True)  52.4 us
    pallas_call x3, Pallas kernels, token_products(): pl.pallas_call(functools.partial(token_products_kernel, len(parts)), grid...  36 us
    pallas_call x4, Pallas kernels, row_call(): pl.pallas_call(kernel, grid=(rows[0] // ROWS,), in_specs=[block if spec i...  29.6 us
    unnamed x104, local copies, waits for them, and re-layouts  20.2 us
  transfers between devices with their start and end apart: 30, of which 17 were waited for; matrix products, arithmetic and copies ran while one was open for 6% of the time, Pallas kernels for 48%

profile of v2, /device:TPU:0, one launch (start us, length us, event | category | flops | bytes accessed | tf_op | source)
XLA Modules:
  0.0 573.8 jit_solution(5365893433506770939)
XLA Ops:
  11.2 3.0 collective-permute-start.4
  14.2 7.0 %copy.55 = bf16[128,8,4,768]{3,1,2,0:T(8,128)(2,1)} copy(bf16[128,8,4,768]{3,2,1,0:T(4,128)(2,1)} %bitcast.178) | data formatting | bytes 12582912
  21.2 4.2 norm_rows.1
  37.8 21.3 %mixer_forward.4 = (f32[512,1024]{1,0:T(8,128)}, bf16[512,3072]{1,0:T(8,128)(2,1)}, f32[16,512]{1,0:T(8,128)}, f32[512,40]{1,0:T(8,128)}, bf16[512,1024]{1,0:T(8...) custom-call(bf16[512,1024]{1,0:T(8,128)(2,1)} %get-tuple-element.127, ...), custom_call_target="tpu_custom_call" | custom-call | flops 536870912 | bytes 524288 | tf_op jit(solution)/shard_map/mixer_forward/pallas_call | solution.py:533
  60.8 21.4 %mixer_forward.5 = (bf16[512,1024]{1,0:T(8,128)(2,1)}, bf16[512,3072]{1,0:T(8,128)(2,1)}, f32[16,512]{1,0:T(8,128)}, f32[512,40]{1,0:T(8,128)}, bf16[512,1024]{1...) custom-call(bf16[512,1024]{1,0:T(8,128)(2,1)} %copy-done.3, ...), custom_call_target="tpu_custom_call" | custom-call | flops 536870912 | bytes 524288 | tf_op jit(solution)/shard_map/mixer_forward/pallas_call | solution.py:533
  84.0 21.6 %mixer_forward.6 = (bf16[512,1024]{1,0:T(8,128)(2,1)}, bf16[512,3072]{1,0:T(8,128)(2,1)}, f32[16,512]{1,0:T(8,128)}, f32[512,40]{1,0:T(8,128)}, bf16[512,1024]{1...) custom-call(bf16[512,1024]{1,0:T(8,128)(2,1)} %collective-permute-do, ...), custom_call_target="tpu_custom_call" | custom-call | flops 536870912 | bytes 524288 | tf_op jit(solution)/shard_map/mixer_forward/pallas_call | solution.py:533
  108.5 21.8 %mixer_forward.7 = (f32[512,1024]{1,0:T(8,128)}, bf16[512,3072]{1,0:T(8,128)(2,1)}, f32[16,512]{1,0:T(8,128)}, f32[512,40]{1,0:T(8,128)}, bf16[512,1024]{1,0:T(8...) custom-call(bf16[512,1024]{1,0:T(8,128)(2,1)} %get-tuple-element.137, ...), custom_call_target="tpu_custom_call" | custom-call | flops 536870912 | bytes 524288 | tf_op jit(solution)/shard_map/mixer_forward/pallas_call | solution.py:533
  131.2 7.7 %middle_rows.1 = (f32[1024,1024]{1,0:T(8,128)}, bf16[1024,1024]{1,0:T(8,128)(2,1)}, bf16[1024,1024]{1,0:T(8,128)(2,1)}) custom-call(bf16[1024,1024]{1,0:T(8,128)(2,1)} %rows_ref.5, f32[1,1024]{1,0:T(1,128)} %bitcast.241, f32[512,1024]{1,0:T(8,128)} %get-tuple-element.128.refs_0_, bf16[512,1024]{1,0:T(8,128)(2,1)} %collective-permute-done.1.refs_1_, ...), custom_call_target="tpu_custom_call" | custom-call | tf_op jit(solution)/shard_map/middle_rows/pallas_call | solution.py:862
  139.0 63.3 %feed_forward.1 = (f32[1024,1024]{1,0:T(8,128)}, f32[1024,1024]{1,0:T(8,128)}, bf16[16,3,64,2816]{3,2,1,0:T(8,128)(2,1)}) custom-call(bf16[1024,1024]{1,0:T(8,128)(2,1)} %get-tuple-element.141.second_ref, bf16[1024,1024]{1,0:T(8,128)(2,1)} %get-tuple-element.142.second_turned_ref, bf16[1024,1024]{1,0:T(8,128)(2,1)} %cot_ref.3, bf16[1024,1024]{1,0:T(8,128)(2,1)} %bitcast.185, ...), custom_call_target="tpu_custom_call" | custom-call | flops 17716740096 | bytes 34603008 | tf_op jit(solution)/shard_map/feed_forward/pallas_call | solution.py:683
  202.4 10.0 %second_back.1 = (bf16[1024,1024]{1,0:T(8,128)(2,1)}, f32[1024,1024]{1,0:T(8,128)}, f32[1,1024]{1,0:T(1,128)}, bf16[512,1024]{1,0:T(8,128)(2,1)}, bf16[512,1024]{1,0:T(8,128)(2,1)}) custom-call(f32[1024,1024]{1,0:T(8,128)} %get-tuple-element.144.back_ref, f32[1024,1024]{1,0:T(8,128)} %get-tuple-element.145.middle_ref, bf16[1024,1024]{1,0:T(8,128)(2,1)} %cot_ref.3, ...), custom_call_target="tpu_custom_call" | custom-call | tf_op jit(solution)/shard_map/second_back/pallas_call | solution.py:862
  215.1 32.3 %mixer_backward.4 = (f32[512,1024]{1,0:T(8,128)}, bf16[512,3072]{1,0:T(8,128)(2,1)}, f32[4,4,512]{2,1,0:T(4,128)}, f32[1,256]{1,0:T(1,128)}, f32[16,1024]{1,0:T(...) custom-call(bf16[512,1024]{1,0:T(8,128)(2,1)} %get-tuple-element.150.cot_ref.refs_5_, ...), custom_call_target="tpu_custom_call" | custom-call | flops 536870912 | bytes 524288 | tf_op jit(solution)/shard_map/mixer_backward/pallas_call | solution.py:600
  248.5 29.7 %mixer_backward.5 = (bf16[512,1024]{1,0:T(8,128)(2,1)}, bf16[512,3072]{1,0:T(8,128)(2,1)}, f32[4,4,512]{2,1,0:T(4,128)}, f32[1,256]{1,0:T(1,128)}, f32[16,1024]{...) custom-call(bf16[512,1024]{1,0:T(8,128)(2,1)} %copy-done.10, ...), custom_call_target="tpu_custom_call" | custom-call | flops 536870912 | bytes 524288 | tf_op jit(solution)/shard_map/mixer_backward/pallas_call | solution.py:600
  279.2 10.2 %token_products.3 = bf16[1024,1024]{1,0:T(8,128)(2,1)} custom-call(bf16[512,1024]{1,0:T(8,128)(2,1)} %get-tuple-element.170.refs_0_, bf16[512,1024]{1,0:T(8,128)(2,1)} %get-tuple-element.172.refs_1_, bf16[512,1024]{1,0:T(8,128)(2,1)} %get-tuple-element.174.refs_2_, bf16[512,1024]{1,0:T(8,128)(2,1)} %get-tuple-element.176.refs_3_, ...), custom_call_target="tpu_custom_call" | custom-call | flops 1073741824 | bytes 2097152 | tf_op jit(solution)/shard_map/token_products/pallas_call | solution.py:734
  291.0 2.7 collective-permute-done.7
  298.8 29.4 %mixer_backward.6 = (bf16[512,1024]{1,0:T(8,128)(2,1)}, bf16[512,3072]{1,0:T(8,128)(2,1)}, f32[4,4,512]{2,1,0:T(4,128)}, f32[1,256]{1,0:T(1,128)}, f32[16,1024]{...) custom-call(bf16[512,1024]{1,0:T(8,128)(2,1)} %copy-done.9, ...), custom_call_target="tpu_custom_call" | custom-call | flops 536870912 | bytes 524288 | tf_op jit(solution)/shard_map/mixer_backward/pallas_call | solution.py:600
  330.3 29.4 %mixer_backward.7 = (f32[512,1024]{1,0:T(8,128)}, bf16[512,3072]{1,0:T(8,128)(2,1)}, f32[4,4,512]{2,1,0:T(4,128)}, f32[1,256]{1,0:T(1,128)}, f32[16,1024]{1,0:T(...) custom-call(bf16[512,1024]{1,0:T(8,128)(2,1)} %get-tuple-element.190.refs_4_.cot_ref, ...), custom_call_target="tpu_custom_call" | custom-call | flops 536870912 | bytes 524288 | tf_op jit(solution)/shard_map/mixer_backward/pallas_call | solution.py:600
  359.8 2.9 collective-permute-start.17
  362.7 13.1 %token_products.4 = bf16[1024,1536]{1,0:T(8,128)(2,1)} custom-call(bf16[512,1024]{1,0:T(8,128)(2,1)} %get-tuple-element.127.low_ref.refs_0_, bf16[512,1024]{1,0:T(8,128)(2,1)} %get-tuple-element.137.low_ref.refs_1_, bf16[512,1024]{1,0:T(8,128)(2,1)} %copy-done.3, bf16[512,1024]{1,0:T(8,128)(2,1)} %collective-permute-done.2.low_ref.refs_3_, ...), custom_call_target="tpu_custom_call" | custom-call | flops 1610612736 | bytes 3145728 | tf_op jit(solution)/shard_map/token_products/pallas_call | solution.py:734
  379.2 3.4 collective-permute-done.18
  383.8 12.7 %token_products.5 = bf16[1024,1536]{1,0:T(8,128)(2,1)} custom-call(bf16[512,1024]{1,0:T(8,128)(2,1)} %get-tuple-element.127.low_ref.refs_0_, bf16[512,1024]{1,0:T(8,128)(2,1)} %get-tuple-element.137.low_ref.refs_1_, bf16[512,1024]{1,0:T(8,128)(2,1)} %copy-done.3, bf16[512,1024]{1,0:T(8,128)(2,1)} %collective-permute-done.2.low_ref.refs_3_, ...), custom_call_target="tpu_custom_call" | custom-call | flops 1610612736 | bytes 3145728 | tf_op jit(solution)/shard_map/token_products/pallas_call | solution.py:734
  396.5 6.0 %collective-permute-done.19 = bf16[4,64,1536]{2,1,0:T(8,128)(2,1)S(1)} collective-permute-done((bf16[4,64,1536]{2,1,0:T(8,128)(2,1)S(1)}, bf16[4,64,1536]{2,1,0:T(8,128)(2,1)S(1)}, u32[]{:S(2)}, u32[]{:S(2)}) %collective-permute-start.19) | collective-permute-done | bytes 786464 | tf_op jit(solution)/shard_map/ppermute | solution.py:1020
  404.5 3.3 collective-permute-done.20
  409.0 7.0 %collective-permute-done.22 = bf16[2,64,1536]{2,1,0:T(8,128)(2,1)S(1)} collective-permute-done((bf16[2,64,1536]{2,1,0:T(8,128)(2,1)S(1)}, bf16[2,64,1536]{2,1,0:T(8,128)(2,1)S(1)}, u32[]{:S(2)}, u32[]{:S(2)}) %collective-permute-start.22) | collective-permute-done | bytes 393248 | tf_op jit(solution)/shard_map/ppermute | solution.py:1020
  418.1 9.6 %collective-permute-done.24 = bf16[4,64,1536]{2,1,0:T(8,128)(2,1)S(1)} collective-permute-done((bf16[4,64,1536]{2,1,0:T(8,128)(2,1)S(1)}, bf16[4,64,1536]{2,1,0:T(8,128)(2,1)S(1)}, u32[]{:S(2)}, u32[]{:S(2)}) %collective-permute-start.24) | collective-permute-done | bytes 786464 | tf_op jit(solution)/shard_map/ppermute | solution.py:1020
  430.6 10.0 %collective-permute-done.25 = bf16[2,64,1536]{2,1,0:T(8,128)(2,1)S(1)} collective-permute-done((bf16[2,64,1536]{2,1,0:T(8,128)(2,1)S(1)}, bf16[2,64,1536]{2,1,0:T(8,128)(2,1)S(1)}, u32[]{:S(2)}, u32[]{:S(2)}) %collective-permute-start.25) | collective-permute-done | bytes 393248 | tf_op jit(solution)/shard_map/ppermute | solution.py:1020
  445.7 7.2 %collective-permute-done.26 = bf16[1,64,1536]{2,1,0:T(8,128)(2,1)S(1)} collective-permute-done((bf16[1,64,1536]{2,1,0:T(8,128)(2,1)S(1)}, bf16[1,64,1536]{2,1,0:T(8,128)(2,1)S(1)}, u32[]{:S(2)}, u32[]{:S(2)}) %collective-permute-start.26) | collective-permute-done | bytes 196640 | tf_op jit(solution)/shard_map/ppermute | solution.py:1020
  457.1 7.6 %first_back.1 = (bf16[1024,1024]{1,0:T(8,128)(2,1)}, f32[1,1024]{1,0:T(1,128)}) custom-call(bf16[1024,1024]{1,0:T(8,128)(2,1)} %rows_ref.5, f32[1024,1024]{1,0:T(8,128)} %get-tuple-element.148.middle_grad_ref, f32[1,1024]{1,0:T(1,128)} %bitcast.211, f32[512,1024]{1,0:T(8,128)} %get-tuple-element.199.refs_0_, ...), custom_call_target="tpu_custom_call" | custom-call | tf_op jit(solution)/shard_map/first_back/pallas_call | solution.py:862
  468.3 6.1 %collective-permute-done.12 = f32[19,1024]{1,0:T(8,128)S(1)} collective-permute-done((f32[19,1024]{1,0:T(8,128)S(1)}, f32[19,1024]{1,0:T(8,128)S(1)}, u32[]{:S(2)}, u32[]{:S(2)}) %collective-permute-start.12) | collective-permute-done | bytes 77856 | tf_op jit(solution)/shard_map/ppermute | solution.py:1020
  474.5 7.2 %collective-permute-done.13 = f32[19,1024]{1,0:T(8,128)S(1)} collective-permute-done((f32[19,1024]{1,0:T(8,128)S(1)}, f32[19,1024]{1,0:T(8,128)S(1)}, u32[]{:S(2)}, u32[]{:S(2)}) %collective-permute-start.13) | collective-permute-done | bytes 77856 | tf_op jit(solution)/shard_map/ppermute | solution.py:1020
  482.2 9.0 %collective-permute-done.14 = f32[19,1024]{1,0:T(8,128)S(1)} collective-permute-done((f32[19,1024]{1,0:T(8,128)S(1)}, f32[19,1024]{1,0:T(8,128)S(1)}, u32[]{:S(2)}, u32[]{:S(2)}) %collective-permute-start.14) | collective-permute-done | bytes 77856 | tf_op jit(solution)/shard_map/ppermute | solution.py:1020
  496.2 52.4 %all-gather.5.cloned.1.call-done.grads_ref = bf16[1024,8320]{1,0:T(8,128)(2,1)} async-done(((bf16[64,8320]{1,0:T(8,128)(2,1)}), bf16[1024,8320]{1,0:T(8,128)(2,1)}) %all-gather.5.cloned.1.call-update) | async-done | bytes 17039376 | tf_op jit(solution)/shard_map/all_gather | solution.py:1298
  548.6 18.4 %spread_grads.1 = (f32[1024,2,1408]{2,1,0:T(2,128)}, f32[1408,1024]{1,0:T(8,128)}, f32[1024,1024]{1,0:T(8,128)}, f32[1024,4,768]{2,1,0:T(4,128)}) custom-call(bf16[1024,8320]{1,0:T(8,128)(2,1)} %all-gather.5.cloned.1.call-done.grads_ref), custom_call_target="tpu_custom_call" | custom-call | tf_op jit(solution)/shard_map/spread_grads/pallas_call | solution.py:989
  (247 shorter events, 67.7 us)
Async XLA Ops:
  7.2 131.8 %all-gather.3.cloned.1.call-start = ((), (), s32[]{:S(2)}) async-start(), calls=%async_computation.1 | async-start | bytes 18382848 | tf_op jit(solution)/shard_map/all_gather | solution.py:1147
  11.2 15.2 %collective-permute-start.4 = (bf16[3,64,1408]{2,1,0:T(8,128)(2,1)S(1)}, bf16[3,64,1408]{2,1,0:T(8,128)(2,1)S(1)}, u32[]{:S(2)}, u32[]{:S(2)}) collective-permute-start(bf16[3,64,1408]{2,1,0:T(8,128)(2,1)S(1)} %pad_maximum_fusion.1), channel_id=1, source_target_pairs={{1,0},{0,1},{3,2},{2,3},{5,4},{4,5},{7,6},{6,7},{9,8},{8,9},{11,10... | collective-permute-start | bytes 1622024 | tf_op jit(solution)/shard_map/ppermute | solution.py:1016
  29.9 397.9 %reduce-scatter.2.cloned.1.call-start = ((), (), s32[]{:S(2)}) async-start(), calls=%async_computation.2 | async-start | bytes 18382848 | tf_op jit(solution)/shard_map/reduce_scatter | solution.py:1190
  30.0 29.8 %collective-permute-start = (bf16[512,1024]{1,0:T(8,128)(2,1)S(1)}, bf16[512,1024]{1,0:T(8,128)(2,1)S(1)}, u32[]{:S(2)}, u32[]{:S(2)}) collective-permute-start(bf16[512,1024]{1,0:T(8,128)(2,1)S(1)} %copy-done.2), channel_id=1, source_target_pairs={{1,0},{0,1},{3,2},{2,3},{5,4},{4,5},{7,6},{6,7},{9,8},{8,9},{11,10... | collective-permute-start | bytes 3145736 | tf_op jit(solution)/shard_map/ppermute | solution.py:1016
  31.8 52.2 %collective-permute-start.2 = (bf16[512,1024]{1,0:T(8,128)(2,1)S(1)}, bf16[512,1024]{1,0:T(8,128)(2,1)}, u32[]{:S(2)}, u32[]{:S(2)}) collective-permute-start(bf16[512,1024]{1,0:T(8,128)(2,1)S(1)} %copy-done.4), channel_id=1, source_target_pairs={{1,0},{0,1},{3,2},{2,3},{5,4},{4,5},{7,6},{6,7},{9,8},{8,9},{11,10... | collective-permute-start | bytes 3145736 | tf_op jit(solution)/shard_map/ppermute | solution.py:1016
  82.2 26.2 %collective-permute-start.1 = (bf16[512,1024]{1,0:T(8,128)(2,1)}, bf16[512,1024]{1,0:T(8,128)(2,1)}, u32[]{:S(2)}, u32[]{:S(2)}) collective-permute-start(bf16[512,1024]{1,0:T(8,128)(2,1)} %get-tuple-element.130), channel_id=1, source_target_pairs={{1,0},{0,1},{3,2},{2,3},{5,4},{4,5},{7,6},{6,7},{9,8},{8,9},{11,10... | collective-permute-start | bytes 3145736 | tf_op jit(solution)/shard_map/ppermute | solution.py:1016
  84.0 21.9 %copy-start.8 = (bf16[1024,1024]{1,0:T(8,128)(2,1)S(1)}, bf16[1024,1024]{1,0:T(8,128)(2,1)}, u32[]{:S(2)}) copy-start(bf16[1024,1024]{1,0:T(8,128)(2,1)} %cot_ref.3) | copy-start | bytes 6291460
  105.6 24.6 %collective-permute-start.3 = (bf16[512,1024]{1,0:T(8,128)(2,1)}, bf16[512,1024]{1,0:T(8,128)(2,1)S(1)}, u32[]{:S(2)}, u32[]{:S(2)}) collective-permute-start(bf16[512,1024]{1,0:T(8,128)(2,1)} %get-tuple-element.135), channel_id=1, source_target_pairs={{1,0},{0,1},{3,2},{2,3},{5,4},{4,5},{7,6},{6,7},{9,8},{8,9},{11,10... | collective-permute-start | bytes 3145736 | tf_op jit(solution)/shard_map/ppermute | solution.py:1016
  202.3 346.3 %all-gather.5.cloned.1.call-start = ((), (), s32[]{:S(2)}) async-start(), calls=%async_computation.3 | async-start | bytes 18104320 | tf_op jit(solution)/shard_map/all_gather | solution.py:1298
  212.4 35.1 %collective-permute-start.6 = (bf16[512,1024]{1,0:T(8,128)(2,1)}, bf16[512,1024]{1,0:T(8,128)(2,1)S(1)}, u32[]{:S(2)}, u32[]{:S(2)}) collective-permute-start(bf16[512,1024]{1,0:T(8,128)(2,1)} %get-tuple-element.150.cot_ref.refs_5_), channel_id=1, source_target_pairs={{1,0},{0,1},{3,2},{2,3},{5,4},{4,5},{7,6},{6,7},{9,8},{8,9},{11,10... | collective-permute-start | bytes 3145736 | tf_op jit(solution)/shard_map/ppermute | solution.py:1016
  214.4 63.9 %collective-permute-start.5 = (bf16[512,1024]{1,0:T(8,128)(2,1)}, bf16[512,1024]{1,0:T(8,128)(2,1)S(1)}, u32[]{:S(2)}, u32[]{:S(2)}) collective-permute-start(bf16[512,1024]{1,0:T(8,128)(2,1)} %get-tuple-element.190.refs_4_.cot_ref), channel_id=1, source_target_pairs={{1,0},{0,1},{3,2},{2,3},{5,4},{4,5},{7,6},{6,7},{9,8},{8,9},{11,10... | collective-permute-start | bytes 3145736 | tf_op jit(solution)/shard_map/ppermute | solution.py:1016
  290.9 2.9 collective-permute-start.7
  295.2 33.4 %collective-permute-start.8 = (bf16[4,64,1024]{2,1,0:T(8,128)(2,1)S(1)}, bf16[4,64,1024]{2,1,0:T(8,128)(2,1)S(1)}, u32[]{:S(2)}, u32[]{:S(2)}) collective-permute-start(bf16[4,64,1024]{2,1,0:T(8,128)(2,1)S(1)} %dynamic-slice_bitcast_fusion.5), channel_id=1, source_target_pairs={{0,4},{2,6},{4,0},{6,2},{8,12},{10,14},{12,8},{14,10},{16,20},{18,... | collective-permute-start | bytes 1572872 | tf_op jit(solution)/shard_map/ppermute | solution.py:1020
  297.0 65.7 %collective-permute-start.10 = (bf16[512,1024]{1,0:T(8,128)(2,1)}, bf16[512,1024]{1,0:T(8,128)(2,1)S(1)}, u32[]{:S(2)}, u32[]{:S(2)}) collective-permute-start(bf16[512,1024]{1,0:T(8,128)(2,1)} %get-tuple-element.167), channel_id=1, source_target_pairs={{1,0},{0,1},{3,2},{2,3},{5,4},{4,5},{7,6},{6,7},{9,8},{8,9},{11,10... | collective-permute-start | bytes 3145736 | tf_op jit(solution)/shard_map/ppermute | solution.py:1016
  328.2 34.5 %collective-permute-start.9 = (bf16[512,1024]{1,0:T(8,128)(2,1)}, bf16[512,1024]{1,0:T(8,128)(2,1)}, u32[]{:S(2)}, u32[]{:S(2)}) collective-permute-start(bf16[512,1024]{1,0:T(8,128)(2,1)} %get-tuple-element.187), channel_id=1, source_target_pairs={{1,0},{0,1},{3,2},{2,3},{5,4},{4,5},{7,6},{6,7},{9,8},{8,9},{11,10... | collective-permute-start | bytes 3145736 | tf_op jit(solution)/shard_map/ppermute | solution.py:1016
  328.6 31.1 %collective-permute-start.16 = (bf16[2,64,1024]{2,1,0:T(8,128)(2,1)S(1)}, bf16[2,64,1024]{2,1,0:T(8,128)(2,1)S(1)}, u32[]{:S(2)}, u32[]{:S(2)}) collective-permute-start(bf16[2,64,1024]{2,1,0:T(8,128)(2,1)S(1)} %dynamic-slice_bitcast_fusion.8), channel_id=1, source_target_pairs={{0,8},{2,10},{4,12},{6,14},{8,0},{10,2},{12,4},{14,6},{16,24},{18,... | collective-permute-start | bytes 786440 | tf_op jit(solution)/shard_map/ppermute | solution.py:1020
  359.8 17.2 %collective-permute-start.17 = (bf16[1,64,1024]{2,1,0:T(8,128)(2,1)S(1)}, bf16[1,64,1024]{2,1,0:T(8,128)(2,1)S(1)}, u32[]{:S(2)}, u32[]{:S(2)}) collective-permute-start(bf16[1,64,1024]{2,1,0:T(8,128)(2,1)S(1)} %constant_dynamic-slice_fusion.3), channel_id=1, source_target_pairs={{0,16},{2,18},{4,20},{6,22},{8,24},{10,26},{12,28},{14,30},{16,0},... | collective-permute-start | bytes 393224 | tf_op jit(solution)/shard_map/ppermute | solution.py:1020
  379.1 3.5 collective-permute-start.18
  382.9 19.6 %collective-permute-start.19 = (bf16[4,64,1536]{2,1,0:T(8,128)(2,1)S(1)}, bf16[4,64,1536]{2,1,0:T(8,128)(2,1)S(1)}, u32[]{:S(2)}, u32[]{:S(2)}) collective-permute-start(bf16[4,64,1536]{2,1,0:T(8,128)(2,1)S(1)} %dynamic-slice_bitcast_fusion.4), channel_id=1, source_target_pairs={{0,4},{2,6},{4,0},{6,2},{8,12},{10,14},{12,8},{14,10},{16,20},{18,... | collective-permute-start | bytes 2359304 | tf_op jit(solution)/shard_map/ppermute | solution.py:1020
  404.3 3.5 collective-permute-start.20
  404.4 11.6 %collective-permute-start.22 = (bf16[2,64,1536]{2,1,0:T(8,128)(2,1)S(1)}, bf16[2,64,1536]{2,1,0:T(8,128)(2,1)S(1)}, u32[]{:S(2)}, u32[]{:S(2)}) collective-permute-start(bf16[2,64,1536]{2,1,0:T(8,128)(2,1)S(1)} %dynamic-slice_bitcast_fusion.7), channel_id=1, source_target_pairs={{0,8},{2,10},{4,12},{6,14},{8,0},{10,2},{12,4},{14,6},{16,24},{18,... | collective-permute-start | bytes 1179656 | tf_op jit(solution)/shard_map/ppermute | solution.py:1020
  408.0 19.6 %collective-permute-start.24 = (bf16[4,64,1536]{2,1,0:T(8,128)(2,1)S(1)}, bf16[4,64,1536]{2,1,0:T(8,128)(2,1)S(1)}, u32[]{:S(2)}, u32[]{:S(2)}) collective-permute-start(bf16[4,64,1536]{2,1,0:T(8,128)(2,1)S(1)} %dynamic-slice_bitcast_fusion.3), channel_id=1, source_target_pairs={{0,4},{2,6},{4,0},{6,2},{8,12},{10,14},{12,8},{14,10},{16,20},{18,... | collective-permute-start | bytes 2359304 | tf_op jit(solution)/shard_map/ppermute | solution.py:1020
  416.1 14.5 %collective-permute-start.23 = (bf16[1,64,1536]{2,1,0:T(8,128)(2,1)S(1)}, bf16[1,64,1536]{2,1,0:T(8,128)(2,1)S(1)}, u32[]{:S(2)}, u32[]{:S(2)}) collective-permute-start(bf16[1,64,1536]{2,1,0:T(8,128)(2,1)S(1)} %constant_dynamic-slice_fusion.2), channel_id=1, source_target_pairs={{0,16},{2,18},{4,20},{6,22},{8,24},{10,26},{12,28},{14,30},{16,0},... | collective-permute-start | bytes 589832 | tf_op jit(solution)/shard_map/ppermute | solution.py:1020
  428.9 13.6 %collective-permute-start.21 = (bf16[192,1408]{1,0:T(8,128)(2,1)S(1)}, bf16[192,1408]{1,0:T(8,128)(2,1)S(1)}, u32[]{:S(2)}, u32[]{:S(2)}) collective-permute-start(bf16[192,1408]{1,0:T(8,128)(2,1)S(1)} %slice.176), channel_id=1, source_target_pairs={{1,0},{0,1},{3,2},{2,3},{5,4},{4,5},{7,6},{6,7},{9,8},{8,9},{11,10... | collective-permute-start | bytes 1622024 | tf_op jit(solution)/shard_map/ppermute | solution.py:1016
  430.5 10.1 %collective-permute-start.25 = (bf16[2,64,1536]{2,1,0:T(8,128)(2,1)S(1)}, bf16[2,64,1536]{2,1,0:T(8,128)(2,1)S(1)}, u32[]{:S(2)}, u32[]{:S(2)}) collective-permute-start(bf16[2,64,1536]{2,1,0:T(8,128)(2,1)S(1)} %dynamic-slice_bitcast_fusion.6), channel_id=1, source_target_pairs={{0,8},{2,10},{4,12},{6,14},{8,0},{10,2},{12,4},{14,6},{16,24},{18,... | collective-permute-start | bytes 1179656 | tf_op jit(solution)/shard_map/ppermute | solution.py:1020
  442.6 10.4 %collective-permute-start.26 = (bf16[1,64,1536]{2,1,0:T(8,128)(2,1)S(1)}, bf16[1,64,1536]{2,1,0:T(8,128)(2,1)S(1)}, u32[]{:S(2)}, u32[]{:S(2)}) collective-permute-start(bf16[1,64,1536]{2,1,0:T(8,128)(2,1)S(1)} %constant_dynamic-slice_fusion.1), channel_id=1, source_target_pairs={{0,16},{2,18},{4,20},{6,22},{8,24},{10,26},{12,28},{14,30},{16,0},... | collective-permute-start | bytes 589832 | tf_op jit(solution)/shard_map/ppermute | solution.py:1020
  465.5 1.4 collective-permute-start.11
  466.9 7.5 %collective-permute-start.12 = (f32[19,1024]{1,0:T(8,128)S(1)}, f32[19,1024]{1,0:T(8,128)S(1)}, u32[]{:S(2)}, u32[]{:S(2)}) collective-permute-start(f32[19,1024]{1,0:T(8,128)S(1)} %add.208), channel_id=1, source_target_pairs={{0,4},{2,6},{4,0},{6,2},{8,12},{10,14},{12,8},{14,10},{16,20},{18,... | collective-permute-start | bytes 233480 | tf_op jit(solution)/shard_map/ppermute | solution.py:1020
  474.5 7.3 %collective-permute-start.13 = (f32[19,1024]{1,0:T(8,128)S(1)}, f32[19,1024]{1,0:T(8,128)S(1)}, u32[]{:S(2)}, u32[]{:S(2)}) collective-permute-start(f32[19,1024]{1,0:T(8,128)S(1)} %add.209), channel_id=1, source_target_pairs={{0,8},{2,10},{4,12},{6,14},{8,0},{10,2},{12,4},{14,6},{16,24},{18,... | collective-permute-start | bytes 233480 | tf_op jit(solution)/shard_map/ppermute | solution.py:1020
  481.8 9.4 %collective-permute-start.14 = (f32[19,1024]{1,0:T(8,128)S(1)}, f32[19,1024]{1,0:T(8,128)S(1)}, u32[]{:S(2)}, u32[]{:S(2)}) collective-permute-start(f32[19,1024]{1,0:T(8,128)S(1)} %add.210), channel_id=1, source_target_pairs={{0,16},{2,18},{4,20},{6,22},{8,24},{10,26},{12,28},{14,30},{16,0},... | collective-permute-start | bytes 233480 | tf_op jit(solution)/shard_map/ppermute | solution.py:1020
  491.3 3.8 collective-permute-start.15
  548.6 18.4 %copy-start.1 = (bf16[1408,1024]{1,0:T(8,128)(2,1)S(1)}, bf16[1408,1024]{1,0:T(8,128)(2,1)}, u32[]{:S(2)}) copy-start(bf16[1408,1024]{1,0:T(8,128)(2,1)} %param.26) | copy-start | bytes 8650756
  (35 other events, 208.3 us)
Sparse Core Ops, SparseCore 0:
  30.0 93.1 all-gather.2
  202.5 192.4 reduce-scatter.1
  455.4 93.2 all-gather.4
